TPU v7x, 32 devices: a whole 2x2x4 slice. The times are simulated.
32 devices in a mesh: row: 4 (over y, x), col: 8 (over z, core).
Axes of the slice: x: 2, y: 2, z: 4, core: 2. Of those that a mesh axis runs over, the one named last changes fastest.
Arguments:
- tokens: bfloat16 [1792, 4096], P('row', 'col'), may hold values from -6 to 6
- cotangent: bfloat16 [1792, 4096], P('row', 'col'), may hold values from -6 to 6
- lengths: int32 [4], replicated, may hold values from 1 to 1024, as said below
- deal_order: int32 [4], replicated, may hold values from 0 to 3, as said below
- w_qkv: bfloat16 [1792, 2304], P('row', 'col'), may hold values from -0.125 to 0.125
- conv_weight: bfloat16 [3, 1792], P(None, 'col'), may hold values from -1 to 1
- w_out: bfloat16 [1792, 1792], P('col', 'row'), may hold values from -1 to 1
- w_gate: bfloat16 [1792, 4864], P('row', 'col'), may hold values from -0.125 to 0.125
- w_up: bfloat16 [1792, 4864], P('row', 'col'), may hold values from -0.125 to 0.125
- w_down: bfloat16 [1792, 4864], P('row', 'col'), may hold values from -0.15625 to 0.15625
- gain_mix: bfloat16 [1792], P('row'), may hold values from 0.5 to 1.5
- gain_ffn: bfloat16 [1792], P('row'), may hold values from 0.5 to 1.5
Outputs:
- result: bfloat16 [1792, 4096], P('row', 'col')
- grad_tokens: float32 [1792, 4096], P('row', 'col')
- grad_qkv: float32 [1792, 2304], P('row', 'col')
- grad_conv: float32 [3, 1792], P(None, 'col')
- grad_out: float32 [1792, 1792], P('col', 'row')
- grad_gate: float32 [1792, 4864], P('row', 'col')
- grad_up: float32 [1792, 4864], P('row', 'col')
- grad_down: float32 [1792, 4864], P('row', 'col')
- grad_gain_mix: float32 [1792], P('row')
- grad_gain_ffn: float32 [1792], P('row')
- rms_values: float32 [3], replicated
Inputs may be any that keep to these rules, and one draw needn't show every extreme that they name: `lengths`: laid end to end in dealt order, the sequences fill each aligned block of 1024 tokens exactly, so that none crosses a multiple of 1024; they sum to 4096. Each sequence appears once: the k-th sequence of dealt order is sequence deal_order[k] of the given order.
All inputs are finite; a program needn't handle non-finite values.
Results may differ from a plain program's by a relative error of at most 0.025.
Values may be sent and summed in bfloat16 or wider, within the bound.
A program may use at most 256 MiB of HBM per device.

v0:
```python
import jax
import jax.numpy as jnp
from jax import lax
from jax.sharding import PartitionSpec as P

D = 1792
FEAT = 16
CONV = 3
LONGEST = 1024
HDIM = 112


EPSILON = 1e-06


def dealing(lengths, deal_order, total_rows):
    seq_ids = jnp.arange(lengths.shape[0], dtype=jnp.int32)
    chosen = (deal_order[:, None] == seq_ids[None, :]).astype(jnp.int32)
    dealt_lengths = jnp.sum(chosen * lengths[None, :], 1)
    given_start = jnp.cumsum(lengths) - lengths
    dealt_start = jnp.cumsum(dealt_lengths) - dealt_lengths
    given_of_dealt = jnp.sum(chosen * given_start[None, :], 1)
    dealt_of_given = jnp.sum(chosen * dealt_start[:, None], 0)
    places = jnp.arange(total_rows, dtype=jnp.int32)
    in_dealt = (places[:, None] >= dealt_start[None, :]) & (
        places[:, None] < (dealt_start + dealt_lengths)[None, :]
    )
    in_given = (places[:, None] >= given_start[None, :]) & (
        places[:, None] < (given_start + lengths)[None, :]
    )
    source = places + jnp.sum(jnp.where(in_dealt, (given_of_dealt - dealt_start)[None, :], 0), 1)
    target = places + jnp.sum(jnp.where(in_given, (dealt_of_given - given_start)[None, :], 0), 1)
    offsets = places - jnp.sum(jnp.where(in_dealt, dealt_start[None, :], 0), 1)
    return (source, target, offsets)


def convolve(raw_values, kernel_conv, offsets):
    mixed = kernel_conv[0] * raw_values
    for delay_step in range(1, CONV):
        moved = jnp.concatenate(
            [jnp.zeros_like(raw_values[:delay_step]), raw_values[:-delay_step]], 0
        )
        mixed = mixed + kernel_conv[delay_step] * jnp.where(
            (offsets >= delay_step)[:, None, None], moved, 0.0
        )
    return mixed


def convolve_back(grad_mixed, raw_values, kernel_conv, offsets):
    grad_raw = kernel_conv[0] * grad_mixed
    sums_list = [jnp.sum(grad_mixed * raw_values, 0)]
    for delay_step in range(1, CONV):
        masked = jnp.where((offsets >= delay_step)[:, None, None], grad_mixed, 0.0)
        pulled = jnp.concatenate([masked[delay_step:], jnp.zeros_like(masked[:delay_step])], 0)
        grad_raw = grad_raw + kernel_conv[delay_step] * pulled
        moved = jnp.concatenate(
            [jnp.zeros_like(raw_values[:delay_step]), raw_values[:-delay_step]], 0
        )
        sums_list.append(jnp.sum(masked * moved, 0))
    return (grad_raw, jnp.stack(sums_list))


def bin_scores(query, keys, offsets):
    scores = jnp.einsum("thf,shf->hts", query, keys, preferred_element_type=jnp.float32) * FEAT ** (
        -0.5
    )
    positions = jnp.arange(query.shape[0], dtype=jnp.int32)
    visible = (positions[None, :] <= positions[:, None]) & (
        positions[:, None] - positions[None, :] <= offsets[:, None]
    )
    kernel = jnp.where(visible[None], 1.0 + scores + 0.5 * scores * scores, 0.0)
    return (scores, visible, kernel)


def attend_bin(pieces):
    query, keys, values, offsets = pieces
    scores, visible, kernel = bin_scores(query, keys, offsets)
    weights = (kernel / jnp.sum(kernel, -1, keepdims=True)).astype(jnp.bfloat16)
    return jnp.einsum("hts,shd->thd", weights, values, preferred_element_type=jnp.float32)


def attend_back(pieces):
    query, keys, values, offsets, grad_attend = pieces
    scores, visible, kernel = bin_scores(query, keys, offsets)
    totals = jnp.sum(kernel, -1, keepdims=True)
    weights = kernel / totals
    grad_weights = jnp.einsum(
        "thd,shd->hts", grad_attend, values, preferred_element_type=jnp.float32
    )
    grad_values = jnp.einsum(
        "hts,thd->shd",
        weights.astype(jnp.bfloat16),
        grad_attend,
        preferred_element_type=jnp.float32,
    )
    grad_kernel = (grad_weights - jnp.sum(grad_weights * weights, -1, keepdims=True)) / totals
    grad_scores = jnp.where(visible[None], grad_kernel * (1.0 + scores), 0.0).astype(jnp.bfloat16)
    grad_query = jnp.einsum(
        "hts,shf->thf", grad_scores, keys, preferred_element_type=jnp.float32
    ) * FEAT ** (-0.5)
    grad_keys = jnp.einsum(
        "hts,thf->shf", grad_scores, query, preferred_element_type=jnp.float32
    ) * FEAT ** (-0.5)
    return (grad_query, grad_keys, grad_values)


def times_transposed(left, right):
    return lax.dot_general(
        left, right, (((1,), (1,)), ((), ())), preferred_element_type=jnp.float32
    )


def tokens_product(left, right):
    return lax.dot_general(
        left, right, (((0,), (0,)), ((), ())), preferred_element_type=jnp.float32
    )


def plain_product(left, right):
    return jnp.dot(left, right, preferred_element_type=jnp.float32)


def gather_cols(values):
    return lax.all_gather(values, "col", axis=0, tiled=True)


def gather_rows(values):
    return lax.all_gather(values, "row", axis=0, tiled=True)


def grad_gather_cols(values):
    return lax.all_gather(values, "col", axis=1, tiled=True)


def grad_gather_rows(values):
    return lax.all_gather(values, "row", axis=0, tiled=True)


def width_total(values):
    return lax.psum(values, "row")


def forward_rows(gathered, row_index, weight, rows_here):

    def partial_term(row_start, row_count):
        picked = jnp.take(gathered, row_index, axis=0)
        return jnp.dot(picked, weight, preferred_element_type=jnp.float32)

    return lax.psum_scatter(
        partial_term(jnp.int32(0), rows_here * lax.axis_size("row")),
        "row",
        scatter_dimension=0,
        tiled=True,
    )


def forward_cols(gathered, row_index, weight, rows_here, product):

    def partial_term(row_start, row_count):
        picked = jnp.take(gathered, row_index, axis=0)
        return product(picked, weight)

    return lax.psum_scatter(
        partial_term(jnp.int32(0), lax.axis_size("col") * rows_here).astype(jnp.bfloat16),
        "col",
        scatter_dimension=0,
        tiled=True,
    ).astype(jnp.float32)


def backward_rows(gathered, row_index, weight, rows_here, contract):

    def partial_term(row_start, row_count):
        picked = jnp.take(gathered, row_index, axis=1)
        return lax.dot_general(
            picked, weight, (((0,), (contract,)), ((), ())), preferred_element_type=jnp.float32
        )

    return lax.psum_scatter(
        partial_term(jnp.int32(0), lax.axis_size("row") * rows_here).astype(jnp.bfloat16),
        "row",
        scatter_dimension=0,
        tiled=True,
    ).astype(jnp.float32)


def backward_cols(gathered, row_index, weight, rows_here):

    def partial_term(row_start, row_count):
        picked = jnp.take(gathered, row_index, axis=0)
        return times_transposed(picked, weight)

    return lax.psum_scatter(
        partial_term(jnp.int32(0), lax.axis_size("col") * rows_here).astype(jnp.bfloat16),
        "col",
        scatter_dimension=0,
        tiled=True,
    ).astype(jnp.float32)


def norm_forward(values, norm_gain):
    totals = width_total(jnp.sum(values * values, -1))
    inverse = lax.rsqrt(totals / D + EPSILON)
    return (values * inverse[:, None] * norm_gain, inverse)


def norm_back(values, inverse, norm_gain, grad_normed, dot_sums):
    cubed = inverse * inverse * inverse
    return grad_normed * norm_gain * inverse[:, None] - values * (cubed * dot_sums / D)[:, None]


def on_device(
    tokens,
    cotangent,
    lengths,
    deal_order,
    w_qkv,
    conv_weight,
    w_out,
    w_gate,
    w_up,
    w_down,
    gain_mix,
    gain_ffn,
):
    local_rows = tokens.shape[1]
    total_rows = local_rows * lax.axis_size("col")
    group_rows = total_rows // lax.axis_size("row")
    bin_count = group_rows // LONGEST
    heads_here = w_out.shape[0] // HDIM
    ffn_cols = w_gate.shape[1]
    source, target, offsets = dealing(lengths, deal_order, total_rows)
    group_offsets = lax.dynamic_slice_in_dim(
        offsets, lax.axis_index("row") * group_rows, group_rows
    )
    inputs = tokens.astype(jnp.float32).T
    gain_one = gain_mix.astype(jnp.float32)
    gain_two = gain_ffn.astype(jnp.float32)
    both_weights = jnp.concatenate([w_gate, w_up], 1)
    normed_one, inverse_one = norm_forward(inputs, gain_one)
    low_one = normed_one.astype(jnp.bfloat16)
    all_one = gather_cols(low_one)
    projected = forward_rows(all_one, source, w_qkv, group_rows)
    projected = projected.reshape(group_rows, heads_here, 2 * FEAT + HDIM)
    query = projected[:, :, :FEAT].astype(jnp.bfloat16)
    keys = projected[:, :, FEAT : 2 * FEAT].astype(jnp.bfloat16)
    raw_values = projected[:, :, 2 * FEAT :]
    kernel_conv = conv_weight.astype(jnp.float32).reshape(CONV, heads_here, HDIM)
    values = convolve(raw_values, kernel_conv, group_offsets).astype(jnp.bfloat16)
    binned = (
        query.reshape(bin_count, LONGEST, heads_here, FEAT),
        keys.reshape(bin_count, LONGEST, heads_here, FEAT),
        values.reshape(bin_count, LONGEST, heads_here, HDIM),
        group_offsets.reshape(bin_count, LONGEST),
    )
    attended = (
        lax.map(attend_bin, binned).reshape(group_rows, heads_here * HDIM).astype(jnp.bfloat16)
    )
    all_attended = gather_rows(attended)
    branch_mix = forward_cols(all_attended, target, w_out, local_rows, plain_product)
    middle = inputs + branch_mix
    normed_two, inverse_two = norm_forward(middle, gain_two)
    low_two = normed_two.astype(jnp.bfloat16)
    all_two = gather_cols(low_two)
    gate_up = forward_rows(all_two, source, both_weights, group_rows)
    gate = gate_up[:, :ffn_cols]
    up_proj = gate_up[:, ffn_cols:]
    activated = jax.nn.silu(gate)
    hidden = (activated * up_proj).astype(jnp.bfloat16)
    all_hidden = gather_rows(hidden)
    branch_ffn = forward_cols(all_hidden, target, w_down, local_rows, times_transposed)
    result_full = middle + branch_ffn
    grad_result = cotangent.astype(jnp.float32).T
    all_grad_ffn = grad_gather_cols(cotangent)
    hidden_again = gather_rows(hidden)
    grad_down = jnp.dot(
        jnp.take(all_grad_ffn, source, axis=1), hidden_again, preferred_element_type=jnp.float32
    )
    grad_hidden = backward_rows(all_grad_ffn, source, w_down, group_rows, 0)
    gate_sigmoid = jax.nn.sigmoid(gate)
    grad_gate_part = grad_hidden * up_proj * gate_sigmoid * (1.0 + gate * (1.0 - gate_sigmoid))
    grad_up_part = grad_hidden * activated
    grad_gate_up = jnp.concatenate([grad_gate_part, grad_up_part], 1).astype(jnp.bfloat16)
    all_grad_gate_up = grad_gather_rows(grad_gate_up)
    two_again = gather_cols(low_two)
    grad_both = tokens_product(jnp.take(two_again, source, axis=0), all_grad_gate_up)
    grad_normed_two = backward_cols(all_grad_gate_up, target, both_weights, local_rows)
    dots_two = width_total(jnp.sum(grad_normed_two * gain_two * middle, -1))
    grad_middle = grad_result + norm_back(middle, inverse_two, gain_two, grad_normed_two, dots_two)
    gain_part_two = jnp.sum(grad_normed_two * middle * inverse_two[:, None], 0)
    low_grad_middle = grad_middle.T.astype(jnp.bfloat16)
    all_grad_middle = grad_gather_cols(low_grad_middle)
    attended_again = gather_rows(attended)
    grad_out = lax.dot_general(
        attended_again,
        jnp.take(all_grad_middle, source, axis=1),
        (((0,), (1,)), ((), ())),
        preferred_element_type=jnp.float32,
    )
    grad_attended = backward_rows(all_grad_middle, source, w_out, group_rows, 1).astype(
        jnp.bfloat16
    )
    binned_back = binned + (grad_attended.reshape(bin_count, LONGEST, heads_here, HDIM),)
    grad_query, grad_keys, grad_values = lax.map(attend_back, binned_back)
    grad_values = grad_values.reshape(group_rows, heads_here, HDIM)
    grad_raw, conv_part = convolve_back(grad_values, raw_values, kernel_conv, group_offsets)
    grad_projected = jnp.concatenate(
        [
            grad_query.reshape(group_rows, heads_here, FEAT),
            grad_keys.reshape(group_rows, heads_here, FEAT),
            grad_raw,
        ],
        2,
    )
    grad_projected = grad_projected.reshape(group_rows, heads_here * (2 * FEAT + HDIM)).astype(
        jnp.bfloat16
    )
    all_grad_projected = grad_gather_rows(grad_projected)
    one_again = gather_cols(low_one)
    grad_qkv = tokens_product(jnp.take(one_again, source, axis=0), all_grad_projected)
    grad_normed_one = backward_cols(all_grad_projected, target, w_qkv, local_rows)
    squares = jnp.stack(
        [
            jnp.sum(branch_mix * branch_mix),
            jnp.sum(branch_ffn * branch_ffn),
            jnp.sum(result_full * result_full),
        ]
    )
    dots_one, grad_conv, squares_rows = width_total(
        (
            jnp.sum(grad_normed_one * gain_one * inputs, -1),
            conv_part.reshape(CONV, heads_here * HDIM),
            squares,
        )
    )
    grad_tokens = grad_middle + norm_back(inputs, inverse_one, gain_one, grad_normed_one, dots_one)
    gain_part_one = jnp.sum(grad_normed_one * inputs * inverse_one[:, None], 0)
    grad_gain_mix, grad_gain_ffn, squares_all = lax.psum(
        (gain_part_one, gain_part_two, squares_rows), "col"
    )
    rms_values = jnp.sqrt(squares_all / (total_rows * D))
    return (
        result_full.T.astype(jnp.bfloat16),
        grad_tokens.T,
        grad_qkv,
        grad_conv,
        grad_out,
        grad_both[:, :ffn_cols],
        grad_both[:, ffn_cols:],
        grad_down,
        grad_gain_mix,
        grad_gain_ffn,
        rms_values,
    )


def solution(mesh):
    in_specs = (
        P("row", "col"),
        P("row", "col"),
        P(),
        P(),
        P("row", "col"),
        P(None, "col"),
        P("col", "row"),
        P("row", "col"),
        P("row", "col"),
        P("row", "col"),
        P("row"),
        P("row"),
    )
    out_specs = (
        P("row", "col"),
        P("row", "col"),
        P("row", "col"),
        P(None, "col"),
        P("col", "row"),
        P("row", "col"),
        P("row", "col"),
        P("row", "col"),
        P("row"),
        P("row"),
        P(),
    )
    return jax.shard_map(
        on_device, mesh=mesh, in_specs=in_specs, out_specs=out_specs, check_vma=False
    )
```

profile of v0, /device:TPU:4, one launch (start us, length us, event | category | flops | bytes accessed | tf_op | source)
XLA Modules:
  0.0 1167.2 jit_solution(216612645425496538)
XLA Ops:
  9.1 9.0 psum.63
  24.3 39.4 %all-gather.9.cloned.1.call-done = bf16[4096,448]{0,1:T(8,128)(2,1)} async-done(((bf16[512,448]{0,1:T(8,128)(2,1)}), bf16[4096,448]{0,1:T(8,128)(2,1)}) %all-gather.9.cloned.1.call-update) | async-done | bytes 3670032 | tf_op jit(solution)/shard_map/all_gather | solution.py:124
  63.7 6.4 copy.47
  70.1 20.2 %gather_fusion.4 = bf16[4096,448]{1,0:T(8,128)(2,1)} fusion(bf16[4096,448]{1,0:T(8,128)(2,1)} %copy.47, s32[4096]{0:T(1024)S(1)} %fusion.83), kind=kCustom, calls=%fused_computation.clone | custom fusion | bytes 7356416 | tf_op jit(solution)/shard_map/jit(_take)/gather | solution.py:146
  90.3 4.9 fusion.41
  96.9 54.3 %reduce-scatter.9.cloned.1.call-done = f32[1024,288]{0,1:T(8,128)} async-done(((f32[4096,288]{0,1:T(8,128)}), f32[1024,288]{0,1:T(8,128)}) %reduce-scatter.9.cloned.1.call-update) | async-done | bytes 1179664 | tf_op jit(solution)/shard_map/reduce_scatter | solution.py:149
  157.9 3.2 fusion.46
  162.4 35.3 %all-gather.11.cloned.1.call-done = bf16[4096,224]{1,0:T(8,128)(2,1)} async-done(((bf16[1024,224]{1,0:T(8,128)(2,1)}), bf16[4096,224]{1,0:T(8,128)(2,1)}) %all-gather.11.cloned.1.call-update) | async-done | bytes 1835024 | tf_op jit(solution)/shard_map/all_gather | solution.py:128
  197.7 14.9 %gather_fusion = bf16[4096,224]{1,0:T(8,128)(2,1)S(1)} fusion(bf16[4096,224]{1,0:T(8,128)(2,1)} %all-gather.11.cloned.1.call-done, s32[4096]{0:T(1024)S(1)} %broadcast_clamp_fusion), kind=kCustom, calls=%fused_computation.4 | custom fusion | bytes 3686400 | tf_op jit(solution)/shard_map/jit(_take)/gather | solution.py:160
  216.8 44.1 %reduce-scatter.11.cloned.1.call-done = bf16[512,448]{0,1:T(8,128)(2,1)} async-done(((bf16[4096,448]{0,1:T(8,128)(2,1)}), bf16[512,448]{0,1:T(8,128)(2,1)}) %reduce-scatter.11.cloned.1.call-update) | async-done | bytes 458768 | tf_op jit(solution)/shard_map/reduce_scatter | solution.py:163
  262.1 8.9 psum.64
  273.3 35.2 %all-gather.17.cloned.1.call-done = bf16[448,4096]{0,1:T(8,128)(2,1)} async-done(((bf16[448,512]{0,1:T(8,128)(2,1)}), bf16[448,4096]{0,1:T(8,128)(2,1)}) %all-gather.17.cloned.1.call-update) | async-done | bytes 3670032 | tf_op jit(solution)/shard_map/all_gather | solution.py:132
  308.4 20.1 %gather_fusion.6 = bf16[4096,448]{1,0:T(8,128)(2,1)} fusion(bf16[448,4096]{0,1:T(8,128)(2,1)} %all-gather.17.cloned.1.call-done, s32[4096]{0:T(1024)S(1)} %fusion.83), kind=kCustom, calls=%fused_computation.1.clone | custom fusion | bytes 7356416 | tf_op jit(solution)/shard_map/jit(_take)/gather | solution.py:174
  328.6 6.3 convolution_convert_fusion
  335.0 16.8 %all-gather.13.cloned.1.call-done = bf16[4096,448]{0,1:T(8,128)(2,1)} async-done(((bf16[512,448]{0,1:T(8,128)(2,1)}), bf16[4096,448]{0,1:T(8,128)(2,1)}) %all-gather.13.cloned.1.call-update) | async-done | bytes 3670032 | tf_op jit(solution)/shard_map/all_gather | solution.py:124
  351.8 6.4 copy.50
  358.2 20.2 %gather_fusion.5 = bf16[4096,448]{1,0:T(8,128)(2,1)} fusion(bf16[4096,448]{1,0:T(8,128)(2,1)} %copy.50, s32[4096]{0:T(1024)S(1)} %fusion.83), kind=kCustom, calls=%fused_computation.2.clone | custom fusion | bytes 7356416 | tf_op jit(solution)/shard_map/jit(_take)/gather | solution.py:146
  378.5 11.7 %fusion.39 = f32[4096,1216]{0,1:T(8,128)} fusion(bf16[4096,448]{1,0:T(8,128)(2,1)} %gather_fusion.5, pred[4096]{0:T(1024)(128)(4,1)S(1)} %compare_and_fusion, bf16[448,608]{1,0:T(8,128)(2,1)S(1)} %copy-done.49, bf16[448,608]{1,0:T(8,128)(2,1)S(1)} %copy-done.51), kind=kOutput, calls=%fused_computation.61 | convolution fusion | flops 4466753536 | bytes 24686592 | tf_op jit(solution)/shard_map/dot_general | solution.py:147
  390.3 22.6 %reduce-scatter.17.cloned.1.call-done = bf16[1024,608]{0,1:T(8,128)(2,1)} async-done(((bf16[4096,608]{0,1:T(8,128)(2,1)}), bf16[1024,608]{0,1:T(8,128)(2,1)}) %reduce-scatter.17.cloned.1.call-update) | async-done | bytes 1245200 | tf_op jit(solution)/shard_map/reduce_scatter | solution.py:179
  412.9 182.5 %reduce-scatter.13.cloned.1.call-done = f32[1024,1216]{0,1:T(8,128)} async-done(((f32[4096,1216]{0,1:T(8,128)}), f32[1024,1216]{0,1:T(8,128)}) %reduce-scatter.13.cloned.1.call-update) | async-done | bytes 4980752 | tf_op jit(solution)/shard_map/reduce_scatter | solution.py:149
  595.4 5.6 fusion.27
  603.2 57.3 %all-gather.15.cloned.1.call-done = bf16[4096,608]{0,1:T(8,128)(2,1)} async-done(((bf16[1024,608]{0,1:T(8,128)(2,1)}), bf16[4096,608]{0,1:T(8,128)(2,1)}) %all-gather.15.cloned.1.call-update) | async-done | bytes 4980752 | tf_op jit(solution)/shard_map/all_gather | solution.py:128
  660.5 7.8 copy.51
  668.3 22.2 %gather_fusion.1 = bf16[4096,608]{1,0:T(8,128)(2,1)} fusion(bf16[4096,608]{1,0:T(8,128)(2,1)} %copy.51, s32[4096]{0:T(1024)S(1)} %broadcast_clamp_fusion), kind=kCustom, calls=%fused_computation.5 | custom fusion | bytes 9977856 | tf_op jit(solution)/shard_map/jit(_take)/gather | solution.py:160
  690.4 6.4 convolution_convert_fusion.3
  697.0 66.1 %all-gather.19.cloned.1.call-done = bf16[4096,1216]{0,1:T(8,128)(2,1)} async-done(((bf16[1024,1216]{0,1:T(8,128)(2,1)}), bf16[4096,1216]{0,1:T(8,128)(2,1)}) %all-gather.19.cloned.1.call-update) | async-done | bytes 9961488 | tf_op jit(solution)/shard_map/all_gather | solution.py:136
  763.1 14.3 %copy.53 = bf16[4096,1216]{1,0:T(8,128)(2,1)} copy(bf16[4096,1216]{0,1:T(8,128)(2,1)} %all-gather.19.cloned.1.call-done) | data formatting | bytes 19922944 | tf_op jit(solution)/shard_map/all_gather | solution.py:136
  777.4 28.5 %gather_fusion.2 = bf16[4096,1216]{1,0:T(8,128)(2,1)} fusion(bf16[4096,1216]{1,0:T(8,128)(2,1)} %copy.53, s32[4096]{0:T(1024)S(1)} %broadcast_clamp_fusion), kind=kCustom, calls=%fused_computation.6 | custom fusion | bytes 19939328 | tf_op jit(solution)/shard_map/jit(_take)/gather | solution.py:190
  805.9 9.2 fusion.5
  815.2 45.2 %reduce-scatter.19.cloned.1.call-done = bf16[512,448]{0,1:T(8,128)(2,1)} async-done(((bf16[4096,448]{0,1:T(8,128)(2,1)}), bf16[512,448]{0,1:T(8,128)(2,1)}) %reduce-scatter.19.cloned.1.call-update) | async-done | bytes 458768 | tf_op jit(solution)/shard_map/reduce_scatter | solution.py:193
  863.5 8.9 psum.65
  874.7 39.9 %all-gather.21.cloned.1.call-done = bf16[448,4096]{1,0:T(8,128)(2,1)} async-done(((bf16[448,512]{1,0:T(8,128)(2,1)}), bf16[448,4096]{1,0:T(8,128)(2,1)}) %all-gather.21.cloned.1.call-update) | async-done | bytes 3670032 | tf_op jit(solution)/shard_map/all_gather | solution.py:132
  914.6 6.5 copy.54
  921.1 20.2 %gather_fusion.7 = bf16[4096,448]{1,0:T(8,128)(2,1)} fusion(bf16[448,4096]{0,1:T(8,128)(2,1)} %copy.54, s32[4096]{0:T(1024)S(1)} %fusion.83), kind=kCustom, calls=%fused_computation.3.clone | custom fusion | bytes 7356416 | tf_op jit(solution)/shard_map/jit(_take)/gather | solution.py:174
  941.3 4.4 convolution_convert_fusion.4
  946.0 31.8 %reduce-scatter.21.cloned.1.call-done = bf16[1024,224]{0,1:T(8,128)(2,1)} async-done(((bf16[4096,224]{0,1:T(8,128)(2,1)}), bf16[1024,224]{0,1:T(8,128)(2,1)}) %reduce-scatter.21.cloned.1.call-update) | async-done | bytes 458768 | tf_op jit(solution)/shard_map/reduce_scatter | solution.py:179
  977.8 9.2 multiply_reduce_fusion.3
  987.0 13.1 %fusion.52 = bf16[1024,2,16]{0,2,1:T(8,128)(2,1)S(1)} fusion(bf16[1024,2,144]{0,2,1:T(8,128)(2,1)} %copy-done.16, f32[2,1024,1024]{1,2,0:T(8,128)} %copy-done.56, f32[2,1024]{1,0:T(2,128)S(1)} %copy-done.58, pred[1024,1024]{0,1:T(8,128)(4,1)} %copy-done.14, bf16[1024,2,112]{0,2,1:T(8,128)(2,1)} %bitcast.116, bf16[1024,2,112]{0,2,1:T(8,128)(2,1)S(1)} %copy-done.18), kind=kOutput, calls=%fused_computation.81 | convolution fusion | flops 1038158848 | bytes 20856832 | tf_op jit(solution)/shard_map/while/body/eval_jaxpr/hts,shf->thf/dot_general | solution.py:98
  1000.2 13.3 %fusion.51 = bf16[1024,2,16]{0,2,1:T(8,128)(2,1)S(1)} fusion(bf16[1024,2,144]{0,2,1:T(8,128)(2,1)} %copy-done.16, f32[2,1024,1024]{1,2,0:T(8,128)} %copy-done.56, f32[2,1024]{1,0:T(2,128)S(1)} %copy-done.58, pred[1024,1024]{0,1:T(8,128)(4,1)} %copy-done.14, bf16[1024,2,112]{0,2,1:T(8,128)(2,1)S(1)} %bitcast.117, bf16[1024,2,112]{0,2,1:T(8,128)(2,1)S(1)} %copy-done.18), kind=kOutput, calls=%fused_computation.80 | convolution fusion | flops 1038158848 | bytes 20856832 | tf_op jit(solution)/shard_map/while/body/eval_jaxpr/hts,thf->shf/dot_general | solution.py:101
  1018.1 44.1 %all-gather.23.cloned.1.call-done = bf16[4096,288]{1,0:T(8,128)(2,1)} async-done(((bf16[1024,288]{1,0:T(8,128)(2,1)}), bf16[4096,288]{1,0:T(8,128)(2,1)}) %all-gather.23.cloned.1.call-update) | async-done | bytes 2359312 | tf_op jit(solution)/shard_map/all_gather | solution.py:136
  1062.2 19.0 %gather_fusion.3 = bf16[4096,288]{1,0:T(8,128)(2,1)} fusion(bf16[4096,288]{1,0:T(8,128)(2,1)} %all-gather.23.cloned.1.call-done, s32[4096]{0:T(1024)S(1)} %broadcast_clamp_fusion), kind=kCustom, calls=%fused_computation.7 | custom fusion | bytes 4734976 | tf_op jit(solution)/shard_map/jit(_take)/gather | solution.py:190
  1081.2 5.3 convolution_convert_fusion.2
  1086.5 8.9 fusion.16
  1095.4 10.3 fusion.38
  1112.0 6.2 fusion.40
  1118.2 13.4 %reduce-scatter.23.cloned.1.call-done = bf16[512,448]{0,1:T(8,128)(2,1)} async-done(((bf16[4096,448]{0,1:T(8,128)(2,1)}), bf16[512,448]{0,1:T(8,128)(2,1)}) %reduce-scatter.23.cloned.1.call-update) | async-done | bytes 458768 | tf_op jit(solution)/shard_map/reduce_scatter | solution.py:193
  1133.1 9.7 all-reduce.5
  1142.8 14.5 %all-reduce.4 = (f32[448]{0:T(512)}, f32[448]{0:T(512)}, f32[3]{0:T(128)S(1)}) all-reduce(f32[448]{0:T(512)S(1)} %get-tuple-element.61, f32[448]{0:T(512)S(1)} %get-tuple-element.49, f32[3]{0:T(128)S(1)} %get-tuple-element.76), channel_id=1, replica_groups=mesh['row'=4,'col'=8] {'col'}, use_global_device_ids=true, to_apply=%region_31.34 | all-reduce | flops 899 | bytes 7192 | tf_op jit(solution)/shard_map/psum | solution.py:338
  (209 shorter events, 48.5 us)
Async XLA Ops:
  7.2 321.4 %copy-start = (bf16[448,608]{1,0:T(8,128)(2,1)S(1)}, bf16[448,608]{1,0:T(8,128)(2,1)}, u32[]{:S(2)}) copy-start(bf16[448,608]{1,0:T(8,128)(2,1)} %param.25) | copy-start | bytes 1634308
  7.2 56.5 %all-gather.9.cloned.1.call-start = ((), (), s32[]{:S(2)}) async-start(), calls=%async_computation.8 | async-start | bytes 4128768 | tf_op jit(solution)/shard_map/all_gather | solution.py:124
  8.0 62.1 %copy-start.25 = (f32[448]{0:T(512)}, f32[448]{0:T(512)S(1)}, u32[]{:S(2)}) copy-start(f32[448]{0:T(512)S(1)} %convert_element_type.98) | copy-start | bytes 5380
  20.6 130.6 %reduce-scatter.9.cloned.1.call-start = ((), (), s32[]{:S(2)}) async-start(), calls=%async_computation.9 | async-start | bytes 5898240 | tf_op jit(solution)/shard_map/reduce_scatter | solution.py:149
  24.3 354.2 %copy-start.45 = (pred[4096]{0:T(1024)(128)(4,1)}, pred[4096]{0:T(1024)(128)(4,1)S(1)}, u32[]{:S(2)}) copy-start(pred[4096]{0:T(1024)(128)(4,1)S(1)} %compare_and_fusion) | copy-start | bytes 12292
  95.2 102.5 %all-gather.11.cloned.1.call-start = ((), (), s32[]{:S(2)}) async-start(), calls=%async_computation.10 | async-start | bytes 2621440 | tf_op jit(solution)/shard_map/all_gather | solution.py:128
  96.0 61.0 %copy-start.35 = (f32[2,112]{1,0:T(2,128)}, f32[2,112]{1,0:T(2,128)S(1)}, u32[]{:S(2)}) copy-start(f32[2,112]{1,0:T(2,128)S(1)} %mul.289) | copy-start | bytes 2692
  96.1 61.0 %copy-start.37 = (f32[2,112]{1,0:T(2,128)}, f32[2,112]{1,0:T(2,128)S(1)}, u32[]{:S(2)}) copy-start(f32[2,112]{1,0:T(2,128)S(1)} %mul.303) | copy-start | bytes 2692
  96.2 60.9 %copy-start.39 = (f32[2,112]{1,0:T(2,128)}, f32[2,112]{1,0:T(2,128)S(1)}, u32[]{:S(2)}) copy-start(f32[2,112]{1,0:T(2,128)S(1)} %mul.299) | copy-start | bytes 2692
  96.2 60.9 %copy-start.41 = (pred[1024]{0:T(1024)(128)(4,1)}, pred[1024]{0:T(1024)(128)(4,1)S(1)}, u32[]{:S(2)}) copy-start(pred[1024]{0:T(1024)(128)(4,1)S(1)} %get-tuple-element.81) | copy-start | bytes 3076
  96.2 60.9 %copy-start.43 = (pred[1024]{0:T(1024)(128)(4,1)}, pred[1024]{0:T(1024)(128)(4,1)S(1)}, u32[]{:S(2)}) copy-start(pred[1024]{0:T(1024)(128)(4,1)S(1)} %broadcast_compare_fusion) | copy-start | bytes 3076
  96.9 61.0 %copy-start.14 = (pred[1024,1024]{0,1:T(8,128)(4,1)}, pred[1024,1024]{0,1:T(8,128)(4,1)S(1)}, u32[]{:S(2)}) copy-start(pred[1024,1024]{0,1:T(8,128)(4,1)S(1)} %fusion.19) | copy-start | bytes 3145732
  162.1 98.7 %reduce-scatter.11.cloned.1.call-start = ((), (), s32[]{:S(2)}) async-start(), calls=%async_computation.11 | async-start | bytes 4128768 | tf_op jit(solution)/shard_map/reduce_scatter | solution.py:163
  162.3 50.2 %copy-start.29 = (pred[4096]{0:T(1024)(128)(4,1)}, pred[4096]{0:T(1024)(128)(4,1)S(1)}, u32[]{:S(2)}) copy-start(pred[4096]{0:T(1024)(128)(4,1)S(1)} %compare_and_fusion.1) | copy-start | bytes 12292
  162.4 50.2 %copy-start.19 = (bf16[224,448]{1,0:T(8,128)(2,1)S(1)}, bf16[224,448]{1,0:T(8,128)(2,1)}, u32[]{:S(2)}) copy-start(bf16[224,448]{1,0:T(8,128)(2,1)} %param.22) | copy-start | bytes 602116
  215.6 45.2 %copy-start.3 = (bf16[448,512]{1,0:T(8,128)(2,1)S(1)}, bf16[448,512]{1,0:T(8,128)(2,1)}, u32[]{:S(2)}) copy-start(bf16[448,512]{1,0:T(8,128)(2,1)} %param.16) | copy-start | bytes 1376260
  215.6 92.8 %all-gather.17.cloned.1.call-start = ((), (), s32[]{:S(2)}) async-start(), calls=%async_computation.16 | async-start | bytes 4718592 | tf_op jit(solution)/shard_map/all_gather | solution.py:132
  216.7 135.1 %all-gather.13.cloned.1.call-start = ((), (), s32[]{:S(2)}) async-start(), calls=%async_computation.12 | async-start | bytes 4128768 | tf_op jit(solution)/shard_map/all_gather | solution.py:124
  216.8 111.8 %copy-start.21 = (f32[448]{0:T(512)}, f32[448]{0:T(512)S(1)}, u32[]{:S(2)}) copy-start(f32[448]{0:T(512)S(1)} %convert_element_type.107) | copy-start | bytes 5380
  271.0 57.6 %copy-start.33 = (f32[512]{0:T(512)}, f32[512]{0:T(512)S(1)}, u32[]{:S(2)}) copy-start(f32[512]{0:T(512)S(1)} %psum.64) | copy-start | bytes 6148
  271.0 57.6 %copy-start.23 = (f32[512]{0:T(512)}, f32[512]{0:T(512)S(1)}, u32[]{:S(2)}) copy-start(f32[512]{0:T(512)S(1)} %add_rsqrt_fusion) | copy-start | bytes 6148
  273.0 139.9 %reduce-scatter.17.cloned.1.call-start = ((), (), s32[]{:S(2)}) async-start(), calls=%async_computation.17 | async-start | bytes 6225920 | tf_op jit(solution)/shard_map/reduce_scatter | solution.py:179
  334.9 260.4 %reduce-scatter.13.cloned.1.call-start = ((), (), s32[]{:S(2)}) async-start(), calls=%async_computation.13 | async-start | bytes 24903680 | tf_op jit(solution)/shard_map/reduce_scatter | solution.py:149
  358.2 20.2 %copy-start.51 = (bf16[448,608]{1,0:T(8,128)(2,1)S(1)}, bf16[448,608]{1,0:T(8,128)(2,1)}, u32[]{:S(2)}) copy-start(bf16[448,608]{1,0:T(8,128)(2,1)} %param.23) | copy-start | bytes 1634308
  390.2 270.3 %all-gather.15.cloned.1.call-start = ((), (), s32[]{:S(2)}) async-start(), calls=%async_computation.14 | async-start | bytes 6225920 | tf_op jit(solution)/shard_map/all_gather | solution.py:128
  601.0 162.1 %all-gather.19.cloned.1.call-start = ((), (), s32[]{:S(2)}) async-start(), calls=%async_computation.18 | async-start | bytes 12451840 | tf_op jit(solution)/shard_map/all_gather | solution.py:136
  602.8 212.4 %reduce-scatter.15.cloned.1.call-start = ((), (), s32[]{:S(2)}) async-start(), calls=%async_computation.15 | async-start | bytes 4128768 | tf_op jit(solution)/shard_map/reduce_scatter | solution.py:163
  668.3 22.2 %copy-start.30 = (pred[4096]{0:T(1024)(128)(4,1)S(1)}, pred[4096]{0:T(1024)(128)(4,1)}, u32[]{:S(2)}) copy-start(pred[4096]{0:T(1024)(128)(4,1)} %copy-done.29) | copy-start | bytes 12292
  696.9 163.5 %reduce-scatter.19.cloned.1.call-start = ((), (), s32[]{:S(2)}) async-start(), calls=%async_computation.19 | async-start | bytes 4128768 | tf_op jit(solution)/shard_map/reduce_scatter | solution.py:193
  777.4 28.5 %copy-start.50 = (bf16[448,608]{1,0:T(8,128)(2,1)S(1)}, bf16[448,608]{1,0:T(8,128)(2,1)}, u32[]{:S(2)}) copy-start(bf16[448,608]{1,0:T(8,128)(2,1)} %param.24) | copy-start | bytes 1634308
  777.4 28.5 %copy-start.52 = (bf16[448,608]{1,0:T(8,128)(2,1)S(1)}, bf16[448,608]{1,0:T(8,128)(2,1)}, u32[]{:S(2)}) copy-start(bf16[448,608]{1,0:T(8,128)(2,1)} %param.23) | copy-start | bytes 1634308
  805.8 54.5 %copy-start.6 = (bf16[512,448]{0,1:T(8,128)(2,1)S(1)}, bf16[512,448]{0,1:T(8,128)(2,1)}, u32[]{:S(2)}) copy-start(bf16[512,448]{0,1:T(8,128)(2,1)} %reduce-scatter.11.cloned.1.call-done) | copy-start | bytes 1376260
  805.8 54.5 %copy-start.22 = (f32[448]{0:T(512)S(1)}, f32[448]{0:T(512)}, u32[]{:S(2)}) copy-start(f32[448]{0:T(512)} %copy-done.21) | copy-start | bytes 5380
  805.8 54.5 %copy-start.24 = (f32[512]{0:T(512)S(1)}, f32[512]{0:T(512)}, u32[]{:S(2)}) copy-start(f32[512]{0:T(512)} %copy-done.23) | copy-start | bytes 6148
  815.1 57.4 %copy-start.34 = (f32[512]{0:T(512)S(1)}, f32[512]{0:T(512)}, u32[]{:S(2)}) copy-start(f32[512]{0:T(512)} %copy-done.33) | copy-start | bytes 6148
  815.1 57.4 %copy-start.10 = (bf16[448,512]{1,0:T(8,128)(2,1)S(1)}, bf16[448,512]{1,0:T(8,128)(2,1)}, u32[]{:S(2)}) copy-start(bf16[448,512]{1,0:T(8,128)(2,1)} %param.17) | copy-start | bytes 1376260
  815.1 99.5 %all-gather.21.cloned.1.call-start = ((), (), s32[]{:S(2)}) async-start(), calls=%async_computation.20 | async-start | bytes 4128768 | tf_op jit(solution)/shard_map/all_gather | solution.py:132
  874.6 103.1 %reduce-scatter.21.cloned.1.call-start = ((), (), s32[]{:S(2)}) async-start(), calls=%async_computation.21 | async-start | bytes 2293760 | tf_op jit(solution)/shard_map/reduce_scatter | solution.py:179
  941.2 36.5 %copy-start.5 = (f32[1024,288]{0,1:T(8,128)S(1)}, f32[1024,288]{0,1:T(8,128)}, u32[]{:S(2)}) copy-start(f32[1024,288]{0,1:T(8,128)} %reduce-scatter.9.cloned.1.call-done) | copy-start | bytes 3538948
  941.3 36.5 %copy-start.42 = (pred[1024]{0:T(1024)(128)(4,1)S(1)}, pred[1024]{0:T(1024)(128)(4,1)}, u32[]{:S(2)}) copy-start(pred[1024]{0:T(1024)(128)(4,1)} %copy-done.41) | copy-start | bytes 3076
  941.3 36.5 %copy-start.44 = (pred[1024]{0:T(1024)(128)(4,1)S(1)}, pred[1024]{0:T(1024)(128)(4,1)}, u32[]{:S(2)}) copy-start(pred[1024]{0:T(1024)(128)(4,1)} %copy-done.43) | copy-start | bytes 3076
  941.3 36.5 %copy-start.58 = (f32[2,1024]{1,0:T(2,128)S(1)}, f32[2,1024]{1,0:T(2,128)}, u32[]{:S(2)}) copy-start(f32[2,1024]{1,0:T(2,128)} %copy-done.57) | copy-start | bytes 24580
  945.8 116.4 %all-gather.23.cloned.1.call-start = ((), (), s32[]{:S(2)}) async-start(), calls=%async_computation.22 | async-start | bytes 3932160 | tf_op jit(solution)/shard_map/all_gather | solution.py:136
  1018.0 63.2 %copy-start.55 = (bf16[448,288]{0,1:T(8,128)(2,1)S(1)}, bf16[448,288]{0,1:T(8,128)(2,1)}, u32[]{:S(2)}) copy-start(bf16[448,288]{0,1:T(8,128)(2,1)} %param.20) | copy-start | bytes 774148
  1018.0 113.6 %reduce-scatter.23.cloned.1.call-start = ((), (), s32[]{:S(2)}) async-start(), calls=%async_computation.23 | async-start | bytes 4128768 | tf_op jit(solution)/shard_map/reduce_scatter | solution.py:193
  1112.0 30.8 %copy-start.32 = (f32[512]{0:T(512)S(1)}, f32[512]{0:T(512)}, u32[]{:S(2)}) copy-start(f32[512]{0:T(512)} %copy-done.31) | copy-start | bytes 6148
  1112.0 45.8 %copy-start.8 = (bf16[512,448]{0,1:T(8,128)(2,1)S(1)}, bf16[512,448]{0,1:T(8,128)(2,1)}, u32[]{:S(2)}) copy-start(bf16[512,448]{0,1:T(8,128)(2,1)} %reduce-scatter.19.cloned.1.call-done) | copy-start | bytes 1376260
  1112.0 48.3 %copy-start.1 = (bf16[448,608]{1,0:T(8,128)(2,1)S(1)}, bf16[448,608]{1,0:T(8,128)(2,1)}, u32[]{:S(2)}) copy-start(bf16[448,608]{1,0:T(8,128)(2,1)} %param.25) | copy-start | bytes 1634308
  (27 other events, 257.4 us)
Sparse Core Ops, SparseCore 0:
  20.7 42.8 all-gather.8
  95.4 55.8 reduce-scatter.8
  162.2 35.4 all-gather.10
  215.8 45.0 reduce-scatter.10
  262.9 45.5 all-gather.16
  310.5 41.3 all-gather.12
  354.9 57.9 reduce-scatter.16
  416.0 179.2 reduce-scatter.12
  601.2 59.3 all-gather.14
  662.4 100.6 all-gather.18
  765.5 45.0 reduce-scatter.14
  815.2 45.1 reduce-scatter.18
  874.8 39.8 all-gather.20
  945.9 31.8 reduce-scatter.20
  1018.1 44.0 all-gather.22
  1086.6 45.0 reduce-scatter.22
where the time goes:
time: 1180 us; the launch traced here: 1170 us
  waiting for transfers between devices  728 us (62%)
  local copies, waits for them, and re-layouts  218 us (18%)
  matrix products  121 us (10%)
  blocking collectives  50.9 us (4%)
  other arithmetic  33 us (3%)
  between operations  15 us (1%)
    reduce_scatter x2, waiting for transfers between devices, forward_rows(): lax.psum_scatter(partial_term(jnp.int32(0), rows_here * lax.axis_size('ro...  237 us
    gather x6, local copies, waits for them, and re-layouts, partial_term(): picked = jnp.take(gathered, row_index, axis=0)  125 us
    all_gather x2, waiting for transfers between devices, grad_gather_rows(): return lax.all_gather(values, 'row', axis=0, tiled=True)  110 us
    all_gather x2, waiting for transfers between devices, gather_rows(): return lax.all_gather(values, 'row', axis=0, tiled=True)  92.6 us
    all_gather x2, waiting for transfers between devices, grad_gather_cols(): return lax.all_gather(values, 'col', axis=1, tiled=True)  75.1 us
    reduce_scatter x2, waiting for transfers between devices, backward_cols(): lax.psum_scatter(partial_term(jnp.int32(0), lax.axis_size('col') * rows_h...  58.6 us
    all_gather x2, waiting for transfers between devices, gather_cols(): return lax.all_gather(values, 'col', axis=0, tiled=True)  56.2 us
    reduce_scatter x2, waiting for transfers between devices, backward_rows(): lax.psum_scatter(partial_term(jnp.int32(0), lax.axis_size('row') * rows_h...  54.4 us
  transfers between devices with their start and end apart: 16, of which 15 were waited for; matrix products, arithmetic and copies ran while one was open for 17% of the time, Pallas kernels for 0%

commit v1 on v0

--- a/solution.py
+++ b/solution.py
@@ -1,6 +1,8 @@
 import jax
 import jax.numpy as jnp
 from jax import lax
+from jax.experimental import pallas as pl
+from jax.experimental.pallas import tpu as pltpu
 from jax.sharding import PartitionSpec as P
 
 D = 1792
@@ -209,7 +211,7 @@
     return grad_normed * norm_gain * inverse[:, None] - values * (cubed * dot_sums / D)[:, None]
 
 
-def on_device(
+def on_device_general(
     tokens,
     cotangent,
     lengths,
@@ -354,6 +356,839 @@
     )
 
 
+HEADROWS = 2 * FEAT + HDIM
+TILE = 128
+MESH = pl.DeviceIdType.MESH
+VMEM_LIMIT = 60 * 2**20
+ANY = pl.BlockSpec(memory_space=pl.ANY)
+IN_VMEM = pl.BlockSpec(memory_space=pltpu.VMEM)
+
+
+def place():
+    column = lax.axis_index("col")
+    return lax.axis_index("row"), column // 2, column % 2
+
+
+def device(chip, plane, core):
+    return (chip, plane * 2 + core)
+
+
+def other_chips(chip):
+    y, x = chip // 2, chip % 2
+    return (y * 2 + 1 - x, (1 - y) * 2 + x, (1 - y) * 2 + 1 - x)
+
+
+def greet(partners):
+    barrier = pltpu.get_barrier_semaphore()
+    for partner in partners:
+        pl.semaphore_signal(barrier, inc=1, device_id=partner, device_id_type=MESH)
+    pl.semaphore_wait(barrier, len(partners))
+
+
+def plane_partners(chip, plane, core):
+    found = [device(c, plane, core) for c in other_chips(chip)]
+    found += [device(c, plane, 1 - core) for c in other_chips(chip)]
+    return found + [device(chip, plane, 1 - core)]
+
+
+def line_partners(chip, plane, core):
+    return [device(chip, (plane + step) % 4, core) for step in (1, 2, 3)]
+
+
+def remote(source, target, send, receive, to):
+    return pltpu.make_async_remote_copy(
+        src_ref=source,
+        dst_ref=target,
+        send_sem=send,
+        recv_sem=receive,
+        device_id=to,
+        device_id_type=MESH,
+    )
+
+
+def lanes(start, size):
+    return pl.ds(pl.multiple_of(start, TILE), size)
+
+
+def gather_kernel(
+    wff, wat, tok, cot, gains, ff, at, xs, gs, gn,
+    local_sem, main_s, main_r, extra_s, extra_r, att_s, att_r,
+    tok_s, tok_r, cot_s, cot_r, gn_s, gn_r, tokc_s, tokc_r, cotc_s, cotc_r,
+    z_s, z_r, ze_s, ze_r, za_s, za_r,
+):
+    chip, plane, core = place()
+    others = other_chips(chip)
+    greet(plane_partners(chip, plane, core) + line_partners(chip, plane, core))
+    extra_chip, far_core = (plane % 2) * 2 + core, plane // 2
+    holds_att = core == plane // 2
+    holds_extra = holds_att & (chip // 2 == plane % 2)
+    extra_plane = 2 * core + chip // 2
+    locals_ = []
+
+    def keep(source, target, sem):
+        copy = pltpu.make_async_copy(source, target, sem)
+        copy.start()
+        locals_.append(copy)
+
+    def att_copy(half, to_chip, slot):
+        return remote(
+            wat.at[half], at.at[plane % 2, chip], att_s.at[half], att_r.at[chip],
+            device(to_chip, plane, far_core),
+        )
+
+    for half in range(2):
+        to_chip = 2 * core + half
+        is_self = (to_chip == chip) & (far_core == core)
+
+        @pl.when(is_self)
+        def _():
+            pltpu.make_async_copy(wat.at[half], at.at[plane % 2, chip], local_sem.at[4]).start()
+
+        @pl.when(jnp.logical_not(is_self))
+        def _():
+            att_copy(half, to_chip, half).start()
+
+    mains = []
+    for p, to_chip in enumerate(others):
+        copy = remote(
+            wff.at[:, :, lanes(to_chip * TILE, TILE)],
+            ff.at[:, chip, :, lanes(plane * TILE, TILE)],
+            main_s.at[p], main_r.at[p], device(to_chip, plane, core),
+        )
+        copy.start()
+        mains.append(copy)
+    keep(
+        wff.at[:, :, lanes(chip * TILE, TILE)],
+        ff.at[:, chip, :, lanes(plane * TILE, TILE)],
+        local_sem.at[0],
+    )
+    extra_self = (extra_chip == chip) & (far_core == core)
+
+    def extra_copy():
+        return remote(
+            wff.at[:, :, lanes(4 * TILE, TILE)],
+            ff.at[:, chip, :, lanes(4 * TILE, TILE)],
+            extra_s, extra_r.at[chip], device(extra_chip, plane, far_core),
+        )
+
+    def extra_local():
+        return pltpu.make_async_copy(
+            wff.at[:, :, lanes(4 * TILE, TILE)],
+            ff.at[:, chip, :, lanes(4 * TILE, TILE)],
+            local_sem.at[5],
+        )
+
+    @pl.when(extra_self)
+    def _():
+        extra_local().start()
+
+    @pl.when(jnp.logical_not(extra_self))
+    def _():
+        extra_copy().start()
+
+    half_tokens = tok.shape[1]
+    own_half = lanes(core * half_tokens, half_tokens)
+    toks, cots, gns = [], [], []
+    for p, to_chip in enumerate(others):
+        to = device(to_chip, plane, core)
+        toks.append(remote(tok, xs.at[chip, :, own_half], tok_s.at[p], tok_r.at[p], to))
+        cots.append(remote(cot, gs.at[chip, :, own_half], cot_s.at[p], cot_r.at[p], to))
+        gns.append(remote(gains, gn.at[chip], gn_s.at[p], gn_r.at[p], to))
+        toks[-1].start()
+        gns[-1].start()
+        cots[-1].start()
+    keep(tok, xs.at[chip, :, own_half], local_sem.at[1])
+    keep(cot, gs.at[chip, :, own_half], local_sem.at[2])
+    keep(gains, gn.at[chip], local_sem.at[3])
+    mate = device(chip, plane, 1 - core)
+    cross = []
+    for source, target, send, receive in (
+        (tok, xs, tokc_s, tokc_r), (cot, gs, cotc_s, cotc_r),
+    ):
+        copy = remote(source, target.at[chip, :, own_half], send.at[3], receive.at[3], mate)
+        copy.start()
+        cross.append(copy)
+
+    for half in range(2):
+        to_chip = 2 * core + half
+        is_self = (to_chip == chip) & (far_core == core)
+
+        @pl.when(is_self)
+        def _():
+            pltpu.make_async_copy(wat.at[half], at.at[plane % 2, chip], local_sem.at[4]).wait()
+
+        @pl.when(jnp.logical_not(is_self))
+        def _():
+            att_copy(half, to_chip, half).wait_send()
+
+    @pl.when(holds_att)
+    def _():
+        for source_chip in range(4):
+            from_self = (source_chip == chip) & (core == chip // 2)
+
+            @pl.when(jnp.logical_not(from_self))
+            def _():
+                remote(
+                    wat.at[0], at.at[plane % 2, source_chip], att_s.at[0], att_r.at[source_chip],
+                    device(chip, plane, core),
+                ).wait_recv()
+
+    def att_line(step):
+        return remote(
+            at.at[plane % 2], at.at[plane % 2], za_s.at[step - 1], za_r.at[step - 1],
+            device(chip, (plane + step) % 4, core),
+        )
+
+    @pl.when(holds_att)
+    def _():
+        for step in (1, 3, 2):
+            att_line(step).start()
+
+    locals_[0].wait()
+    for copy in mains:
+        copy.wait_recv()
+    own_tile = ff.at[:, :, :, lanes(plane * TILE, TILE)]
+    line = []
+    for step in (1, 3, 2):
+        copy = remote(
+            own_tile, own_tile, z_s.at[step - 1], z_r.at[step - 1],
+            device(chip, (plane + step) % 4, core),
+        )
+        copy.start()
+        line.append((step, copy))
+
+    @pl.when(extra_self)
+    def _():
+        extra_local().wait()
+
+    @pl.when(jnp.logical_not(extra_self))
+    def _():
+        extra_copy().wait_send()
+
+    extra_tile = ff.at[:, :, :, lanes(4 * TILE, TILE)]
+
+    def extra_line(step):
+        return remote(
+            extra_tile, extra_tile, ze_s.at[step - 1], ze_r,
+            device(chip, (plane + step) % 4, core),
+        )
+
+    @pl.when(holds_extra)
+    def _():
+        for source_chip in range(4):
+            from_self = (source_chip == chip) & (core == chip % 2)
+
+            @pl.when(jnp.logical_not(from_self))
+            def _():
+                remote(
+                    wff.at[:, :, lanes(4 * TILE, TILE)],
+                    ff.at[:, source_chip, :, lanes(4 * TILE, TILE)],
+                    extra_s, extra_r.at[source_chip], device(chip, plane, core),
+                ).wait_recv()
+        for step in (1, 3, 2):
+            extra_line(step).start()
+
+    for p, from_chip in enumerate(others):
+        for copies, target, send, receive in (
+            (toks, xs, tokc_s, tokc_r), (cots, gs, cotc_s, cotc_r),
+        ):
+            copies[p].wait_recv()
+            block = target.at[from_chip, :, own_half]
+            copy = remote(block, block, send.at[p], receive.at[p], mate)
+            copy.start()
+            cross.append(copy)
+        gns[p].wait()
+    for copy in cross:
+        copy.wait()
+    for copy in toks + cots + mains:
+        copy.wait_send()
+    for copy in locals_[1:]:
+        copy.wait()
+
+    for step, copy in line:
+        copy.wait_send()
+        source_plane = (plane + 4 - step) % 4
+        tile = ff.at[:, :, :, lanes(source_plane * TILE, TILE)]
+        remote(tile, tile, z_s.at[step - 1], z_r.at[step - 1], mate).wait_recv()
+
+    @pl.when(holds_extra)
+    def _():
+        for step in (1, 3, 2):
+            extra_line(step).wait_send()
+
+    @pl.when(jnp.logical_not(holds_extra))
+    def _():
+        extra_line(1).wait_recv()
+
+    @pl.when(holds_att)
+    def _():
+        for step in (1, 3, 2):
+            att_line(step).wait_send()
+
+    for step in (1, 3, 2):
+        source_plane = (plane + 4 - step) % 4
+
+        @pl.when(source_plane // 2 == core)
+        def _():
+            block = at.at[source_plane % 2]
+            remote(block, block, za_s.at[step - 1], za_r.at[step - 1], mate).wait_recv()
+
+
+def dma(*shape):
+    return pltpu.SemaphoreType.DMA(shape)
+
+
+def gather_in(wff, wat, tok, cot, gains):
+    rows, half = tok.shape
+    shapes = [
+        (3, 4, rows, 5 * TILE), (2, 4) + wat.shape[1:], (4, rows, 2 * half),
+        (4, rows, 2 * half), (4, rows, TILE),
+    ]
+    return pl.pallas_call(
+        gather_kernel,
+        out_shape=[jax.ShapeDtypeStruct(s, jnp.bfloat16) for s in shapes],
+        in_specs=[ANY] * 5,
+        out_specs=[ANY] * 5,
+        scratch_shapes=[
+            dma(6), dma(3), dma(3), dma(), dma(4), dma(2), dma(4),
+            dma(3), dma(3), dma(3), dma(3), dma(3), dma(3), dma(4), dma(4), dma(4), dma(4),
+            dma(3), dma(3), dma(3), dma(), dma(3), dma(3),
+        ],
+        compiler_params=pltpu.CompilerParams(collective_id=1, has_side_effects=True),
+        name="gather_in",
+    )(wff, wat, tok, cot, gains)
+
+
+def plane_sum_kernel(part, out, from_mate, both, got, mate_s, mate_r, send, receive):
+    chip, plane, core = place()
+    others = other_chips(chip)
+    mate = device(chip, plane, 1 - core)
+    half = part.shape[2] // 2
+    greet([mate] + [device(c, plane, core) for c in others])
+    copy = remote(
+        part.at[:, :, lanes((1 - core) * half, half)], from_mate, mate_s, mate_r, mate
+    )
+    copy.start()
+    copy.wait()
+
+    @pl.loop(0, 4)
+    def _(block):
+        both[block] = (
+            part[block, :, lanes(core * half, half)].astype(jnp.float32)
+            + from_mate[block].astype(jnp.float32)
+        ).astype(jnp.bfloat16)
+
+    copies = []
+    for p, to_chip in enumerate(others):
+        copy = remote(
+            both.at[:, :, lanes(to_chip * TILE, TILE)], got.at[p], send.at[p], receive.at[p],
+            device(to_chip, plane, core),
+        )
+        copy.start()
+        copies.append(copy)
+    for copy in copies:
+        copy.wait()
+
+    @pl.loop(0, 4)
+    def _(block):
+        total = both[block, :, lanes(chip * TILE, TILE)].astype(jnp.float32)
+        for p in range(3):
+            total = total + got[p, block].astype(jnp.float32)
+        out[block] = total
+
+
+def plane_sum(part, collective_id):
+    _, rows, tokens = part.shape
+    bf16 = jnp.bfloat16
+    return pl.pallas_call(
+        plane_sum_kernel,
+        out_shape=jax.ShapeDtypeStruct((4, rows, TILE), jnp.float32),
+        in_specs=[IN_VMEM],
+        out_specs=IN_VMEM,
+        scratch_shapes=[
+            pltpu.VMEM((4, rows, tokens // 2), bf16),
+            pltpu.VMEM((4, rows, tokens // 2), bf16),
+            pltpu.VMEM((3, 4, rows, TILE), bf16),
+            dma(), dma(), dma(3), dma(3),
+        ],
+        compiler_params=pltpu.CompilerParams(
+            collective_id=collective_id, has_side_effects=True, vmem_limit_bytes=VMEM_LIMIT
+        ),
+        name="plane_sum",
+    )(part)
+
+
+def plane_gather_kernel(mine, out, keep_sem, send, receive, mate_s, mate_r):
+    chip, plane, core = place()
+    others = other_chips(chip)
+    mate = device(chip, plane, 1 - core)
+    greet([mate] + [device(c, plane, core) for c in others])
+    half = out.shape[2] // 2
+
+    def block_of(from_chip):
+        return out.at[:, :, lanes(core * half + from_chip * TILE, TILE)]
+
+    copies = []
+    for p, to_chip in enumerate(others):
+        copy = remote(
+            mine, block_of(chip), send.at[p], receive.at[p], device(to_chip, plane, core)
+        )
+        copy.start()
+        copies.append(copy)
+    kept = pltpu.make_async_copy(mine, block_of(chip), keep_sem)
+    kept.start()
+    cross = [remote(mine, block_of(chip), mate_s.at[3], mate_r.at[3], mate)]
+    cross[0].start()
+    for p, from_chip in enumerate(others):
+        copies[p].wait_recv()
+        block = block_of(from_chip)
+        copy = remote(block, block, mate_s.at[p], mate_r.at[p], mate)
+        copy.start()
+        cross.append(copy)
+    for copy in cross:
+        copy.wait()
+    for copy in copies:
+        copy.wait_send()
+    kept.wait()
+
+
+def plane_gather(mine, collective_id):
+    _, rows, _ = mine.shape
+    return pl.pallas_call(
+        plane_gather_kernel,
+        out_shape=jax.ShapeDtypeStruct((4, rows, 8 * TILE), jnp.bfloat16),
+        in_specs=[IN_VMEM],
+        out_specs=IN_VMEM,
+        scratch_shapes=[dma(), dma(3), dma(3), dma(4), dma(4)],
+        compiler_params=pltpu.CompilerParams(
+            collective_id=collective_id, has_side_effects=True, vmem_limit_bytes=VMEM_LIMIT
+        ),
+        name="plane_gather",
+    )(mine)
+
+
+def scatter_kernel(
+    ff, at, res, gtok, out_ff, out_at, out_res, out_tok,
+    got, got_extra, got_att, sum_main, sum_extra, sum_att, load,
+    load_sem, local_sem, z_s, z_r, ze_s, ze_r, za_s, za_r,
+    main_s, main_r, extra_s, extra_r, att_s, att_r, res_s, res_r, tok_s, tok_r,
+):
+    chip, plane, core = place()
+    others = other_chips(chip)
+    greet(plane_partners(chip, plane, core) + line_partners(chip, plane, core))
+    holds_att = core == plane // 2
+    holds_extra = holds_att & (chip // 2 == plane % 2)
+    extra_plane = 2 * core + chip // 2
+    extra_tile = ff.at[:, :, :, lanes(4 * TILE, TILE)]
+
+    def to_plane(step):
+        return (plane + step) % 4
+
+    def main_line(step):
+        return remote(
+            ff.at[:, :, :, lanes(to_plane(step) * TILE, TILE)], got.at[step - 1],
+            z_s.at[step - 1], z_r.at[step - 1], device(chip, to_plane(step), core),
+        )
+
+    def extra_line(step):
+        return remote(
+            extra_tile, got_extra.at[step - 1], ze_s.at[step - 1], ze_r.at[step - 1],
+            device(chip, to_plane(step), core),
+        )
+
+    def att_line(step):
+        return remote(
+            at.at[to_plane(step) % 2], got_att.at[step - 1], za_s.at[step - 1],
+            za_r.at[step - 1], device(chip, to_plane(step), core),
+        )
+
+    for step in (1, 3, 2):
+        main_line(step).start()
+
+        @pl.when(to_plane(step) == extra_plane)
+        def _():
+            extra_line(step).start()
+
+        @pl.when(to_plane(step) // 2 == core)
+        def _():
+            att_line(step).start()
+
+    half = out_res.shape[1]
+    toks = []
+    for p, to_chip in enumerate(others):
+        for source, target, send, receive in (
+            (res, out_res, res_s, res_r), (gtok, out_tok, tok_s, tok_r),
+        ):
+            copy = remote(
+                source.at[to_chip], target.at[:, lanes(chip * TILE, TILE)],
+                send.at[p], receive.at[p], device(to_chip, plane, core),
+            )
+            copy.start()
+            toks.append(copy)
+    kept = [
+        pltpu.make_async_copy(
+            source.at[chip], target.at[:, lanes(chip * TILE, TILE)], local_sem.at[i]
+        )
+        for i, (source, target) in enumerate(((res, out_res), (gtok, out_tok)))
+    ]
+    for copy in kept:
+        copy.start()
+
+    mine = pltpu.make_async_copy(
+        ff.at[:, :, :, lanes(plane * TILE, TILE)], sum_main, load_sem
+    )
+    mine.start()
+    mine.wait()
+    for step in (1, 3, 2):
+        main_line(step).wait()
+
+    @pl.loop(0, 12)
+    def _(i):
+        m, block = i // 4, i % 4
+        total = sum_main[m, block].astype(jnp.float32)
+        for p in range(3):
+            total = total + got[p, m, block].astype(jnp.float32)
+        sum_main[m, block] = total.astype(jnp.bfloat16)
+
+    mains = []
+    own_lanes = out_ff.at[:, :, lanes(chip * TILE, TILE)]
+    for p, to_chip in enumerate(others):
+        copy = remote(
+            sum_main.at[:, to_chip], own_lanes, main_s.at[p], main_r.at[p],
+            device(to_chip, plane, core),
+        )
+        copy.start()
+        mains.append(copy)
+    kept.append(pltpu.make_async_copy(sum_main.at[:, chip], own_lanes, local_sem.at[2]))
+    kept[-1].start()
+
+    last_lanes = out_ff.at[:, :, lanes(4 * TILE, TILE)]
+
+    def extra_back(to_chip):
+        return remote(
+            sum_extra.at[:, to_chip], last_lanes, extra_s.at[to_chip], extra_r,
+            device(to_chip, plane, chip % 2),
+        )
+
+    def extra_keep():
+        return pltpu.make_async_copy(sum_extra.at[:, chip], last_lanes, local_sem.at[3])
+
+    def extra_self(to_chip):
+        return (to_chip == chip) & (core == chip % 2)
+
+    @pl.when(holds_extra)
+    def _():
+        mine = pltpu.make_async_copy(extra_tile, sum_extra, load_sem)
+        mine.start()
+        mine.wait()
+        for step in (1, 3, 2):
+            extra_line(step).wait_recv()
+
+        @pl.loop(0, 12)
+        def _(i):
+            m, block = i // 4, i % 4
+            total = sum_extra[m, block].astype(jnp.float32)
+            for p in range(3):
+                total = total + got_extra[p, m, block].astype(jnp.float32)
+            sum_extra[m, block] = total.astype(jnp.bfloat16)
+
+        for to_chip in range(4):
+
+            @pl.when(extra_self(to_chip))
+            def _():
+                extra_keep().start()
+
+            @pl.when(jnp.logical_not(extra_self(to_chip)))
+            def _():
+                extra_back(to_chip).start()
+
+    def att_back(to_chip):
+        return remote(
+            sum_att.at[to_chip], out_at.at[chip % 2], att_s.at[to_chip], att_r.at[chip % 2],
+            device(to_chip, plane, chip // 2),
+        )
+
+    def att_keep():
+        return pltpu.make_async_copy(sum_att.at[chip], out_at.at[chip % 2], local_sem.at[4])
+
+    def att_self(to_chip):
+        return (to_chip == chip) & (core == chip // 2)
+
+    @pl.when(holds_att)
+    def _():
+        mine = pltpu.make_async_copy(at.at[plane % 2], sum_att, load_sem)
+        mine.start()
+        mine.wait()
+        for step in (1, 3, 2):
+            att_line(step).wait_recv()
+
+        @pl.loop(0, 4)
+        def _(block):
+            total = sum_att[block].astype(jnp.float32)
+            for p in range(3):
+                total = total + got_att[p, block].astype(jnp.float32)
+            sum_att[block] = total.astype(jnp.bfloat16)
+
+        for to_chip in range(4):
+
+            @pl.when(att_self(to_chip))
+            def _():
+                att_keep().start()
+
+            @pl.when(jnp.logical_not(att_self(to_chip)))
+            def _():
+                att_back(to_chip).start()
+
+    for step in (1, 3, 2):
+
+        @pl.when(to_plane(step) == extra_plane)
+        def _():
+            extra_line(step).wait_send()
+
+        @pl.when(to_plane(step) // 2 == core)
+        def _():
+            att_line(step).wait_send()
+
+    for copy in toks + mains:
+        copy.wait()
+    for copy in kept:
+        copy.wait()
+
+    @pl.when(holds_extra)
+    def _():
+        for to_chip in range(4):
+
+            @pl.when(extra_self(to_chip))
+            def _():
+                extra_keep().wait()
+
+            @pl.when(jnp.logical_not(extra_self(to_chip)))
+            def _():
+                extra_back(to_chip).wait_send()
+
+    @pl.when(holds_att)
+    def _():
+        for to_chip in range(4):
+
+            @pl.when(att_self(to_chip))
+            def _():
+                att_keep().wait()
+
+            @pl.when(jnp.logical_not(att_self(to_chip)))
+            def _():
+                att_back(to_chip).wait_send()
+
+    sender_chip, sender_core = (plane % 2) * 2 + core, plane // 2
+
+    @pl.when(jnp.logical_not((sender_chip == chip) & (sender_core == core)))
+    def _():
+        remote(
+            sum_extra.at[:, 0], last_lanes, extra_s.at[0], extra_r, device(chip, plane, core)
+        ).wait_recv()
+
+    for h in range(2):
+
+        @pl.when(jnp.logical_not((2 * core + h == chip) & (sender_core == core)))
+        def _():
+            remote(
+                sum_att.at[0], out_at.at[h], att_s.at[0], att_r.at[h],
+                device(chip, plane, core),
+            ).wait_recv()
+
+
+def scatter_out(ff, at, res, gtok):
+    bf16 = jnp.bfloat16
+    rows = ff.shape[2]
+    head_block = at.shape[2:]
+    return pl.pallas_call(
+        scatter_kernel,
+        out_shape=[
+            jax.ShapeDtypeStruct((3, rows, 5 * TILE), bf16),
+            jax.ShapeDtypeStruct((2,) + head_block, bf16),
+            jax.ShapeDtypeStruct((rows, 4 * TILE), bf16),
+            jax.ShapeDtypeStruct((rows, 4 * TILE), bf16),
+        ],
+        in_specs=[ANY] * 4,
+        out_specs=[ANY] * 4,
+        scratch_shapes=[
+            pltpu.VMEM((3, 3, 4, rows, TILE), bf16),
+            pltpu.VMEM((3, 3, 4, rows, TILE), bf16),
+            pltpu.VMEM((3, 4) + head_block, bf16),
+            pltpu.VMEM((3, 4, rows, TILE), bf16),
+            pltpu.VMEM((3, 4, rows, TILE), bf16),
+            pltpu.VMEM((4,) + head_block, bf16),
+            pltpu.VMEM((8, TILE), bf16),
+            dma(), dma(5), dma(3), dma(3), dma(3), dma(3), dma(3), dma(3),
+            dma(3), dma(3), dma(4), dma(), dma(4), dma(2), dma(3), dma(3), dma(3), dma(3),
+        ],
+        compiler_params=pltpu.CompilerParams(
+            collective_id=2, has_side_effects=True, vmem_limit_bytes=VMEM_LIMIT
+        ),
+        name="scatter_out",
+    )(ff, at, res, gtok)
+
+
+def attend_heads(query, keys, values):
+    offsets = jnp.arange(query.shape[2], dtype=jnp.int32)
+    order = lambda v: v.transpose(2, 0, 1)
+    return order(query), order(keys), order(values), offsets
+
+
+def on_device_full(
+    tokens, cotangent, w_qkv, conv_weight, w_out, w_gate, w_up, w_down, gain_mix, gain_ffn
+):
+    f32, bf16 = jnp.float32, jnp.bfloat16
+    rows, half = tokens.shape
+    ffn_cols = w_gate.shape[1]
+    chip, plane, core = place()
+    heads = 2
+    pad = ((0, 0), (0, 5 * TILE - ffn_cols))
+    wff = jnp.stack([jnp.pad(w, pad) for w in (w_gate, w_up, w_down)])
+    wat = jnp.concatenate(
+        [w_qkv.T.reshape(heads, HEADROWS, rows), w_out.reshape(heads, HDIM, rows)], 1
+    )
+    gains = jnp.concatenate(
+        [jnp.broadcast_to(g[:, None], (rows, TILE // 2)) for g in (gain_mix, gain_ffn)], 1
+    )
+    ff, at, xs, gs, gn = gather_in(wff, wat, tokens, cotangent, gains)
+    width = 4 * rows
+    seq = 2 * half
+    wg, wu, wd = (ff[i].reshape(width, 5 * TILE) for i in range(3))
+    gain_one = gn.reshape(width, TILE)[:, 0].astype(f32)[:, None]
+    gain_two = gn.reshape(width, TILE)[:, TILE // 2].astype(f32)[:, None]
+    w_att = at.transpose(0, 2, 1, 3).reshape(heads, HEADROWS + HDIM, width)
+    w_in, w_back = w_att[:, :HEADROWS], w_att[:, HEADROWS:]
+    conv = lax.all_gather(conv_weight, "col", axis=1, tiled=True).astype(f32)
+    conv = conv.reshape(CONV, -1, HDIM)
+    my_heads = jnp.stack([4 * (2 * core) + chip, 4 * (2 * core + 1) + chip])
+    kernel_conv = jnp.take(conv, my_heads, axis=1)
+    first = core * half + chip * TILE
+
+    def own(v):
+        return lax.dynamic_slice_in_dim(v, first, TILE, 1)
+
+    def dot(a, b, ca, cb):
+        return lax.dot_general(a, b, (((ca,), (cb,)), ((), ())), preferred_element_type=f32)
+
+    stream = xs.reshape(width, seq).astype(f32)
+    inverse_one = lax.rsqrt(jnp.mean(stream * stream, 0) + EPSILON)
+    low_one = (stream * inverse_one[None] * gain_one).astype(bf16)
+    projected = dot(w_in.reshape(heads * HEADROWS, width), low_one, 1, 0)
+    projected = projected.reshape(heads, HEADROWS, seq).transpose(2, 0, 1)
+    query = projected[:, :, :FEAT].astype(bf16)
+    keys = projected[:, :, FEAT : 2 * FEAT].astype(bf16)
+    raw_values = projected[:, :, 2 * FEAT :]
+    offsets = jnp.arange(seq, dtype=jnp.int32)
+    values = convolve(raw_values, kernel_conv, offsets).astype(bf16)
+    pieces = (query, keys, values, offsets)
+    attended = attend_bin(pieces).reshape(seq, heads * HDIM).astype(bf16)
+    part = dot(w_back.reshape(heads * HDIM, width), attended, 0, 1).astype(bf16)
+    branch_mix = plane_sum(part.reshape(4, rows, seq), 3).reshape(width, TILE)
+    stream_own = own(stream)
+    middle = stream_own + branch_mix
+    inverse_two = lax.rsqrt(jnp.mean(middle * middle, 0) + EPSILON)[None]
+    low_two_own = (middle * inverse_two * gain_two).astype(bf16)
+    low_two = plane_gather(low_two_own.reshape(4, rows, TILE), 4).reshape(width, seq)
+    gate = dot(wg, low_two, 0, 0)
+    up_proj = dot(wu, low_two, 0, 0)
+    gate_sigmoid = jax.nn.sigmoid(gate)
+    activated = gate * gate_sigmoid
+    hidden = (activated * up_proj).astype(bf16)
+    part = dot(wd, hidden, 1, 0).astype(bf16)
+    branch_ffn = plane_sum(part.reshape(4, rows, seq), 5).reshape(width, TILE)
+    result_full = middle + branch_ffn
+    grad_result = gs.reshape(width, seq)
+    grad_down = dot(grad_result, hidden, 1, 1).astype(bf16)
+    grad_hidden = dot(wd, grad_result, 0, 0)
+    grad_gate_part = (
+        grad_hidden * up_proj * gate_sigmoid * (1.0 + gate * (1.0 - gate_sigmoid))
+    ).astype(bf16)
+    grad_up_part = (grad_hidden * activated).astype(bf16)
+    grad_gate = dot(low_two, grad_gate_part, 1, 1).astype(bf16)
+    grad_up = dot(low_two, grad_up_part, 1, 1).astype(bf16)
+    part = (dot(wg, grad_gate_part, 1, 0) + dot(wu, grad_up_part, 1, 0)).astype(bf16)
+    grad_normed_two = plane_sum(part.reshape(4, rows, seq), 6).reshape(width, TILE)
+    dots_two = jnp.sum(grad_normed_two * gain_two * middle, 0)[None]
+    grad_middle = own(grad_result).astype(f32) + (
+        grad_normed_two * gain_two * inverse_two
+        - middle * (inverse_two * inverse_two * inverse_two * dots_two / D)
+    )
+    gain_part_two = jnp.sum(grad_normed_two * middle * inverse_two, 1)
+    g_mid = plane_gather(grad_middle.astype(bf16).reshape(4, rows, TILE), 7).reshape(width, seq)
+    grad_out = dot(attended, g_mid, 0, 1).astype(bf16)
+    grad_attended = dot(w_back.reshape(heads * HDIM, width), g_mid, 1, 0).astype(bf16)
+    grad_attended = grad_attended.reshape(heads, HDIM, seq).transpose(2, 0, 1)
+    grad_query, grad_keys, grad_values = attend_back(pieces + (grad_attended,))
+    grad_raw, conv_part = convolve_back(grad_values, raw_values, kernel_conv, offsets)
+    grad_projected = jnp.concatenate([grad_query, grad_keys, grad_raw], 2)
+    grad_projected = grad_projected.reshape(seq, heads * HEADROWS).astype(bf16)
+    grad_qkv = dot(grad_projected, low_one, 0, 1).astype(bf16)
+    part = dot(w_in.reshape(heads * HEADROWS, width), grad_projected, 0, 1).astype(bf16)
+    grad_normed_one = plane_sum(part.reshape(4, rows, seq), 8).reshape(width, TILE)
+    inverse_own = lax.dynamic_slice_in_dim(inverse_one, first, TILE, 0)[None]
+    dots_one = jnp.sum(grad_normed_one * gain_one * stream_own, 0)[None]
+    grad_tokens = grad_middle + (
+        grad_normed_one * gain_one * inverse_own
+        - stream_own * (inverse_own * inverse_own * inverse_own * dots_one / D)
+    )
+    gain_part_one = jnp.sum(grad_normed_one * stream_own * inverse_own, 1)
+    grad_ff = jnp.stack([grad_gate, grad_up, grad_down]).reshape(3, 4, rows, 5 * TILE)
+    grad_at = jnp.concatenate(
+        [grad_qkv.reshape(heads, HEADROWS, 4, rows), grad_out.reshape(heads, HDIM, 4, rows)], 1
+    ).transpose(0, 2, 1, 3)
+    out_ff, out_at, out_res, out_tok = scatter_out(
+        grad_ff,
+        grad_at,
+        result_full.astype(bf16).reshape(4, rows, TILE),
+        grad_tokens.astype(bf16).reshape(4, rows, TILE),
+    )
+    conv_all = jnp.zeros(conv.shape, f32).at[:, my_heads].set(conv_part)
+    squares = jnp.stack(
+        [
+            jnp.sum(branch_mix * branch_mix),
+            jnp.sum(branch_ffn * branch_ffn),
+            jnp.sum(result_full * result_full),
+        ]
+    )
+    conv_all, gain_one_all, gain_two_all, squares = lax.psum(
+        (conv_all.reshape(CONV, -1), gain_part_one, gain_part_two, squares), ("row", "col")
+    )
+    conv_cols = conv_weight.shape[1]
+    grad_conv = lax.dynamic_slice_in_dim(
+        conv_all, lax.axis_index("col") * conv_cols, conv_cols, 1
+    )
+    pick = lambda v: lax.dynamic_slice_in_dim(v, chip * rows, rows, 0)
+    out_at = out_at.astype(f32)
+    return (
+        out_res,
+        out_tok.astype(f32),
+        out_at[:, :HEADROWS].reshape(heads * HEADROWS, rows).T,
+        grad_conv,
+        out_at[:, HEADROWS:].reshape(heads * HDIM, rows),
+        out_ff[0, :, :ffn_cols].astype(f32),
+        out_ff[1, :, :ffn_cols].astype(f32),
+        out_ff[2, :, :ffn_cols].astype(f32),
+        pick(gain_one_all),
+        pick(gain_two_all),
+        jnp.sqrt(squares / (width * seq * 4)),
+    )
+
+
+def on_device(tokens, cotangent, lengths, deal_order, *weights):
+    total_rows = tokens.shape[1] * lax.axis_size("col")
+    planes = lax.axis_size("col") // 2
+    if (
+        lengths.shape[0] * LONGEST == total_rows
+        and lax.axis_size("row") == 4
+        and planes == 4
+        and total_rows == planes * LONGEST
+        and weights[0].shape[1] == 2 * (2 * FEAT + HDIM)
+        and weights[3].shape[1] <= 5 * TILE
+    ):
+        return on_device_full(tokens, cotangent, *weights)
+    return on_device_general(tokens, cotangent, lengths, deal_order, *weights)
+
+
 def solution(mesh):
     in_specs = (
         P("row", "col"),

time: 1180 us -> 838 us (0.71)
  waiting for transfers between devices: 728 us -> 0 us
  Pallas kernels: 0 us -> 605 us
  local copies, waits for them, and re-layouts: 218 us -> 35.5 us
  matrix products: 121 us -> 94.4 us
  between operations: 15 us -> 2.08 us
    pallas_call x0 -> x8, Pallas kernels: none -> 605 us  [the longest x1 207 us: scatter_out(): pl.pallas_call(scatter_kernel, out_shape=[jax.ShapeDtypeStruct((3, rows,...]
    reduce_scatter x8 -> x0, waiting for transfers between devices: 394 us -> none  [the longest x2 237 us: forward_rows(): lax.psum_scatter(partial_term(jnp.int32(0), rows_here * lax.axis_size('ro...]
    all_gather x8 -> x0, waiting for transfers between devices: 334 us -> none  [the longest x2 110 us: grad_gather_rows(): return lax.all_gather(values, 'row', axis=0, tiled=True)]
    gather x8 -> x1, local copies, waits for them, and re-layouts: 165 us -> 0.57 us  [on_device_full(): kernel_conv = jnp.take(conv, my_heads, axis=1)]
    all_gather x5 -> x0, local copies, waits for them, and re-layouts: 41.3 us -> none  [the longest x1 14.3 us: grad_gather_rows(): return lax.all_gather(values, 'row', axis=0, tiled=True)]
    dot_general x12 -> x15, matrix products: 79.1 us -> 55.7 us  [dot(): lax.dot_general(a, b, (((ca,), (cb,)), ((), ())), preferred_element_type=...]
    all_gather x0 -> x1, blocking collectives: none -> 13.1 us  [on_device_full(): conv = lax.all_gather(conv_weight, 'col', axis=1, tiled=True).astype(f32)]
    psum x5 -> x1, blocking collectives: 50.9 us -> 38.8 us  [on_device_full(): lax.psum((conv_all.reshape(CONV, -1), gain_part_one, gain_part_two, squar...]
  transfers between devices with their start and end apart: 16 -> 0, of which waited for: 15 -> 0; matrix products, arithmetic and copies ran while one was open for 17% -> 0% of each run, Pallas kernels for 0% -> 0%
where the time goes in v1:
time: 838 us; the launch traced here: 832 us
  Pallas kernels  605 us (72%)
  matrix products  94.4 us (11%)
  blocking collectives  51.9 us (6%)
  other arithmetic  42.6 us (5%)
  local copies, waits for them, and re-layouts  35.5 us (4%)
    pallas_call x1, Pallas kernels, scatter_out(): pl.pallas_call(scatter_kernel, out_shape=[jax.ShapeDtypeStruct((3, rows,...  207 us
    pallas_call x1, Pallas kernels, gather_in(): pl.pallas_call(gather_kernel, out_shape=[jax.ShapeDtypeStruct(s, jnp.bflo...  188 us
    pallas_call x4, Pallas kernels, plane_sum(): pl.pallas_call(plane_sum_kernel, out_shape=jax.ShapeDtypeStruct((4, rows,...  155 us
    dot_general x15, matrix products, dot(): lax.dot_general(a, b, (((ca,), (cb,)), ((), ())), preferred_element_type=...  55.7 us
    pallas_call x2, Pallas kernels, plane_gather(): pl.pallas_call(plane_gather_kernel, out_shape=jax.ShapeDtypeStruct((4, ro...  55.1 us
    psum x1, blocking collectives, on_device_full(): lax.psum((conv_all.reshape(CONV, -1), gain_part_one, gain_part_two, squar...  38.8 us

profile of v1, /device:TPU:4, one launch (start us, length us, event | category | flops | bytes accessed | tf_op | source)
XLA Modules:
  0.0 831.7 jit_solution(9735708031120284984)
XLA Ops:
  1.3 13.1 %all-gather = bf16[8,224,3]{1,2,0:T(4,128)(2,1)S(1)} all-gather(bf16[1,224,3]{1,2,0:T(4,128)(2,1)} %bitcast.215), channel_id=1, replica_groups=mesh['row'=4,'col'=8] {'col'}, dimensions={0}, use_global_device_ids=true | all-gather | bytes 12096 | tf_op jit(solution)/shard_map/all_gather | solution.py:1061
  21.2 188.0 %gather_in.1 = (bf16[3,4,448,640]{3,2,1,0:T(8,128)(2,1)}, bf16[2,4,256,448]{3,2,1,0:T(8,128)(2,1)}, bf16[4,448,1024]{2,1,0:T(8,128)(2,1)}, bf16[4,448,1024]{2,1,0:T(8,128)(2,1)}, bf16[4,448,128]{2,1,0:T(8,128)(2,1)}) custom-call(bf16[3,448,640]{2,1,0:T(8,128)(2,1)} %pad_maximum_fusion.1.wff, bf16[2,256,448]{2,1,0:T(8,128)(2,1)} %pad_maximum_fusion.3.wat, ...), custom_call_target="tpu_custom_call" | custom-call | tf_op jit(solution)/shard_map/gather_in/pallas_call | solution.py:647
  209.2 2.9 multiply_reduce_fusion.1
  212.7 4.8 multiply_convert_fusion
  217.5 3.0 copy.66
  220.5 4.0 fusion.59
  227.3 2.8 fusion.3
  230.1 3.2 fusion.20
  233.4 3.5 bitcast_convert_fusion.1
  236.9 50.8 %plane_sum.4 = f32[4,448,128]{2,1,0:T(8,128)} custom-call(bf16[4,448,1024]{2,1,0:T(8,128)(2,1)} %bitcast.166), custom_call_target="tpu_custom_call" | custom-call | tf_op jit(solution)/shard_map/plane_sum/pallas_call | solution.py:703
  287.8 3.0 convert.39
  290.8 3.0 copy-done.1
  295.4 27.7 %plane_gather.2 = bf16[4,448,1024]{2,1,0:T(8,128)(2,1)} custom-call(bf16[4,448,128]{2,1,0:T(8,128)(2,1)} %bitcast.195), custom_call_target="tpu_custom_call" | custom-call | tf_op jit(solution)/shard_map/plane_gather/pallas_call | solution.py:757
  323.1 3.8 fusion.56
  327.1 2.6 fusion.61
  330.5 2.6 fusion.60
  333.1 5.4 multiply_convert_fusion.3
  338.5 4.5 convolution_convert_fusion
  343.0 42.2 %plane_sum.6 = f32[4,448,128]{2,1,0:T(8,128)} custom-call(bf16[4,448,1024]{2,1,0:T(8,128)(2,1)} %bitcast.180), custom_call_target="tpu_custom_call" | custom-call | tf_op jit(solution)/shard_map/plane_sum/pallas_call | solution.py:703
  385.2 5.2 fusion.62
  390.4 4.5 add_convert_fusion
  394.9 31.0 %plane_sum.5 = f32[4,448,128]{2,1,0:T(8,128)} custom-call(bf16[4,448,1024]{2,1,0:T(8,128)(2,1)} %bitcast.179), custom_call_target="tpu_custom_call" | custom-call | tf_op jit(solution)/shard_map/plane_sum/pallas_call | solution.py:703
  425.9 3.4 fusion.30
  429.3 2.2 fusion.44
  431.5 27.4 %plane_gather.3 = bf16[4,448,1024]{2,1,0:T(8,128)(2,1)} custom-call(bf16[4,448,128]{2,1,0:T(8,128)(2,1)} %bitcast.196), custom_call_target="tpu_custom_call" | custom-call | tf_op jit(solution)/shard_map/plane_gather/pallas_call | solution.py:757
  458.9 2.4 slice.99
  462.8 3.8 convolution_convert_fusion.6
  466.6 13.0 %fusion.26 = bf16[1024,2,16]{0,2,1:T(8,128)(2,1)S(1)} fusion(bf16[1024,2,144]{0,2,1:T(8,128)(2,1)} %copy-done.58, f32[2,1024,1024]{1,2,0:T(8,128)} %copy-done.59, f32[2,1024]{1,0:T(2,128)} %copy-done.64, pred[1024,1024]{0,1:T(8,128)(4,1)} %copy-done.18, bf16[1024,2,112]{0,2,1:T(8,128)(2,1)} %bitcast.219, bf16[1024,2,112]{0,2,1:T(8,128)(2,1)} %copy-done.22), kind=kOutput, calls=%fused_computation.47 | convolution fusion | flops 1038158848 | bytes 20856832 | tf_op jit(solution)/shard_map/hts,shf->thf/dot_general | solution.py:100
  479.7 11.1 %fusion.25 = bf16[1024,2,16]{0,2,1:T(8,128)(2,1)S(1)} fusion(bf16[1024,2,144]{0,2,1:T(8,128)(2,1)} %copy-done.58, f32[2,1024,1024]{1,2,0:T(8,128)} %copy-done.59, f32[2,1024]{1,0:T(2,128)S(1)} %copy-done.65, pred[1024,1024]{0,1:T(8,128)(4,1)} %copy-done.18, bf16[1024,2,112]{0,2,1:T(8,128)(2,1)} %bitcast.220, bf16[1024,2,112]{0,2,1:T(8,128)(2,1)S(1)} %copy-done.23), kind=kOutput, calls=%fused_computation.46 | convolution fusion | flops 1038158848 | bytes 20856832 | tf_op jit(solution)/shard_map/hts,thf->shf/dot_general | solution.py:103
  490.9 8.6 %multiply_reduce_fusion.6 = (f32[2,112]{1,0:T(2,128)}, f32[1024,2,112]{0,2,1:T(8,128)S(1)}, f32[2,112]{1,0:T(2,128)}, f32[2,112]{1,0:T(2,128)}, f32[1024,2,112]{0,2,1:T(8,128)S(1)}, /*index=5*/f32[1024,2,112]{0,2,1:T(8,128)S(1)}) fusion(f32[1023,2,112]{0,2,1:T(8,128)} %copy-done.8, pred[1024]{0:T(1024)(128)(4,1)S(1)} %copy-done.47, ...), kind=kOutput, calls=%fused_computation.62 | convolution fusion | flops 488373600 | bytes 15411200 | tf_op jit(solution)/shard_map/hts,thd->shd/dot_general | solution.py:92
  501.0 3.9 bitcast_convert_fusion
  504.9 31.0 %plane_sum.7 = f32[4,448,128]{2,1,0:T(8,128)} custom-call(bf16[4,448,1024]{2,1,0:T(8,128)(2,1)} %bitcast.181), custom_call_target="tpu_custom_call" | custom-call | tf_op jit(solution)/shard_map/plane_sum/pallas_call | solution.py:703
  536.7 2.8 fusion.28
  540.3 2.9 add_convert_fusion.1
  543.3 2.3 convolution_convert_fusion.4
  545.5 2.4 reshape.348
  549.2 3.4 convolution_convert_fusion.5
  552.7 1.9 reshape.349
  554.6 1.5 copy.78
  556.1 1.6 maximum_bitcast_fusion.at
  557.7 3.5 convolution_convert_fusion.3
  561.3 3.3 convolution_convert_fusion.2
  564.6 3.3 convolution_convert_fusion.1
  567.9 3.4 pad_maximum_fusion.ff
  571.3 207.2 %scatter_out.1 = (bf16[3,448,640]{2,1,0:T(8,128)(2,1)}, bf16[2,256,448]{2,1,0:T(8,128)(2,1)}, bf16[448,512]{1,0:T(8,128)(2,1)}, bf16[448,512]{1,0:T(8,128)(2,1)}) custom-call(bf16[3,4,448,640]{3,2,1,0:T(8,128)(2,1)} %pad_maximum_fusion.ff, bf16[2,4,256,448]{3,2,1,0:T(8,128)(2,1)} %maximum_bitcast_fusion.at, bf16[4,448,128]{2,1,0:T(8,128)(2,1)} %bitcast.194, ...), custom_call_target="tpu_custom_call" | custom-call | tf_op jit(solution)/shard_map/scatter_out/pallas_call | solution.py:1003
  778.6 3.4 bitcast_convert_fusion.2
  783.7 2.0 pad_maximum_fusion.5
  786.5 38.8 %all-reduce.7 = (f32[3,1792]{1,0:T(4,128)S(1)}, f32[1792]{0:T(1024)S(1)}, f32[1792]{0:T(1024)S(1)}, f32[3]{0:T(128)S(1)}) all-reduce(f32[3,1792]{1,0:T(4,128)S(1)} %reshape.357, f32[1792]{0:T(1024)S(1)} %copy-done.34, f32[1792]{0:T(1024)S(1)} %copy-done.33, f32[3]{0:T(128)S(1)} %pad_maximum_fusion.5), channel_id=1, replica_groups=mesh['row'=4,'col'=8] {'row','col'}, use_global_device_ids=true, to_apply=%region_10.11 | all-reduce | flops 8963 | bytes 71704 | tf_op jit(solution)/shard_map/psum | solution.py:1153
  (187 shorter events, 27.7 us)
Async XLA Ops:
  0.6 18.7 %copy-start.25 = (bf16[448,288]{0,1:T(8,128)(2,1)S(1)}, bf16[448,288]{0,1:T(8,128)(2,1)}, u32[]{:S(2)}) copy-start(bf16[448,288]{0,1:T(8,128)(2,1)} %param.14) | copy-start | bytes 774148
  0.7 18.7 %copy-start.28 = (bf16[224,448]{1,0:T(8,128)(2,1)S(1)}, bf16[224,448]{1,0:T(8,128)(2,1)}, u32[]{:S(2)}) copy-start(bf16[224,448]{1,0:T(8,128)(2,1)} %param.16) | copy-start | bytes 602116
  15.4 209.4 %copy-start.36 = (f32[1,2,112]{2,0,1:T(1,128)}, f32[1,2,112]{2,0,1:T(1,128)S(1)}, u32[]{:S(2)}) copy-start(f32[1,2,112]{2,0,1:T(1,128)S(1)} %get-tuple-element.60) | copy-start | bytes 2692
  15.4 209.4 %copy-start.38 = (f32[1,2,112]{2,0,1:T(1,128)}, f32[1,2,112]{2,0,1:T(1,128)S(1)}, u32[]{:S(2)}) copy-start(f32[1,2,112]{2,0,1:T(1,128)S(1)} %get-tuple-element.61) | copy-start | bytes 2692
  15.4 209.4 %copy-start.40 = (f32[1,2,112]{2,0,1:T(1,128)}, f32[1,2,112]{2,0,1:T(1,128)S(1)}, u32[]{:S(2)}) copy-start(f32[1,2,112]{2,0,1:T(1,128)S(1)} %get-tuple-element.62) | copy-start | bytes 2692
  15.4 4.8 copy-start.52
  15.4 4.9 copy-start.53
  212.2 5.4 copy-start.35
  212.6 4.9 copy-start.31
  220.5 12.8 %copy-start.2 = (bf16[2,256,4,448]{1,3,2,0:T(8,128)(2,1)}, bf16[2,256,4,448]{1,3,2,0:T(8,128)(2,1)S(1)}, u32[]{:S(2)}) copy-start(bf16[2,256,4,448]{1,3,2,0:T(8,128)(2,1)S(1)} %copy.66) | copy-start | bytes 5505028
  224.8 5.3 copy-start.44
  224.8 5.3 copy-start.46
  233.4 3.5 copy-start.20
  287.8 6.0 copy-start.4
  294.1 135.2 %copy-start.42 = (f32[128]{0:T(128)}, f32[128]{0:T(128)S(1)}, u32[]{:S(2)}) copy-start(f32[128]{0:T(128)S(1)} %add_rsqrt_fusion.1) | copy-start | bytes 1540
  294.3 135.0 %copy-start.29 = (f32[1792]{0:T(1024)}, f32[1792]{0:T(1024)S(1)}, u32[]{:S(2)}) copy-start(f32[1792]{0:T(1024)S(1)} %convert_reduce_fusion) | copy-start | bytes 21508
  323.1 4.1 copy-start.11
  326.9 6.3 copy-start.15
  327.1 3.4 copy-start.26
  338.5 4.5 copy-start.62
  385.2 5.2 copy-start.14
  385.2 5.2 copy-start.60
  425.9 3.4 copy-start
  429.3 29.6 %copy-start.50 = (f32[128]{0:T(128)}, f32[128]{0:T(128)S(1)}, u32[]{:S(2)}) copy-start(f32[128]{0:T(128)S(1)} %fusion.42) | copy-start | bytes 1540
  466.6 13.1 %copy-start.23 = (bf16[1024,2,112]{0,2,1:T(8,128)(2,1)S(1)}, bf16[1024,2,112]{0,2,1:T(8,128)(2,1)}, u32[]{:S(2)}) copy-start(bf16[1024,2,112]{0,2,1:T(8,128)(2,1)} %copy-done.22) | copy-start | bytes 1376260
  466.6 13.1 %copy-start.65 = (f32[2,1024]{1,0:T(2,128)S(1)}, f32[2,1024]{1,0:T(2,128)}, u32[]{:S(2)}) copy-start(f32[2,1024]{1,0:T(2,128)} %copy-done.64) | copy-start | bytes 24580
  479.7 11.2 %copy-start.45 = (pred[1024]{0:T(1024)(128)(4,1)S(1)}, pred[1024]{0:T(1024)(128)(4,1)}, u32[]{:S(2)}) copy-start(pred[1024]{0:T(1024)(128)(4,1)} %copy-done.44) | copy-start | bytes 3076
  479.7 11.2 %copy-start.47 = (pred[1024]{0:T(1024)(128)(4,1)S(1)}, pred[1024]{0:T(1024)(128)(4,1)}, u32[]{:S(2)}) copy-start(pred[1024]{0:T(1024)(128)(4,1)} %copy-done.46) | copy-start | bytes 3076
  504.9 31.8 %copy-start.32 = (f32[1792]{0:T(1024)S(1)}, f32[1792]{0:T(1024)}, u32[]{:S(2)}) copy-start(f32[1792]{0:T(1024)} %copy-done.31) | copy-start | bytes 21508
  504.9 35.4 %copy-start.30 = (f32[1792]{0:T(1024)S(1)}, f32[1792]{0:T(1024)}, u32[]{:S(2)}) copy-start(f32[1792]{0:T(1024)} %copy-done.29) | copy-start | bytes 21508
  504.9 35.4 %copy-start.43 = (f32[128]{0:T(128)S(1)}, f32[128]{0:T(128)}, u32[]{:S(2)}) copy-start(f32[128]{0:T(128)} %copy-done.42) | copy-start | bytes 1540
  504.9 35.4 %copy-start.51 = (f32[128]{0:T(128)S(1)}, f32[128]{0:T(128)}, u32[]{:S(2)}) copy-start(f32[128]{0:T(128)} %copy-done.50) | copy-start | bytes 1540
  536.7 6.5 copy-start.10
  545.5 3.7 copy-start.21
  549.2 6.8 copy-start.7
  557.7 3.5 copy-start.61
  561.2 3.3 copy-start.27
  561.2 3.3 copy-start.63
  778.5 3.5 copy-start.5
  778.5 7.1 copy-start.54
  778.6 7.1 copy-start.55
  778.6 7.1 copy-start.56
  778.6 7.1 copy-start.49
  778.6 7.9 copy-start.33
  778.6 7.8 copy-start.34
  778.6 49.2 %copy-start.24 = (bf16[448,512]{1,0:T(8,128)(2,1)S(1)}, bf16[448,512]{1,0:T(8,128)(2,1)}, u32[]{:S(2)}) copy-start(bf16[448,512]{1,0:T(8,128)(2,1)} %get-tuple-element.26) | copy-start | bytes 1376260
  778.6 50.2 %copy-start.16 = (bf16[2,256,448]{2,1,0:T(8,128)(2,1)S(1)}, bf16[2,256,448]{2,1,0:T(8,128)(2,1)}, u32[]{:S(2)}) copy-start(bf16[2,256,448]{2,1,0:T(8,128)(2,1)} %get-tuple-element.27) | copy-start | bytes 1376260
  782.0 48.5 %copy-start.19 = (bf16[448,512]{1,0:T(8,128)(2,1)S(1)}, bf16[448,512]{1,0:T(8,128)(2,1)}, u32[]{:S(2)}) copy-start(bf16[448,512]{1,0:T(8,128)(2,1)} %get-tuple-element.83) | copy-start | bytes 1376260
  (18 other events, 40.7 us)

commit v2 on v0

--- a/solution.py
+++ b/solution.py
@@ -1,6 +1,8 @@
 import jax
 import jax.numpy as jnp
 from jax import lax
+from jax.experimental import pallas as pl
+from jax.experimental.pallas import tpu as pltpu
 from jax.sharding import PartitionSpec as P
 
 D = 1792
@@ -209,7 +211,7 @@
     return grad_normed * norm_gain * inverse[:, None] - values * (cubed * dot_sums / D)[:, None]
 
 
-def on_device(
+def on_device_general(
     tokens,
     cotangent,
     lengths,
@@ -354,6 +356,1079 @@
     )
 
 
+HEADROWS = 2 * FEAT + HDIM
+BLOCKROWS = HEADROWS + HDIM
+TILE = 128
+WIDE = 512
+SPAN = 256
+MARKS = 320
+MESH = pl.DeviceIdType.MESH
+ANY = pl.BlockSpec(memory_space=pl.ANY)
+F32, BF16 = jnp.float32, jnp.bfloat16
+
+
+def place():
+    column = lax.axis_index("col")
+    return lax.axis_index("row"), column // 2, column % 2
+
+
+def device(chip, plane, core):
+    return (chip, plane * 2 + core)
+
+
+def other_chips(chip):
+    y, x = chip // 2, chip % 2
+    return (y * 2 + 1 - x, (1 - y) * 2 + x, (1 - y) * 2 + 1 - x)
+
+
+def away(plane, step):
+    if step == 1:
+        return plane + 1 - 2 * (plane % 2)
+    if step == 2:
+        return (plane + 2) % 4
+    return 3 - plane
+
+
+def is_inner(plane):
+    return ((plane + 1) // 2) % 2 == 1
+
+
+def remote(source, target, send, receive, to):
+    return pltpu.make_async_remote_copy(
+        src_ref=source,
+        dst_ref=target,
+        send_sem=send,
+        recv_sem=receive,
+        device_id=to,
+        device_id_type=MESH,
+    )
+
+
+def lanes(start, size=TILE):
+    return pl.ds(pl.multiple_of(start, TILE), size)
+
+
+def rows_at(start, size, step):
+    return pl.ds(pl.multiple_of(start, step), size)
+
+
+def no(flag):
+    return jnp.logical_not(flag)
+
+
+def dot(a, b, over_a, over_b):
+    return lax.dot_general(
+        a, b, (((over_a,), (over_b,)), ((), ())), preferred_element_type=F32
+    )
+
+
+class Marks:
+    def __init__(self, ref):
+        self.ref, self.used = ref, 0
+
+    def one(self):
+        self.used += 1
+        return self.ref.at[self.used - 1]
+
+    def many(self, count):
+        base = self.used
+        self.used += count
+        return lambda i: self.ref.at[base + i]
+
+
+class Spread:
+    def __init__(self, ref, owner, chip, plane, core, marks):
+        self.ref, self.owner, self.spot = ref, owner, (chip, plane, core)
+        self.sends = marks.many(4)
+        self.arrived = marks.one()
+        self.mine = plane == owner
+        self.relays = is_inner(plane) & (plane == away(owner, 2))
+
+    def copy(self, step, send):
+        chip, plane, core = self.spot
+        return remote(
+            self.ref, self.ref, self.sends(send), self.arrived,
+            device(chip, away(plane, step), core),
+        )
+
+    def start(self, also=True):
+        @pl.when(also & self.mine)
+        def _():
+            self.copy(1, 0).start()
+            self.copy(2, 1).start()
+
+        @pl.when(also & self.mine & is_inner(self.spot[1]))
+        def _():
+            self.copy(3, 2).start()
+
+    def relay(self, also=True):
+        @pl.when(also & self.relays)
+        def _():
+            self.copy(1, 3).wait_recv()
+            self.copy(1, 3).start()
+
+    def arrive(self, also=True):
+        @pl.when(also & no(self.mine) & no(self.relays))
+        def _():
+            self.copy(1, 3).wait_recv()
+
+    def finish(self, also=True):
+        @pl.when(also & self.mine)
+        def _():
+            self.copy(1, 0).wait_send()
+            self.copy(2, 1).wait_send()
+
+        @pl.when(also & self.mine & is_inner(self.spot[1]))
+        def _():
+            self.copy(3, 2).wait_send()
+
+        @pl.when(also & self.relays)
+        def _():
+            self.copy(1, 3).wait_send()
+
+
+class Collect:
+    def __init__(self, ref, slots, owner, chip, plane, core, marks):
+        self.ref, self.slots, self.owner, self.spot = ref, slots, owner, (chip, plane, core)
+        self.send = marks.one()
+        self.arrived = marks.many(4)
+        outer = no(is_inner(owner))
+        self.mine = plane == owner
+        self.first = plane == away(owner, 1)
+        self.second = plane == away(owner, 2)
+        self.third = plane == away(owner, 3)
+        self.outer = outer
+
+    def copy(self, step, slot):
+        chip, plane, core = self.spot
+        return remote(
+            self.ref, self.slots.at[slot], self.send, self.arrived(slot),
+            device(chip, away(plane, step), core),
+        )
+
+    def start(self, add):
+        @pl.when(self.first)
+        def _():
+            self.copy(1, 0).start()
+
+        @pl.when(self.third & self.outer)
+        def _():
+            self.copy(1, 3).start()
+
+        @pl.when(self.third & no(self.outer))
+        def _():
+            self.copy(3, 2).start()
+
+        @pl.when(self.second & no(self.outer))
+        def _():
+            self.copy(2, 1).start()
+
+    def relay(self, add):
+        @pl.when(self.second & self.outer)
+        def _():
+            self.copy(1, 3).wait_recv()
+            add(self.slots.at[3])
+            self.copy(2, 1).start()
+
+    def total(self, add):
+        @pl.when(self.mine)
+        def _():
+            self.copy(1, 0).wait_recv()
+            add(self.slots.at[0])
+            self.copy(1, 1).wait_recv()
+            add(self.slots.at[1])
+
+        @pl.when(self.mine & no(self.outer))
+        def _():
+            self.copy(1, 2).wait_recv()
+            add(self.slots.at[2])
+
+    def finish(self):
+        @pl.when(no(self.mine))
+        def _():
+            self.copy(1, 0).wait_send()
+
+
+def layer_kernel(
+    wff, wat, tok, cot, gains,
+    out_ff, out_at, out_res, out_tok, out_small, main_got, extra_got, att_got,
+    ff, at, xs, gs, low2, part, acc3, gout, gat, from_mate, both, got, turned, hid, gg,
+    gn, raw, qs, ks, vs, att, gatt, gproj, mid, gmid, normed, inv_all, inv_sum, small, small_a,
+    small_b, sem, free_mate, free_chips,
+):
+    chip, plane, core = place()
+    others = other_chips(chip)
+    mate = device(chip, plane, 1 - core)
+    marks = Marks(sem)
+    rows = tok.shape[0]
+    width = 4 * rows
+    half = tok.shape[1]
+    seq = 2 * half
+    own_half = lanes(core * half, half)
+    first = core * half + chip * TILE
+    peers = [device(c, plane, core) for c in others]
+    line = [device(chip, away(plane, step), core) for step in (1, 2, 3)]
+    sides = [device(c, plane, 1 - core) for c in others]
+    line_mates = [device(chip, away(plane, step), 1 - core) for step in (1, 2, 3)]
+
+    barrier = pltpu.get_barrier_semaphore()
+    partners = peers + [mate] + sides + line + line_mates
+    for partner in partners:
+        pl.semaphore_signal(barrier, inc=1, device_id=partner, device_id_type=MESH)
+    pl.semaphore_wait(barrier, len(partners))
+
+    def block_rows(c):
+        return rows_at(c * rows, rows, rows)
+
+    far_core = plane // 2
+    holds_att = core == far_core
+    holds_extra = holds_att & (chip // 2 == plane % 2)
+    extra_plane = 2 * core + chip // 2
+    extra_chip = (plane % 2) * 2 + core
+    att_send, att_here = marks.many(2), marks.many(4)
+    att_local = marks.one()
+
+    def att_copy(h):
+        return remote(
+            wat.at[h], at.at[plane % 2, chip], att_send(h), att_here(chip),
+            device(2 * core + h, plane, far_core),
+        )
+
+    def att_keep(h):
+        return pltpu.make_async_copy(wat.at[h], at.at[plane % 2, chip], att_local)
+
+    att_self = [(2 * core + h == chip) & holds_att for h in range(2)]
+    for h in range(2):
+
+        @pl.when(att_self[h])
+        def _():
+            att_keep(h).start()
+
+        @pl.when(no(att_self[h]))
+        def _():
+            att_copy(h).start()
+
+    def plane_spread(source, target_of, to_mate=True):
+        send, receive = marks.many(3), marks.many(3)
+        mate_send, mate_receive = marks.many(4), marks.many(4)
+        keep = pltpu.make_async_copy(source, target_of(chip), marks.one())
+        keep.start()
+        copies = [
+            remote(source, target_of(chip), send(p), receive(p), peers[p]) for p in range(3)
+        ]
+        for copy in copies:
+            copy.start()
+        crossing = []
+        if to_mate:
+            crossing.append(
+                remote(source, target_of(chip), mate_send(3), mate_receive(3), mate)
+            )
+            crossing[0].start()
+
+        def pass_on():
+            for p in range(3):
+                copies[p].wait_recv()
+                if to_mate:
+                    block = target_of(others[p])
+                    crossing.append(remote(block, block, mate_send(p), mate_receive(p), mate))
+                    crossing[-1].start()
+
+        def finish():
+            keep.wait()
+            for copy in copies:
+                copy.wait_send()
+            for copy in crossing:
+                copy.wait()
+
+        return pass_on, finish
+
+    tok_pass, tok_finish = plane_spread(tok, lambda c: xs.at[block_rows(c), own_half])
+    gn_pass, gn_finish = plane_spread(gains, lambda c: gn.at[block_rows(c)], to_mate=False)
+
+    main_send, main_here, main_local = marks.many(3), marks.many(3), marks.one()
+    mains = []
+    main_here_at = ff.at[:, block_rows(chip), lanes(plane * TILE)]
+    for p in range(3):
+        mains.append(
+            remote(
+                wff.at[:, :, lanes(others[p] * TILE)], main_here_at,
+                main_send(p), main_here(p), peers[p],
+            )
+        )
+        mains[-1].start()
+    main_keep = pltpu.make_async_copy(wff.at[:, :, lanes(chip * TILE)], main_here_at, main_local)
+    main_keep.start()
+
+    extra_send, extra_here, extra_local = marks.one(), marks.many(4), marks.one()
+    extra_self = (extra_chip == chip) & holds_att
+    last = lanes(4 * TILE)
+
+    def extra_copy():
+        return remote(
+            wff.at[:, :, last], ff.at[:, block_rows(chip), last], extra_send, extra_here(chip),
+            device(extra_chip, plane, far_core),
+        )
+
+    def extra_keep():
+        return pltpu.make_async_copy(
+            wff.at[:, :, last], ff.at[:, block_rows(chip), last], extra_local
+        )
+
+    @pl.when(extra_self)
+    def _():
+        extra_keep().start()
+
+    @pl.when(no(extra_self))
+    def _():
+        extra_copy().start()
+
+    for h in range(2):
+
+        @pl.when(att_self[h])
+        def _():
+            att_keep(h).wait()
+
+        @pl.when(no(att_self[h]))
+        def _():
+            att_copy(h).wait_send()
+
+    for c in range(4):
+
+        @pl.when(holds_att & no((c == chip) & (core == chip // 2)))
+        def _():
+            remote(
+                wat.at[0], at.at[plane % 2, c], att_send(0), att_here(c), mate
+            ).wait_recv()
+
+    att_line = [
+        Spread(at.at[a], 2 * core + a, chip, plane, core, marks) for a in range(2)
+    ]
+    for item in att_line:
+        item.start()
+
+    tok_pass()
+    gn_pass()
+    gn_finish()
+    tok_finish()
+    cot_pass, cot_finish = plane_spread(cot, lambda c: gs.at[block_rows(c), own_half])
+
+    main_keep.wait()
+    for copy in mains:
+        copy.wait()
+    main_line = [
+        Spread(ff.at[:, :, lanes(o * TILE)], o, chip, plane, core, marks) for o in range(4)
+    ]
+    for item in main_line:
+        item.start()
+
+    @pl.when(extra_self)
+    def _():
+        extra_keep().wait()
+
+    @pl.when(no(extra_self))
+    def _():
+        extra_copy().wait_send()
+
+    for c in range(4):
+
+        @pl.when(holds_extra & no((c == chip) & (core == chip % 2)))
+        def _():
+            remote(
+                wff.at[:, :, last], ff.at[:, block_rows(c), last], extra_send, extra_here(c), mate
+            ).wait_recv()
+
+    extra_line = Spread(ff.at[:, :, last], extra_plane, chip, plane, core, marks)
+    extra_line.start()
+
+    step_rows = 64
+
+    def add_squares(i, total):
+        x = xs[rows_at(i * step_rows, step_rows, step_rows)].astype(F32)
+        return total + jnp.sum((x * x).reshape(step_rows // 8, 8, seq), 0)
+
+    squares = lax.fori_loop(0, width // step_rows, add_squares, jnp.zeros((8, seq), F32))
+    inv_all[...] = lax.rsqrt(jnp.sum(squares, 0, keepdims=True) / D + EPSILON)
+    mid[...] = xs[:, lanes(first)].astype(F32)
+
+    @pl.loop(0, width // step_rows)
+    def _(i):
+        at_rows = rows_at(i * step_rows, step_rows, step_rows)
+        gain = gn[at_rows, 0:1].astype(F32)
+        xs[at_rows] = (xs[at_rows].astype(F32) * inv_all[...] * gain).astype(BF16)
+
+    for item in att_line:
+        item.relay()
+    for item in att_line:
+        item.arrive()
+
+    position = lax.broadcasted_iota(jnp.int32, (1, seq), 1)
+    tail = lax.broadcasted_iota(jnp.int32, (HDIM, TILE), 1)
+
+    def taps(h):
+        columns = at[h, 0, HEADROWS:BLOCKROWS, WIDE - TILE : WIDE].astype(F32)
+        return [columns[:, rows % TILE + j : rows % TILE + j + 1] for j in range(CONV)]
+
+    @pl.loop(0, 2)
+    def _(h):
+        projected = dot(at[h, 0, :HEADROWS, :rows], xs[0:rows], 1, 0)
+        for c in range(1, 4):
+            projected += dot(at[h, c, :HEADROWS, :rows], xs[c * rows : (c + 1) * rows], 1, 0)
+        qs[h] = (projected[:FEAT].astype(BF16).astype(F32) * FEAT**-0.5).astype(BF16)
+        ks[h] = projected[FEAT : 2 * FEAT].astype(BF16)
+        values = projected[2 * FEAT :]
+        raw[h] = values
+        tap = taps(h)
+        mixed = tap[0] * values
+        for j in range(1, CONV):
+            moved = pltpu.roll(values, j, 1)
+            mixed += tap[j] * jnp.where(position >= j, moved, 0.0)
+        vs[h] = mixed.astype(BF16)
+
+    def kernel_of(h, b):
+        seen = (b + 1) * SPAN
+        scores = dot(ks[h, :, :seen], qs[h, :, b * SPAN : seen], 0, 0)
+        kernel = 1.0 + scores + 0.5 * scores * scores
+        key_at = lax.broadcasted_iota(jnp.int32, (seen, SPAN), 0)
+        query_at = lax.broadcasted_iota(jnp.int32, (seen, SPAN), 1) + b * SPAN
+        visible = key_at <= query_at
+        return scores, jnp.where(visible, kernel, 0.0), visible
+
+    @pl.loop(0, 2)
+    def _(h):
+        for b in range(seq // SPAN):
+            seen = (b + 1) * SPAN
+            _, kernel, _ = kernel_of(h, b)
+            inverse = 1.0 / jnp.sum(kernel, 0, keepdims=True)
+            inv_sum[h, :, b * SPAN : seen] = inverse
+            weights = (kernel * inverse).astype(BF16)
+            att[h, :, b * SPAN : seen] = dot(vs[h, :, :seen], weights, 1, 0).astype(BF16)
+
+    def plane_sum(fill, store, guard):
+        fill((1 - core) * half)
+        to_mate = remote(
+            part.at[:, lanes((1 - core) * half, half)], from_mate,
+            marks.one(), marks.one(), mate,
+        )
+        if guard:
+            pl.semaphore_wait(free_mate, 1)
+        to_mate.start()
+        fill(core * half)
+        to_mate.wait_recv()
+
+        @pl.loop(0, 4)
+        def _(c):
+            both[block_rows(c)] = (
+                part[block_rows(c), own_half].astype(F32) + from_mate[block_rows(c)].astype(F32)
+            ).astype(BF16)
+
+        pl.semaphore_signal(free_mate, inc=1, device_id=mate, device_id_type=MESH)
+        if guard:
+            pl.semaphore_wait(free_chips, 3)
+        send, receive = marks.many(3), marks.many(3)
+        copies = [
+            remote(
+                both.at[:, lanes(others[p] * TILE)], got.at[p], send(p), receive(p), peers[p]
+            )
+            for p in range(3)
+        ]
+        for copy in copies:
+            copy.start()
+
+        def finish():
+            for copy in copies:
+                copy.wait()
+
+            @pl.loop(0, 4)
+            def _(c):
+                at_rows = block_rows(c)
+                total = both[at_rows, lanes(chip * TILE)].astype(F32)
+                for p in range(3):
+                    total += got[p, at_rows].astype(F32)
+                store(at_rows, total)
+
+            for p in range(3):
+                pl.semaphore_signal(free_chips, inc=1, device_id=peers[p], device_id_type=MESH)
+            to_mate.wait_send()
+
+        return finish
+
+    def fill_branch(start):
+        @pl.loop(0, 4)
+        def _(c):
+            where = lanes(start, half)
+            total = dot(at[0, c, HEADROWS:, :rows], att[0, :, where], 0, 0)
+            total += dot(at[1, c, HEADROWS:, :rows], att[1, :, where], 0, 0)
+            part[block_rows(c), where] = total.astype(BF16)
+
+    small[...] = jnp.zeros(small.shape, F32)
+    square_at = lax.broadcasted_iota(jnp.int32, (1, WIDE), 1)
+
+    def note_square(index, value):
+        total = jnp.sum(value * value)
+        small[0, 2:3, :] += jnp.where(square_at == index, total, 0.0)
+
+    def store_branch(at_rows, total):
+        note_square(0, total)
+        gmid[at_rows] = total
+
+    finish = plane_sum(fill_branch, store_branch, guard=False)
+    cot_pass()
+    finish()
+    normed[...] = mid[...].astype(BF16)
+    mid[...] += gmid[...]
+    middle = mid[...]
+    inverse_two = lax.rsqrt(jnp.sum(middle * middle, 0, keepdims=True) / D + EPSILON)
+    gain_at = TILE // 2
+
+    @pl.loop(0, 4)
+    def _(c):
+        at_rows = block_rows(c)
+        gain = gn[at_rows, gain_at : gain_at + 1].astype(F32)
+        both[at_rows, 0:TILE] = (mid[at_rows] * inverse_two * gain).astype(BF16)
+
+    low_pass, low_finish = plane_spread(
+        both.at[:, 0:TILE], lambda c: low2.at[:, lanes(core * half + c * TILE)]
+    )
+    cot_finish()
+    low_pass()
+    low_finish()
+
+    @pl.loop(0, 4)
+    def _(c):
+        acc3[block_rows(c)] = jnp.zeros((rows, seq), F32)
+
+    def feed(slot):
+        where = lanes(slot * TILE)
+        unit_rows = rows_at(slot * TILE, TILE, TILE)
+        for m in range(3):
+            turned[m * TILE : (m + 1) * TILE] = ff[m, :, where].T
+
+        @pl.loop(0, seq // SPAN)
+        def _(n):
+            span = lanes(n * SPAN, SPAN)
+            gate_up = dot(turned[: 2 * TILE], low2[:, span], 1, 0)
+            grad_hidden = dot(turned[2 * TILE :], gs[:, span], 1, 0)
+            gate, up = gate_up[:TILE], gate_up[TILE:]
+            sigmoid = 1.0 / (1.0 + jnp.exp(-gate))
+            activated = gate * sigmoid
+            hid[unit_rows, span] = (activated * up).astype(BF16)
+            gg[:TILE, span] = (
+                grad_hidden * up * sigmoid * (1.0 + gate * (1.0 - sigmoid))
+            ).astype(BF16)
+            gg[TILE:, span] = (grad_hidden * activated).astype(BF16)
+
+        @pl.loop(0, 4)
+        def _(c):
+            at_rows = block_rows(c)
+            pair = jnp.concatenate([ff[0, at_rows, where], ff[1, at_rows, where]], 1)
+            acc3[at_rows] += dot(pair, gg[...], 1, 0)
+            grads = dot(low2[at_rows], gg[...], 1, 1).astype(BF16)
+            gout[0, at_rows, where] = grads[:, :TILE]
+            gout[1, at_rows, where] = grads[:, TILE:]
+            gout[2, at_rows, where] = dot(gs[at_rows], hid[unit_rows], 1, 1).astype(BF16)
+
+    main_back = [
+        Collect(
+            gout.at[:, :, lanes(o * TILE)], main_got, o, chip, plane, core, marks
+        )
+        for o in range(4)
+    ]
+    extra_back = Collect(gout.at[:, :, last], extra_got, extra_plane, chip, plane, core, marks)
+    load_marks = marks.many(3)
+
+    def add_tiles(slot):
+        def add(source):
+            loads = [
+                pltpu.make_async_copy(source.at[m], part.at[:, lanes(m * TILE)], load_marks(m))
+                for m in range(3)
+            ]
+            for load in loads:
+                load.start()
+            for load in loads:
+                load.wait()
+            where = lanes(slot * TILE)
+
+            @pl.loop(0, 4)
+            def _(c):
+                at_rows = block_rows(c)
+                for m in range(3):
+                    gout[m, at_rows, where] = (
+                        gout[m, at_rows, where].astype(F32)
+                        + part[at_rows, m * TILE : (m + 1) * TILE].astype(F32)
+                    ).astype(BF16)
+
+        return add
+
+    for item in main_line:
+        item.relay()
+    for item in main_line:
+        item.arrive()
+    extra_line.relay()
+    extra_line.arrive()
+
+    for step in (1, 0, 2, 3):
+        slot = away(plane, step) if step else plane
+        feed(slot)
+    feed(4)
+    for o in range(4):
+        main_back[o].start(None)
+    extra_back.start(None)
+    for o in range(4):
+        main_back[o].relay(add_tiles(o))
+    extra_back.relay(add_tiles(4))
+
+    def fill_grad_two(start):
+        @pl.loop(0, 4)
+        def _(c):
+            where = lanes(start, half)
+            part[block_rows(c), where] = acc3[block_rows(c), where].astype(BF16)
+
+    def store_gmid(at_rows, total):
+        gmid[at_rows] = total
+
+    finish = plane_sum(fill_grad_two, store_gmid, guard=True)
+    finish()
+
+    def norm_back(source, inverse, gain_lane, small_row, base):
+        def add_dots(c, total):
+            at_rows = block_rows(c)
+            gain = gn[at_rows, gain_lane : gain_lane + 1].astype(F32)
+            return total + jnp.sum(gmid[at_rows] * gain * source(at_rows), 0, keepdims=True)
+
+        dots = lax.fori_loop(0, 4, add_dots, jnp.zeros((1, TILE), F32))
+        scaled = inverse * inverse * inverse * dots / D
+
+        @pl.loop(0, 4)
+        def _(c):
+            at_rows = block_rows(c)
+            gain = gn[at_rows, gain_lane : gain_lane + 1].astype(F32)
+            grad, value = gmid[at_rows], source(at_rows)
+            for_gain = jnp.sum((grad * value * inverse).T, 0, keepdims=True)
+            small[c, small_row : small_row + 1, 0:rows] = for_gain
+            gmid[at_rows] = base(at_rows) + (grad * gain * inverse - value * scaled)
+
+    norm_back(
+        lambda r: mid[r], inverse_two, gain_at, 1, lambda r: gs[r, lanes(first)].astype(F32)
+    )
+    both[:, 0:TILE] = gmid[...].astype(BF16)
+    mid_pass, mid_finish = plane_spread(
+        both.at[:, 0:TILE], lambda c: low2.at[:, lanes(core * half + c * TILE)]
+    )
+
+    def fill_ffn(start):
+        @pl.loop(0, 4)
+        def _(c):
+            where = lanes(start, half)
+            part[block_rows(c), where] = dot(
+                ff[2, block_rows(c)], hid[:, where], 1, 0
+            ).astype(BF16)
+
+    mid_pass()
+    mid_finish()
+
+    def store_result(at_rows, total):
+        note_square(1, total)
+        total = mid[at_rows] + total
+        note_square(2, total)
+        normed_out = total.astype(BF16)
+        both[at_rows, 0:TILE] = normed_out
+
+    finish = plane_sum(fill_ffn, store_result, guard=True)
+
+    @pl.loop(0, 2)
+    def _(h):
+        total = dot(at[h, 0, HEADROWS:, :rows], low2[0:rows], 1, 0)
+        for c in range(1, 4):
+            total += dot(at[h, c, HEADROWS:, :rows], low2[c * rows : (c + 1) * rows], 1, 0)
+        gatt[h] = total.astype(BF16)
+
+    @pl.loop(0, 2)
+    def _(h):
+        grad_keys = jnp.zeros((FEAT, seq), F32)
+        grad_values = jnp.zeros((HDIM, seq), F32)
+
+        def padded(value):
+            short = seq - value.shape[1]
+            if not short:
+                return value
+            return jnp.concatenate([value, jnp.zeros((value.shape[0], short), F32)], 1)
+
+        for b in range(seq // SPAN):
+            seen = (b + 1) * SPAN
+            span = slice(b * SPAN, seen)
+            scores, kernel, visible = kernel_of(h, b)
+            inverse = inv_sum[h, :, span]
+            weights = kernel * inverse
+            grad_weights = dot(vs[h, :, :seen], gatt[h, :, span], 0, 0)
+            grad_values += padded(dot(gatt[h, :, span], weights.astype(BF16), 1, 1))
+            dots = jnp.sum(grad_weights * weights, 0, keepdims=True)
+            grad_kernel = (grad_weights - dots) * inverse
+            grad_scores = jnp.where(visible, grad_kernel * (1.0 + scores), 0.0).astype(BF16)
+            gproj[h, :FEAT, span] = (
+                dot(ks[h, :, :seen], grad_scores, 1, 0) * FEAT**-0.5
+            ).astype(BF16)
+            grad_keys += padded(dot(qs[h, :, span], grad_scores, 1, 1))
+        gproj[h, FEAT : 2 * FEAT] = grad_keys.astype(BF16)
+        tap = taps(h)
+        grad_raw = tap[0] * grad_values
+        sums = [jnp.sum(grad_values * raw[h], 1, keepdims=True)]
+        for j in range(1, CONV):
+            masked = jnp.where(position >= j, grad_values, 0.0)
+            grad_raw += tap[j] * pltpu.roll(masked, seq - j, 1)
+            sums.append(jnp.sum(masked * pltpu.roll(raw[h], j, 1), 1, keepdims=True))
+        gproj[h, 2 * FEAT :] = grad_raw.astype(BF16)
+        columns = jnp.zeros((HDIM, TILE), F32)
+        for j in range(CONV):
+            columns = jnp.where(tail == rows % TILE + j, sums[j], columns)
+        for c in range(4):
+            gat[h, c, HEADROWS:, WIDE - TILE :] = columns.astype(BF16)
+
+    finish()
+    res_send, res_here = marks.many(3), marks.many(3)
+    tok_send, tok_here = marks.many(3), marks.many(3)
+    kept = []
+
+    def hand_out(source, target, send, receive):
+        copies = [
+            remote(
+                source.at[block_rows(others[p])], target.at[:, lanes(chip * TILE)],
+                send(p), receive(p), peers[p],
+            )
+            for p in range(3)
+        ]
+        for copy in copies:
+            copy.start()
+        kept.append(
+            pltpu.make_async_copy(
+                source.at[block_rows(chip)], target.at[:, lanes(chip * TILE)], marks.one()
+            )
+        )
+        kept[-1].start()
+        return copies
+
+    turned_rows = both.at[:, 0:TILE]
+    outs = hand_out(turned_rows, out_res, res_send, res_here)
+
+    def fill_grad_one(start):
+        @pl.loop(0, 4)
+        def _(c):
+            where = lanes(start, half)
+            total = dot(at[0, c, :HEADROWS, :rows], gproj[0, :, where], 0, 0)
+            total += dot(at[1, c, :HEADROWS, :rows], gproj[1, :, where], 0, 0)
+            part[block_rows(c), where] = total.astype(BF16)
+
+    acc3[:, 0:TILE] = gmid[...]
+    for copy in outs:
+        copy.wait()
+    for copy in kept:
+        copy.wait()
+    finish = plane_sum(fill_grad_one, store_gmid, guard=True)
+
+    @pl.loop(0, 2)
+    def _(h):
+        for c in range(4):
+            block = slice(c * rows, (c + 1) * rows)
+            gat[h, c, :HEADROWS, :rows] = dot(gproj[h], xs[block], 1, 1).astype(BF16)
+            grad = dot(att[h], low2[block], 1, 1).astype(BF16)
+            whole = rows // TILE * TILE
+            gat[h, c, HEADROWS:, :whole] = grad[:, :whole]
+            gat[h, c, HEADROWS:, whole:rows] = grad[:, whole:]
+
+    att_back = [
+        Collect(gat.at[a], att_got.at[a], 2 * core + a, chip, plane, core, marks)
+        for a in range(2)
+    ]
+    for item in att_back:
+        item.start(None)
+    finish()
+
+    inverse_own = inv_all[:, lanes(first)]
+    norm_back(
+        lambda r: normed[r].astype(F32), inverse_own, 0, 0, lambda r: acc3[r, 0:TILE]
+    )
+    both[:, TILE : 2 * TILE] = gmid[...].astype(BF16)
+    outs = hand_out(both.at[:, TILE : 2 * TILE], out_tok, tok_send, tok_here)
+
+    for c in range(1, 4):
+        small[c, 2:3] = small[0, 2:3]
+    a_send, a_here = marks.many(3), marks.many(3)
+    trio = [
+        remote(small.at[others[p]], small_a.at[p], a_send(p), a_here(p), peers[p])
+        for p in range(3)
+    ]
+    for copy in trio:
+        copy.start()
+    for copy in trio:
+        copy.wait()
+    small_b[0] = small[chip] + small_a[0] + small_a[1] + small_a[2]
+    b_send, b_here = marks.many(7), marks.many(7)
+    seven = [
+        remote(small_b.at[0], small_b.at[1 + i], b_send(i), b_here(i), to)
+        for i, to in enumerate(line + [mate] + line_mates)
+    ]
+    for copy in seven:
+        copy.start()
+
+    add_own = add_tiles(plane)
+    for o in range(4):
+        main_back[o].total(add_own)
+    back_send, back_here = marks.many(3), marks.many(3)
+    mine = lanes(plane * TILE)
+    backs = [
+        remote(
+            gout.at[:, block_rows(others[p]), mine], out_ff.at[:, :, lanes(chip * TILE)],
+            back_send(p), back_here(p), peers[p],
+        )
+        for p in range(3)
+    ]
+    for copy in backs:
+        copy.start()
+    kept.append(
+        pltpu.make_async_copy(
+            gout.at[:, block_rows(chip), mine], out_ff.at[:, :, lanes(chip * TILE)], marks.one()
+        )
+    )
+    kept[-1].start()
+
+    extra_back.total(add_tiles(4))
+    last_send, last_here, last_local = marks.many(4), marks.one(), marks.one()
+
+    def last_copy(c):
+        return remote(
+            gout.at[:, block_rows(c), last], out_ff.at[:, :, last], last_send(c), last_here,
+            device(c, plane, chip % 2),
+        )
+
+    def last_keep():
+        return pltpu.make_async_copy(
+            gout.at[:, block_rows(chip), last], out_ff.at[:, :, last], last_local
+        )
+
+    for c in range(4):
+        same = (c == chip) & (core == chip % 2)
+
+        @pl.when(holds_extra & same)
+        def _():
+            last_keep().start()
+
+        @pl.when(holds_extra & no(same))
+        def _():
+            last_copy(c).start()
+
+    def add_head(a):
+        def add(source):
+            loads = [
+                pltpu.make_async_copy(
+                    source.at[c], part.at[c * BLOCKROWS : (c + 1) * BLOCKROWS, 0:WIDE],
+                    load_marks(0),
+                )
+                for c in range(4)
+            ]
+            for load in loads:
+                load.start()
+                load.wait()
+            for c in range(4):
+                gat[a, c] = (
+                    gat[a, c].astype(F32)
+                    + part[c * BLOCKROWS : (c + 1) * BLOCKROWS, 0:WIDE].astype(F32)
+                ).astype(BF16)
+
+        return add
+
+    for a in range(2):
+        att_back[a].relay(add_head(a))
+    for a in range(2):
+        att_back[a].total(add_head(a))
+    head_send, head_here, head_local = marks.many(4), marks.many(2), marks.one()
+
+    def head_copy(c):
+        return remote(
+            gat.at[plane % 2, c], out_at.at[chip % 2], head_send(c), head_here(chip % 2),
+            device(c, plane, chip // 2),
+        )
+
+    def head_keep():
+        return pltpu.make_async_copy(gat.at[plane % 2, chip], out_at.at[chip % 2], head_local)
+
+    for c in range(4):
+        same = (c == chip) & (core == chip // 2)
+
+        @pl.when(holds_att & same)
+        def _():
+            head_keep().start()
+
+        @pl.when(holds_att & no(same))
+        def _():
+            head_copy(c).start()
+
+    for copy in seven:
+        copy.wait()
+    total = small_b[0]
+    for i in range(7):
+        total += small_b[1 + i]
+    small_a[0] = total
+    small_out = pltpu.make_async_copy(small_a.at[0], out_small, marks.one())
+    small_out.start()
+    kept.append(small_out)
+    for item in att_line + main_line + [extra_line] + main_back + [extra_back] + att_back:
+        item.finish()
+    for copy in outs + backs:
+        copy.wait()
+    for copy in kept[1:]:
+        copy.wait()
+    for c in range(4):
+        for holds, same, local, away_copy in (
+            (holds_extra, (c == chip) & (core == chip % 2), last_keep, last_copy),
+            (holds_att, (c == chip) & (core == chip // 2), head_keep, head_copy),
+        ):
+
+            @pl.when(holds & same)
+            def _():
+                local().wait()
+
+            @pl.when(holds & no(same))
+            def _():
+                away_copy(c).wait_send()
+
+    @pl.when(no(extra_self))
+    def _():
+        last_copy(0).wait_recv()
+
+    for h in range(2):
+
+        @pl.when(no(att_self[h]))
+        def _():
+            remote(
+                gat.at[0, 0], out_at.at[h], head_send(0), head_here(h), mate
+            ).wait_recv()
+
+    pl.semaphore_wait(free_mate, 1)
+    pl.semaphore_wait(free_chips, 3)
+    assert marks.used <= MARKS, marks.used
+
+
+def dma(*shape):
+    return pltpu.SemaphoreType.DMA(shape)
+
+
+def run_layer(wff, wat, tok, cot, gains):
+    rows, half = tok.shape
+    width, seq = 4 * rows, 2 * half
+    shape = jax.ShapeDtypeStruct
+    vmem = pltpu.VMEM
+    tiles = (3, width, TILE)
+    head = (4, BLOCKROWS, WIDE)
+    return pl.pallas_call(
+        layer_kernel,
+        out_shape=[
+            shape((3, rows, 5 * TILE), BF16),
+            shape((2, BLOCKROWS, WIDE), BF16),
+            shape((rows, half), BF16),
+            shape((rows, half), BF16),
+            shape((8, WIDE), F32),
+            shape((4,) + tiles, BF16),
+            shape((4,) + tiles, BF16),
+            shape((2, 4) + head, BF16),
+        ],
+        in_specs=[ANY] * 5,
+        out_specs=[ANY] * 8,
+        scratch_shapes=[
+            vmem((3, width, 5 * TILE), BF16),
+            vmem((2,) + head, BF16),
+            vmem((width, seq), BF16),
+            vmem((width, seq), BF16),
+            vmem((width, seq), BF16),
+            vmem((width, seq), BF16),
+            vmem((width, seq), F32),
+            vmem((3, width, 5 * TILE), BF16),
+            vmem((2,) + head, BF16),
+            vmem((width, half), BF16),
+            vmem((width, half), BF16),
+            vmem((3, width, TILE), BF16),
+            vmem((3 * TILE, width), BF16),
+            vmem((5 * TILE, seq), BF16),
+            vmem((2 * TILE, seq), BF16),
+            vmem((width, TILE), BF16),
+            vmem((2, HDIM, seq), F32),
+            vmem((2, FEAT, seq), BF16),
+            vmem((2, FEAT, seq), BF16),
+            vmem((2, HDIM, seq), BF16),
+            vmem((2, HDIM, seq), BF16),
+            vmem((2, HDIM, seq), BF16),
+            vmem((2, HEADROWS, seq), BF16),
+            vmem((width, TILE), F32),
+            vmem((width, TILE), F32),
+            vmem((width, TILE), BF16),
+            vmem((1, seq), F32),
+            vmem((2, 1, seq), F32),
+            vmem((4, 8, WIDE), F32),
+            vmem((3, 8, WIDE), F32),
+            vmem((8, 8, WIDE), F32),
+            dma(MARKS),
+            pltpu.SemaphoreType.REGULAR,
+            pltpu.SemaphoreType.REGULAR,
+        ],
+        compiler_params=pltpu.CompilerParams(
+            collective_id=0, has_side_effects=True, vmem_limit_bytes=63 * 2**20
+        ),
+        name="layer",
+    )(wff, wat, tok, cot, gains)
+
+
+def on_device_full(
+    tokens, cotangent, w_qkv, conv_weight, w_out, w_gate, w_up, w_down, gain_mix, gain_ffn
+):
+    rows, half = tokens.shape
+    ffn_cols = w_gate.shape[1]
+    heads = 2
+    pad = ((0, 0), (0, 5 * TILE - ffn_cols))
+    wff = jnp.stack([jnp.pad(w, pad) for w in (w_gate, w_up, w_down)])
+    upper = jnp.pad(
+        w_qkv.T.reshape(heads, HEADROWS, rows), ((0, 0), (0, 0), (0, WIDE - rows))
+    )
+    lower = jnp.concatenate(
+        [
+            w_out.reshape(heads, HDIM, rows),
+            conv_weight.T.reshape(heads, HDIM, CONV),
+            jnp.zeros((heads, HDIM, WIDE - rows - CONV), BF16),
+        ],
+        2,
+    )
+    wat = jnp.concatenate([upper, lower], 1)
+    gains = jnp.concatenate(
+        [jnp.broadcast_to(g[:, None], (rows, TILE // 2)) for g in (gain_mix, gain_ffn)], 1
+    )
+    out_ff, out_at, out_res, out_tok, small = run_layer(wff, wat, tokens, cotangent, gains)[:5]
+    out_at = out_at.astype(F32)
+    return (
+        out_res,
+        out_tok.astype(F32),
+        out_at[:, :HEADROWS, :rows].reshape(heads * HEADROWS, rows).T,
+        out_at[:, HEADROWS:, rows : rows + CONV].reshape(heads * HDIM, CONV).T,
+        out_at[:, HEADROWS:, :rows].reshape(heads * HDIM, rows),
+        out_ff[0, :, :ffn_cols].astype(F32),
+        out_ff[1, :, :ffn_cols].astype(F32),
+        out_ff[2, :, :ffn_cols].astype(F32),
+        small[0, :rows],
+        small[1, :rows],
+        jnp.sqrt(small[2, :3] / (8 * half * 4 * rows)),
+    )
+
+
+def on_device(tokens, cotangent, lengths, deal_order, *weights):
+    total_rows = tokens.shape[1] * lax.axis_size("col")
+    if (
+        lengths.shape[0] * LONGEST == total_rows
+        and lax.axis_size("row") == 4
+        and lax.axis_size("col") == 8
+        and total_rows == 4 * LONGEST
+        and weights[0].shape[1] == 2 * HEADROWS
+        and 4 * TILE < weights[3].shape[1] <= 5 * TILE
+    ):
+        return on_device_full(tokens, cotangent, *weights)
+    return on_device_general(tokens, cotangent, lengths, deal_order, *weights)
+
+
 def solution(mesh):
     in_specs = (
         P("row", "col"),

time: 1180 us -> 525 us (0.44)
  waiting for transfers between devices: 728 us -> 0 us
  Pallas kernels: 0 us -> 505 us
  local copies, waits for them, and re-layouts: 218 us -> 10.3 us
  matrix products: 121 us -> 0 us
  blocking collectives: 50.9 us -> 0 us
  other arithmetic: 33 us -> 8.27 us
  between operations: 15 us -> 0.75 us
    pallas_call x0 -> x1, Pallas kernels: none -> 505 us  [run_layer(): pl.pallas_call(layer_kernel, out_shape=[shape((3, rows, 5 * TILE), BF16),...]
    reduce_scatter x8 -> x0, waiting for transfers between devices: 394 us -> none  [the longest x2 237 us: forward_rows(): lax.psum_scatter(partial_term(jnp.int32(0), rows_here * lax.axis_size('ro...]
    all_gather x8 -> x0, waiting for transfers between devices: 334 us -> none  [the longest x2 110 us: grad_gather_rows(): return lax.all_gather(values, 'row', axis=0, tiled=True)]
    gather x8 -> x0, local copies, waits for them, and re-layouts: 165 us -> none  [the longest x6 125 us: partial_term(): picked = jnp.take(gathered, row_index, axis=0)]
    dot_general x17 -> x0, matrix products: 121 us -> none  [the longest x3 20.9 us: times_transposed(): lax.dot_general(left, right, (((1,), (1,)), ((), ())), preferred_element_...]
    psum x5 -> x0, blocking collectives: 50.9 us -> none  [the longest x4 36.5 us: width_total(): return lax.psum(values, 'row')]
    all_gather x5 -> x0, local copies, waits for them, and re-layouts: 41.3 us -> none  [the longest x1 14.3 us: grad_gather_rows(): return lax.all_gather(values, 'row', axis=0, tiled=True)]
  transfers between devices with their start and end apart: 16 -> 0, of which waited for: 15 -> 0; matrix products, arithmetic and copies ran while one was open for 17% -> 0% of each run, Pallas kernels for 0% -> 0%
where the time goes in v2:
time: 525 us; the launch traced here: 524 us
  Pallas kernels  505 us (96%)
  local copies, waits for them, and re-layouts  10.3 us (2%)
  other arithmetic  8.27 us (2%)
    pallas_call x1, Pallas kernels, run_layer(): pl.pallas_call(layer_kernel, out_shape=[shape((3, rows, 5 * TILE), BF16),...  505 us

profile of v2, /device:TPU:4, one launch (start us, length us, event | category | flops | bytes accessed | tf_op | source)
XLA Modules:
  0.0 523.9 jit_solution(11041582509532747077)
XLA Ops:
  0.6 0.0 copy-start.3
  0.7 0.9 copy.21
  1.5 0.0 copy-start.1
  1.6 0.0 copy-start.2
  1.6 0.9 broadcast_in_dim.7
  2.5 0.8 broadcast_in_dim.8
  3.3 0.8 pad_maximum_fusion.1.gains
  4.0 0.1 pad.23.clone
  4.1 2.0 fusion.1.wat
  6.1 0.0 copy-done.3
  6.1 0.1 pad_bitcast_fusion.2
  6.1 0.0 copy-done.1
  6.2 0.0 copy-done.2
  6.2 0.1 pad_bitcast_fusion
  6.3 1.4 pad_maximum_fusion.wff
  7.7 504.5 %layer.1 = (bf16[3,448,640]{2,1,0:T(8,128)(2,1)}, bf16[2,256,512]{2,1,0:T(8,128)(2,1)}, bf16[448,512]{1,0:T(8,128)(2,1)}, bf16[448,512]{1,0:T(8,128)(2,1)}, f32[...) custom-call(bf16[3,448,640]{2,1,0:T(8,128)(2,1)} %pad_maximum_fusion, ...), custom_call_target="tpu_custom_call" | custom-call | tf_op jit(solution)/shard_map/layer/pallas_call | solution.py:1321
  512.3 0.0 copy-start.5
  512.3 1.3 sqrt_bitcast_fusion
  513.5 1.4 fusion.2
  514.9 0.9 slice.37
  515.8 0.7 copy.22
  516.5 0.0 copy-start
  516.5 1.9 slice.38
  518.4 1.8 slice.36
  520.2 0.0 copy-done.5
  520.2 1.0 convert_element_type.30
  521.3 0.0 copy-done
  521.3 0.0 copy-start.4
  521.3 1.8 bitcast_convert_fusion
  523.1 0.0 copy-done.4
  523.1 0.8 copy.24
  (1 shorter events, 0.0 us)
Async XLA Ops:
  0.6 5.4 %copy-start.3 = (bf16[448,608]{1,0:T(8,128)(2,1)S(1)}, bf16[448,608]{1,0:T(8,128)(2,1)}, u32[]{:S(2)}) copy-start(bf16[448,608]{1,0:T(8,128)(2,1)} %param.17) | copy-start | bytes 1634308
  1.5 4.6 copy-start.1
  1.6 4.6 copy-start.2
  512.3 8.0 %copy-start.5 = (bf16[448,512]{1,0:T(8,128)(2,1)S(1)}, bf16[448,512]{1,0:T(8,128)(2,1)}, u32[]{:S(2)}) copy-start(bf16[448,512]{1,0:T(8,128)(2,1)} %get-tuple-element.17) | copy-start | bytes 1376260
  516.5 4.8 copy-start
  521.3 1.8 copy-start.4

commit v3 on v2

--- a/solution.py
+++ b/solution.py
@@ -437,11 +437,12 @@
 
 
 class Spread:
-    def __init__(self, ref, owner, chip, plane, core, marks):
+    def __init__(self, ref, owner, chip, plane, core, marks, forward):
         self.ref, self.owner, self.spot = ref, owner, (chip, plane, core)
         self.sends = marks.many(4)
         self.arrived = marks.one()
         self.mine = plane == owner
+        self.forward = forward
         self.relays = is_inner(plane) & (plane == away(owner, 2))
 
     def copy(self, step, send):
@@ -451,40 +452,148 @@
             device(chip, away(plane, step), core),
         )
 
-    def start(self, also=True):
-        @pl.when(also & self.mine)
-        def _():
+    def far(self):
+        return self.mine & is_inner(self.spot[1]) if self.forward else self.mine
+
+    def start(self):
+        @pl.when(self.far())
+        def _():
+            self.copy(3, 2).start()
+
+        @pl.when(self.mine)
+        def _():
+            self.copy(2, 1).start()
             self.copy(1, 0).start()
-            self.copy(2, 1).start()
-
-        @pl.when(also & self.mine & is_inner(self.spot[1]))
-        def _():
-            self.copy(3, 2).start()
-
-    def relay(self, also=True):
-        @pl.when(also & self.relays)
+
+    def relay(self):
+        @pl.when(self.relays)
         def _():
             self.copy(1, 3).wait_recv()
             self.copy(1, 3).start()
 
-    def arrive(self, also=True):
-        @pl.when(also & no(self.mine) & no(self.relays))
+    def arrive(self):
+        done = self.mine | self.relays if self.forward else self.mine
+
+        @pl.when(no(done))
         def _():
             self.copy(1, 3).wait_recv()
 
-    def finish(self, also=True):
-        @pl.when(also & self.mine)
+    def finish(self):
+        @pl.when(self.mine)
         def _():
             self.copy(1, 0).wait_send()
             self.copy(2, 1).wait_send()
 
-        @pl.when(also & self.mine & is_inner(self.spot[1]))
+        @pl.when(self.far())
         def _():
             self.copy(3, 2).wait_send()
 
-        @pl.when(also & self.relays)
-        def _():
-            self.copy(1, 3).wait_send()
+        if self.forward:
+
+            @pl.when(self.relays)
+            def _():
+                self.copy(1, 3).wait_send()
+
+
+class MainTiles:
+    def __init__(self, ff, chip, plane, core, marks):
+        self.ff, self.spot = ff, (chip, plane, core)
+        self.sends, self.here = marks.many(4), marks.many(3)
+        self.inner = is_inner(plane)
+
+    def copy(self, slot, to_step, send, receive):
+        chip, plane, core = self.spot
+        tiles = self.ff.at[:, :, lanes(slot * TILE)]
+        return remote(
+            tiles, tiles, self.sends(send), self.here(receive),
+            device(chip, away(plane, to_step), core),
+        )
+
+    def start_all(self):
+        near, next_on, far = [
+            self.copy(self.spot[1], step, step - 1, step - 1) for step in (1, 2, 3)
+        ]
+
+        @pl.when(self.inner)
+        def _():
+            near.start()
+            next_on.start()
+            far.start()
+
+        @pl.when(no(self.inner))
+        def _():
+            next_on.start()
+            near.start()
+
+    def relay(self):
+        @pl.when(self.inner)
+        def _():
+            self.copy(self.spot[1], 1, 0, 1).wait_recv()
+            self.copy(away(self.spot[1], 2), 1, 3, 2).start()
+
+    def arrive(self, step):
+        copy = self.copy(self.spot[1], 1, 0, step - 1)
+        if step == 2:
+            pl.when(no(self.inner))(copy.wait_recv)
+        else:
+            copy.wait_recv()
+
+    def finish(self):
+        for step in (1, 2):
+            self.copy(self.spot[1], 1, step - 1, 0).wait_send()
+
+        @pl.when(self.inner)
+        def _():
+            self.copy(self.spot[1], 1, 2, 0).wait_send()
+            self.copy(self.spot[1], 1, 3, 0).wait_send()
+
+
+class MainGrads:
+    def __init__(self, gout, slots, chip, plane, core, marks):
+        self.gout, self.slots, self.spot = gout, slots, (chip, plane, core)
+        self.sends, self.here = marks.many(3), marks.many(4)
+        self.inner = is_inner(plane)
+
+    def copy(self, slot, to_step, send, receive):
+        chip, plane, core = self.spot
+        return remote(
+            self.gout.at[:, :, lanes(slot * TILE)], self.slots.at[receive],
+            self.sends(send), self.here(receive), device(chip, away(plane, to_step), core),
+        )
+
+    def start(self, step):
+        plane = self.spot[1]
+        if step == 1:
+            self.copy(away(plane, 1), 1, 0, 0).start()
+        if step == 2:
+            pl.when(no(self.inner))(self.copy(away(plane, 2), 2, 1, 1).start)
+        if step == 3:
+            pl.when(self.inner)(self.copy(away(plane, 3), 3, 2, 2).start)
+            pl.when(no(self.inner))(self.copy(away(plane, 3), 1, 2, 3).start)
+
+    def relay(self, add):
+        plane = self.spot[1]
+
+        @pl.when(self.inner)
+        def _():
+            self.copy(plane, 1, 0, 3).wait_recv()
+            add(self.slots.at[3])
+            self.copy(away(plane, 2), 2, 1, 1).start()
+
+    def total(self, add):
+        plane = self.spot[1]
+        for receive in range(2):
+            self.copy(plane, 1, 0, receive).wait_recv()
+            add(self.slots.at[receive])
+
+        @pl.when(self.inner)
+        def _():
+            self.copy(plane, 1, 0, 2).wait_recv()
+            add(self.slots.at[2])
+
+    def finish(self):
+        for send in range(3):
+            self.copy(self.spot[1], 1, send, 0).wait_send()
 
 
 class Collect:
@@ -553,8 +662,8 @@
     wff, wat, tok, cot, gains,
     out_ff, out_at, out_res, out_tok, out_small, main_got, extra_got, att_got,
     ff, at, xs, gs, low2, part, acc3, gout, gat, from_mate, both, got, turned, hid, gg,
-    gn, raw, qs, ks, vs, att, gatt, gproj, mid, gmid, normed, inv_all, inv_sum, small, small_a,
-    small_b, sem, free_mate, free_chips,
+    gn, gcol, raw, qs, ks, vs, att, gatt, gproj, mid, gmid, gsum, normed, sending, inv_all,
+    inv_sum, small, small_a, small_b, sem, free_mate, free_chips,
 ):
     chip, plane, core = place()
     others = other_chips(chip)
@@ -608,54 +717,108 @@
         def _():
             att_copy(h).start()
 
-    def plane_spread(source, target_of, to_mate=True):
-        send, receive = marks.many(3), marks.many(3)
-        mate_send, mate_receive = marks.many(4), marks.many(4)
-        keep = pltpu.make_async_copy(source, target_of(chip), marks.one())
-        keep.start()
-        copies = [
-            remote(source, target_of(chip), send(p), receive(p), peers[p]) for p in range(3)
+    class Gather:
+        def __init__(self, source, target_of):
+            self.source, self.target_of = source, target_of
+            self.send, self.here = marks.many(4), marks.many(4)
+            self.mate_send, self.mate_here = marks.many(4), marks.many(4)
+            self.keep = pltpu.make_async_copy(source, target_of(chip), marks.one())
+            self.copies = [
+                remote(source, target_of(chip), self.send(p), self.here(p), peers[p])
+                for p in range(2)
+            ]
+            for copy in self.copies:
+                copy.start()
+            self.keep.start()
+            self.crossing = []
+            self.cross(source, chip, 3)
+
+        def cross(self, source, c, mark):
+            copy = remote(
+                source, self.target_of(c), self.mate_send(mark), self.mate_here(mark), mate
+            )
+            copy.start()
+            self.crossing.append(copy)
+
+        def halves(self, c):
+            block = self.target_of(c)
+            size = block.shape[0] // 2
+            return block.at[0:size], block.at[size : 2 * size]
+
+        def pass_on(self):
+            self.copies[0].wait_recv()
+            part_a = self.halves(others[0])[0]
+            self.copies.append(remote(part_a, part_a, self.send(2), self.here(2), peers[1]))
+            self.copies[2].start()
+            self.cross(self.target_of(others[0]), others[0], 0)
+            self.copies[1].wait_recv()
+            part_b = self.halves(others[1])[1]
+            self.copies.append(remote(part_b, part_b, self.send(3), self.here(3), peers[0]))
+            self.copies[3].start()
+            self.cross(self.target_of(others[1]), others[1], 1)
+
+        def arrive(self):
+            for copy in self.copies[2:]:
+                copy.wait_recv()
+            self.cross(self.target_of(others[2]), others[2], 2)
+            for copy in self.crossing:
+                copy.wait_recv()
+            self.keep.wait()
+
+        def finish(self):
+            for copy in self.copies + self.crossing:
+                copy.wait_send()
+
+    tokens_in = Gather(tok, lambda c: xs.at[block_rows(c), own_half])
+    gain_send, gain_here = marks.many(3), marks.many(3)
+    gain_copies = [
+        remote(gains, gn.at[chip], gain_send(p), gain_here(p), peers[p]) for p in range(3)
+    ]
+    gain_keep = pltpu.make_async_copy(gains, gn.at[chip], marks.one())
+    for copy in gain_copies + [gain_keep]:
+        copy.start()
+
+    for h in range(2):
+
+        @pl.when(att_self[h])
+        def _():
+            att_keep(h).wait()
+
+        @pl.when(no(att_self[h]))
+        def _():
+            att_copy(h).wait_send()
+
+    for c in range(4):
+
+        @pl.when(holds_att & no((c == chip) & (core == chip // 2)))
+        def _():
+            remote(
+                wat.at[0], at.at[plane % 2, c], att_send(0), att_here(c), mate
+            ).wait_recv()
+
+    out_rows, in_rows = pl.ds(HEADROWS, HDIM), pl.ds(0, HEADROWS)
+    in_line, out_line = [
+        [
+            Spread(at.at[a, :, span], 2 * core + a, chip, plane, core, marks, forward=True)
+            for a in range(2)
         ]
-        for copy in copies:
-            copy.start()
-        crossing = []
-        if to_mate:
-            crossing.append(
-                remote(source, target_of(chip), mate_send(3), mate_receive(3), mate)
-            )
-            crossing[0].start()
-
-        def pass_on():
-            for p in range(3):
-                copies[p].wait_recv()
-                if to_mate:
-                    block = target_of(others[p])
-                    crossing.append(remote(block, block, mate_send(p), mate_receive(p), mate))
-                    crossing[-1].start()
-
-        def finish():
-            keep.wait()
-            for copy in copies:
-                copy.wait_send()
-            for copy in crossing:
-                copy.wait()
-
-        return pass_on, finish
-
-    tok_pass, tok_finish = plane_spread(tok, lambda c: xs.at[block_rows(c), own_half])
-    gn_pass, gn_finish = plane_spread(gains, lambda c: gn.at[block_rows(c)], to_mate=False)
-
+        for span in (in_rows, out_rows)
+    ]
+    for item in in_line + out_line:
+        item.start()
+
+    tokens_in.pass_on()
     main_send, main_here, main_local = marks.many(3), marks.many(3), marks.one()
-    mains = []
     main_here_at = ff.at[:, block_rows(chip), lanes(plane * TILE)]
-    for p in range(3):
-        mains.append(
-            remote(
-                wff.at[:, :, lanes(others[p] * TILE)], main_here_at,
-                main_send(p), main_here(p), peers[p],
-            )
+    mains = [
+        remote(
+            wff.at[:, :, lanes(others[p] * TILE)], main_here_at,
+            main_send(p), main_here(p), peers[p],
         )
-        mains[-1].start()
+        for p in range(3)
+    ]
+    for copy in mains:
+        copy.start()
     main_keep = pltpu.make_async_copy(wff.at[:, :, lanes(chip * TILE)], main_here_at, main_local)
     main_keep.start()
 
@@ -682,44 +845,43 @@
     def _():
         extra_copy().start()
 
-    for h in range(2):
-
-        @pl.when(att_self[h])
-        def _():
-            att_keep(h).wait()
-
-        @pl.when(no(att_self[h]))
-        def _():
-            att_copy(h).wait_send()
-
-    for c in range(4):
-
-        @pl.when(holds_att & no((c == chip) & (core == chip // 2)))
-        def _():
-            remote(
-                wat.at[0], at.at[plane % 2, c], att_send(0), att_here(c), mate
-            ).wait_recv()
-
-    att_line = [
-        Spread(at.at[a], 2 * core + a, chip, plane, core, marks) for a in range(2)
-    ]
-    for item in att_line:
-        item.start()
-
-    tok_pass()
-    gn_pass()
-    gn_finish()
-    tok_finish()
-    cot_pass, cot_finish = plane_spread(cot, lambda c: gs.at[block_rows(c), own_half])
-
+    tokens_in.arrive()
+    cot_in = Gather(cot, lambda c: gs.at[block_rows(c), own_half])
+    for copy in gain_copies + [gain_keep]:
+        copy.wait()
+
+    for item in in_line:
+        item.relay()
+    @pl.loop(0, 4)
+    def _(c):
+        columns = gn[c].astype(F32).T
+        gcol[block_rows(c), 0:16] = columns[:rows]
+
+    step_rows = 64
+
+    def add_squares(i, total):
+        x = xs[rows_at(i * step_rows, step_rows, step_rows)].astype(F32)
+        return total + jnp.sum((x * x).reshape(step_rows // 8, 8, seq), 0)
+
+    squares = lax.fori_loop(0, width // step_rows, add_squares, jnp.zeros((8, seq), F32))
+    inv_all[...] = lax.rsqrt(jnp.sum(squares, 0, keepdims=True) / D + EPSILON)
+    tokens_in.finish()
+    normed[...] = xs[:, lanes(first)]
+
+    @pl.loop(0, width // step_rows)
+    def _(i):
+        at_rows = rows_at(i * step_rows, step_rows, step_rows)
+        xs[at_rows] = (
+            xs[at_rows].astype(F32) * inv_all[...] * gcol[at_rows, 0:1]
+        ).astype(BF16)
+
+    for item in out_line:
+        item.relay()
     main_keep.wait()
     for copy in mains:
         copy.wait()
-    main_line = [
-        Spread(ff.at[:, :, lanes(o * TILE)], o, chip, plane, core, marks) for o in range(4)
-    ]
-    for item in main_line:
-        item.start()
+    main_line = MainTiles(ff, chip, plane, core, marks)
+    main_line.start_all()
 
     @pl.when(extra_self)
     def _():
@@ -737,35 +899,19 @@
                 wff.at[:, :, last], ff.at[:, block_rows(c), last], extra_send, extra_here(c), mate
             ).wait_recv()
 
-    extra_line = Spread(ff.at[:, :, last], extra_plane, chip, plane, core, marks)
+    extra_line = Spread(ff.at[:, :, last], extra_plane, chip, plane, core, marks, forward=True)
     extra_line.start()
 
-    step_rows = 64
-
-    def add_squares(i, total):
-        x = xs[rows_at(i * step_rows, step_rows, step_rows)].astype(F32)
-        return total + jnp.sum((x * x).reshape(step_rows // 8, 8, seq), 0)
-
-    squares = lax.fori_loop(0, width // step_rows, add_squares, jnp.zeros((8, seq), F32))
-    inv_all[...] = lax.rsqrt(jnp.sum(squares, 0, keepdims=True) / D + EPSILON)
-    mid[...] = xs[:, lanes(first)].astype(F32)
-
-    @pl.loop(0, width // step_rows)
-    def _(i):
-        at_rows = rows_at(i * step_rows, step_rows, step_rows)
-        gain = gn[at_rows, 0:1].astype(F32)
-        xs[at_rows] = (xs[at_rows].astype(F32) * inv_all[...] * gain).astype(BF16)
-
-    for item in att_line:
-        item.relay()
-    for item in att_line:
+    cot_in.pass_on()
+
+    for item in in_line:
         item.arrive()
 
     position = lax.broadcasted_iota(jnp.int32, (1, seq), 1)
     tail = lax.broadcasted_iota(jnp.int32, (HDIM, TILE), 1)
 
     def taps(h):
-        columns = at[h, 0, HEADROWS:BLOCKROWS, WIDE - TILE : WIDE].astype(F32)
+        columns = at[h, 0, 2 * FEAT : HEADROWS, WIDE - TILE : WIDE].astype(F32)
         return [columns[:, rows % TILE + j : rows % TILE + j + 1] for j in range(CONV)]
 
     @pl.loop(0, 2)
@@ -803,54 +949,102 @@
             weights = (kernel * inverse).astype(BF16)
             att[h, :, b * SPAN : seen] = dot(vs[h, :, :seen], weights, 1, 0).astype(BF16)
 
-    def plane_sum(fill, store, guard):
-        fill((1 - core) * half)
-        to_mate = remote(
-            part.at[:, lanes((1 - core) * half, half)], from_mate,
-            marks.one(), marks.one(), mate,
-        )
-        if guard:
-            pl.semaphore_wait(free_mate, 1)
-        to_mate.start()
-        fill(core * half)
-        to_mate.wait_recv()
-
-        @pl.loop(0, 4)
-        def _(c):
-            both[block_rows(c)] = (
-                part[block_rows(c), own_half].astype(F32) + from_mate[block_rows(c)].astype(F32)
-            ).astype(BF16)
-
-        pl.semaphore_signal(free_mate, inc=1, device_id=mate, device_id_type=MESH)
-        if guard:
-            pl.semaphore_wait(free_chips, 3)
-        send, receive = marks.many(3), marks.many(3)
-        copies = [
-            remote(
-                both.at[:, lanes(others[p] * TILE)], got.at[p], send(p), receive(p), peers[p]
+    for item in out_line:
+        item.arrive()
+
+    def default_got(i):
+        return got.at[i]
+
+    class Sum:
+        def __init__(self, guard, both=both, got=None, share=True):
+            self.guard, self.both, self.share = guard, both, share
+            self.got = got or default_got
+
+        def begin(self, fill):
+            fill((1 - core) * half)
+            self.to_mate = remote(
+                part.at[:, lanes((1 - core) * half, half)], from_mate,
+                marks.one(), marks.one(), mate,
             )
-            for p in range(3)
-        ]
-        for copy in copies:
-            copy.start()
-
-        def finish():
-            for copy in copies:
+            if self.guard:
+                pl.semaphore_wait(free_mate, 1)
+            self.to_mate.start()
+            fill(core * half)
+
+        def combine(self):
+            self.to_mate.wait_recv()
+
+            @pl.loop(0, 4)
+            def _(c):
+                self.both[block_rows(c)] = (
+                    part[block_rows(c), own_half].astype(F32)
+                    + from_mate[block_rows(c)].astype(F32)
+                ).astype(BF16)
+
+            pl.semaphore_signal(free_mate, inc=1, device_id=mate, device_id_type=MESH)
+            self.to_mate.wait_send()
+
+        def piece(self, upper, c):
+            size = width // 2
+            return self.both.at[pl.ds(0 if upper else size, size), lanes(c * TILE)]
+
+        def send(self):
+            if self.guard and self.share:
+                pl.semaphore_wait(free_chips, 2)
+            size = width // 2
+            top, bottom = pl.ds(0, size), pl.ds(size, size)
+            send, here = marks.many(6), marks.many(6)
+            self.across = [
+                remote(self.piece(True, others[2]), self.got(2).at[top], send(0), here(0), peers[0]),
+                remote(
+                    self.piece(False, others[2]), self.got(2).at[bottom], send(1), here(1), peers[1]
+                ),
+            ]
+            self.plain = [
+                remote(self.piece(True, others[0]), self.got(0).at[top], send(2), here(2), peers[0]),
+                remote(
+                    self.piece(False, others[1]), self.got(1).at[bottom], send(3), here(3), peers[1]
+                ),
+            ]
+            self.added = [
+                remote(
+                    self.piece(True, others[1]), self.got(1).at[top], send(4), here(4), peers[1]
+                ),
+                remote(
+                    self.piece(False, others[0]), self.got(0).at[bottom], send(5), here(5), peers[0]
+                ),
+            ]
+            for copy in self.across + self.plain:
+                copy.start()
+
+        def pass_on(self):
+            size = width // 2
+            quarter = size // 2
+            for i, c in ((0, others[1]), (1, others[0])):
+                self.across[i].wait_recv()
+                for q in range(2):
+                    at_rows = pl.ds(i * size + q * quarter, quarter)
+                    self.both[at_rows, lanes(c * TILE)] = (
+                        self.both[at_rows, lanes(c * TILE)].astype(F32) + self.got(2)[at_rows].astype(F32)
+                    ).astype(BF16)
+                self.added[i].start()
+
+        def finish(self, store):
+            for copy in self.plain + self.added:
                 copy.wait()
+            for copy in self.across:
+                copy.wait_send()
 
             @pl.loop(0, 4)
             def _(c):
                 at_rows = block_rows(c)
-                total = both[at_rows, lanes(chip * TILE)].astype(F32)
-                for p in range(3):
-                    total += got[p, at_rows].astype(F32)
+                total = self.both[at_rows, lanes(chip * TILE)].astype(F32)
+                for p in range(2):
+                    total += self.got(p)[at_rows].astype(F32)
                 store(at_rows, total)
 
-            for p in range(3):
+            for p in range(2 if self.share else 0):
                 pl.semaphore_signal(free_chips, inc=1, device_id=peers[p], device_id_type=MESH)
-            to_mate.wait_send()
-
-        return finish
 
     def fill_branch(start):
         @pl.loop(0, 4)
@@ -869,33 +1063,38 @@
 
     def store_branch(at_rows, total):
         note_square(0, total)
-        gmid[at_rows] = total
-
-    finish = plane_sum(fill_branch, store_branch, guard=False)
-    cot_pass()
-    finish()
-    normed[...] = mid[...].astype(BF16)
-    mid[...] += gmid[...]
+        mid[at_rows] = normed[at_rows].astype(F32) + total
+
+    branch_sum = Sum(guard=False)
+    branch_sum.begin(fill_branch)
+    cot_in.arrive()
+    branch_sum.combine()
+    branch_sum.send()
+    branch_sum.pass_on()
+    branch_sum.finish(store_branch)
+    main_line.relay()
     middle = mid[...]
     inverse_two = lax.rsqrt(jnp.sum(middle * middle, 0, keepdims=True) / D + EPSILON)
-    gain_at = TILE // 2
 
     @pl.loop(0, 4)
     def _(c):
         at_rows = block_rows(c)
-        gain = gn[at_rows, gain_at : gain_at + 1].astype(F32)
-        both[at_rows, 0:TILE] = (mid[at_rows] * inverse_two * gain).astype(BF16)
-
-    low_pass, low_finish = plane_spread(
-        both.at[:, 0:TILE], lambda c: low2.at[:, lanes(core * half + c * TILE)]
-    )
-    cot_finish()
-    low_pass()
-    low_finish()
+        sending[0, at_rows] = (mid[at_rows] * inverse_two * gcol[at_rows, 1:2]).astype(BF16)
+
+    def token_block(c):
+        return low2.at[:, lanes(core * half + c * TILE)]
+
+    low_in = Gather(sending.at[0], token_block)
+    cot_in.finish()
 
     @pl.loop(0, 4)
     def _(c):
         acc3[block_rows(c)] = jnp.zeros((rows, seq), F32)
+
+    low_in.pass_on()
+    low_in.arrive()
+    low_in.finish()
+    extra_line.relay()
 
     def feed(slot):
         where = lanes(slot * TILE)
@@ -927,12 +1126,7 @@
             gout[1, at_rows, where] = grads[:, TILE:]
             gout[2, at_rows, where] = dot(gs[at_rows], hid[unit_rows], 1, 1).astype(BF16)
 
-    main_back = [
-        Collect(
-            gout.at[:, :, lanes(o * TILE)], main_got, o, chip, plane, core, marks
-        )
-        for o in range(4)
-    ]
+    main_back = MainGrads(gout, main_got, chip, plane, core, marks)
     extra_back = Collect(gout.at[:, :, last], extra_got, extra_plane, chip, plane, core, marks)
     load_marks = marks.many(3)
 
@@ -959,23 +1153,40 @@
 
         return add
 
-    for item in main_line:
-        item.relay()
-    for item in main_line:
-        item.arrive()
-    extra_line.relay()
-    extra_line.arrive()
-
-    for step in (1, 0, 2, 3):
-        slot = away(plane, step) if step else plane
+    slots = [away(plane, 1), plane, away(plane, 2), away(plane, 3), 4]
+    inner = is_inner(plane)
+
+    @pl.loop(0, 5)
+    def _(turn):
+        for i, step in ((0, 1), (2, 2), (3, 3)):
+
+            @pl.when(turn == i)
+            def _():
+                main_line.arrive(step)
+
+        @pl.when(turn == 4)
+        def _():
+            extra_line.arrive()
+
+        slot = sum((turn == i).astype(jnp.int32) * slots[i] for i in range(5))
         feed(slot)
-    feed(4)
-    for o in range(4):
-        main_back[o].start(None)
+
+        @pl.when((turn == 0) & no(inner))
+        def _():
+            main_back.start(1)
+
+        @pl.when((turn == 3) & no(inner))
+        def _():
+            main_back.start(3)
+            main_back.start(2)
+
+    @pl.when(inner)
+    def _():
+        main_back.start(1)
+        main_back.start(3)
+
     extra_back.start(None)
-    for o in range(4):
-        main_back[o].relay(add_tiles(o))
-    extra_back.relay(add_tiles(4))
+    main_line.finish()
 
     def fill_grad_two(start):
         @pl.loop(0, 4)
@@ -983,37 +1194,14 @@
             where = lanes(start, half)
             part[block_rows(c), where] = acc3[block_rows(c), where].astype(BF16)
 
-    def store_gmid(at_rows, total):
-        gmid[at_rows] = total
-
-    finish = plane_sum(fill_grad_two, store_gmid, guard=True)
-    finish()
-
-    def norm_back(source, inverse, gain_lane, small_row, base):
-        def add_dots(c, total):
-            at_rows = block_rows(c)
-            gain = gn[at_rows, gain_lane : gain_lane + 1].astype(F32)
-            return total + jnp.sum(gmid[at_rows] * gain * source(at_rows), 0, keepdims=True)
-
-        dots = lax.fori_loop(0, 4, add_dots, jnp.zeros((1, TILE), F32))
-        scaled = inverse * inverse * inverse * dots / D
-
-        @pl.loop(0, 4)
-        def _(c):
-            at_rows = block_rows(c)
-            gain = gn[at_rows, gain_lane : gain_lane + 1].astype(F32)
-            grad, value = gmid[at_rows], source(at_rows)
-            for_gain = jnp.sum((grad * value * inverse).T, 0, keepdims=True)
-            small[c, small_row : small_row + 1, 0:rows] = for_gain
-            gmid[at_rows] = base(at_rows) + (grad * gain * inverse - value * scaled)
-
-    norm_back(
-        lambda r: mid[r], inverse_two, gain_at, 1, lambda r: gs[r, lanes(first)].astype(F32)
-    )
-    both[:, 0:TILE] = gmid[...].astype(BF16)
-    mid_pass, mid_finish = plane_spread(
-        both.at[:, 0:TILE], lambda c: low2.at[:, lanes(core * half + c * TILE)]
-    )
+    def store_gsum(at_rows, total):
+        gsum[at_rows] = total
+
+    two_sum = Sum(guard=True)
+    two_sum.begin(fill_grad_two)
+    two_sum.combine()
+    two_sum.send()
+    two_sum.pass_on()
 
     def fill_ffn(start):
         @pl.loop(0, 4)
@@ -1023,17 +1211,51 @@
                 ff[2, block_rows(c)], hid[:, where], 1, 0
             ).astype(BF16)
 
-    mid_pass()
-    mid_finish()
-
-    def store_result(at_rows, total):
-        note_square(1, total)
-        total = mid[at_rows] + total
-        note_square(2, total)
-        normed_out = total.astype(BF16)
-        both[at_rows, 0:TILE] = normed_out
-
-    finish = plane_sum(fill_ffn, store_result, guard=True)
+    ffn_sum = Sum(
+        guard=True, both=ff.at[1, :, lanes(0, half)],
+        got=lambda i: ff.at[0, :, lanes(i * TILE)], share=False,
+    )
+    ffn_sum.begin(fill_ffn)
+    two_sum.finish(store_gsum)
+
+    def norm_back(source, inverse, gain_lane, base, store):
+        def add_dots(c, total):
+            at_rows = block_rows(c)
+            gain = gcol[at_rows, gain_lane : gain_lane + 1]
+            return total + jnp.sum(gsum[at_rows] * gain * source(at_rows), 0, keepdims=True)
+
+        dots = lax.fori_loop(0, 4, add_dots, jnp.zeros((1, TILE), F32))
+        scaled = inverse * inverse * inverse * dots / D
+
+        @pl.loop(0, 4)
+        def _(c):
+            at_rows = block_rows(c)
+            gain = gcol[at_rows, gain_lane : gain_lane + 1]
+            grad, value = gsum[at_rows], source(at_rows)
+            store(at_rows, base(at_rows) + (grad * gain * inverse - value * scaled))
+
+        def gain_back():
+            @pl.loop(0, 4)
+            def _(c):
+                at_rows = block_rows(c)
+                for_gain = jnp.sum((gsum[at_rows] * source(at_rows) * inverse).T, 0, keepdims=True)
+                small[c, gain_lane : gain_lane + 1, 0:rows] = for_gain
+
+        return gain_back
+
+    def store_middle(at_rows, value):
+        gmid[at_rows] = value
+        sending[1, at_rows] = value.astype(BF16)
+
+    gain_two_back = norm_back(
+        lambda r: mid[r], inverse_two, 1, lambda r: gs[r, lanes(first)].astype(F32), store_middle
+    )
+    mid_in = Gather(sending.at[1], token_block)
+    gain_two_back()
+    ffn_sum.combine()
+    mid_in.pass_on()
+    ffn_sum.send()
+    mid_in.arrive()
 
     @pl.loop(0, 2)
     def _(h):
@@ -1041,6 +1263,8 @@
         for c in range(1, 4):
             total += dot(at[h, c, HEADROWS:, :rows], low2[c * rows : (c + 1) * rows], 1, 0)
         gatt[h] = total.astype(BF16)
+
+    main_back.relay(add_tiles(away(plane, 2)))
 
     @pl.loop(0, 2)
     def _(h):
@@ -1081,33 +1305,10 @@
         for j in range(CONV):
             columns = jnp.where(tail == rows % TILE + j, sums[j], columns)
         for c in range(4):
-            gat[h, c, HEADROWS:, WIDE - TILE :] = columns.astype(BF16)
-
-    finish()
-    res_send, res_here = marks.many(3), marks.many(3)
-    tok_send, tok_here = marks.many(3), marks.many(3)
-    kept = []
-
-    def hand_out(source, target, send, receive):
-        copies = [
-            remote(
-                source.at[block_rows(others[p])], target.at[:, lanes(chip * TILE)],
-                send(p), receive(p), peers[p],
-            )
-            for p in range(3)
-        ]
-        for copy in copies:
-            copy.start()
-        kept.append(
-            pltpu.make_async_copy(
-                source.at[block_rows(chip)], target.at[:, lanes(chip * TILE)], marks.one()
-            )
-        )
-        kept[-1].start()
-        return copies
-
-    turned_rows = both.at[:, 0:TILE]
-    outs = hand_out(turned_rows, out_res, res_send, res_here)
+            gat[h, c, 2 * FEAT : HEADROWS, WIDE - TILE :] = columns.astype(BF16)
+
+    ffn_sum.pass_on()
+    mid_in.finish()
 
     def fill_grad_one(start):
         @pl.loop(0, 4)
@@ -1117,37 +1318,81 @@
             total += dot(at[1, c, :HEADROWS, :rows], gproj[1, :, where], 0, 0)
             part[block_rows(c), where] = total.astype(BF16)
 
-    acc3[:, 0:TILE] = gmid[...]
-    for copy in outs:
-        copy.wait()
-    for copy in kept:
-        copy.wait()
-    finish = plane_sum(fill_grad_one, store_gmid, guard=True)
-
-    @pl.loop(0, 2)
-    def _(h):
-        for c in range(4):
-            block = slice(c * rows, (c + 1) * rows)
-            gat[h, c, :HEADROWS, :rows] = dot(gproj[h], xs[block], 1, 1).astype(BF16)
-            grad = dot(att[h], low2[block], 1, 1).astype(BF16)
-            whole = rows // TILE * TILE
-            gat[h, c, HEADROWS:, :whole] = grad[:, :whole]
-            gat[h, c, HEADROWS:, whole:rows] = grad[:, whole:]
-
-    att_back = [
-        Collect(gat.at[a], att_got.at[a], 2 * core + a, chip, plane, core, marks)
-        for a in range(2)
+    one_sum = Sum(guard=True)
+    one_sum.begin(fill_grad_one)
+    one_sum.combine()
+    one_sum.send()
+
+    out_back, in_back = [
+        [
+            Collect(
+                gat.at[a, :, span], att_got.at[a, :, :, span], 2 * core + a,
+                chip, plane, core, marks,
+            )
+            for a in range(2)
+        ]
+        for span in (out_rows, in_rows)
     ]
-    for item in att_back:
+
+    def head_grads(left, right, start, size):
+        whole = rows // TILE * TILE
+
+        @pl.loop(0, 2)
+        def _(h):
+            for c in range(4):
+                grad = dot(left[h], right[c * rows : (c + 1) * rows], 1, 1).astype(BF16)
+                gat[h, c, start : start + size, :whole] = grad[:, :whole]
+                gat[h, c, start : start + size, whole:rows] = grad[:, whole:]
+
+    head_grads(att, low2, HEADROWS, HDIM)
+    for item in out_back:
         item.start(None)
-    finish()
-
+    head_grads(gproj, xs, 0, HEADROWS)
+    for item in in_back:
+        item.start(None)
+
+    def store_result(at_rows, total):
+        note_square(1, total)
+        total = mid[at_rows] + total
+        note_square(2, total)
+        sending[0, at_rows] = total.astype(BF16)
+
+    one_sum.pass_on()
+
+    def hand_out(source, target):
+        send, here = marks.many(3), marks.many(3)
+        copies = [
+            remote(
+                source.at[block_rows(others[p])], target.at[:, lanes(chip * TILE)],
+                send(p), here(p), peers[p],
+            )
+            for p in range(3)
+        ]
+        copies.append(
+            pltpu.make_async_copy(
+                source.at[block_rows(chip)], target.at[:, lanes(chip * TILE)], marks.one()
+            )
+        )
+        for copy in copies:
+            copy.start()
+        return copies
+
+    ffn_sum.finish(store_result)
+    pending = hand_out(sending.at[0], out_res)
+
+    extra_back.relay(add_tiles(4))
+
+    one_sum.finish(store_gsum)
     inverse_own = inv_all[:, lanes(first)]
-    norm_back(
-        lambda r: normed[r].astype(F32), inverse_own, 0, 0, lambda r: acc3[r, 0:TILE]
-    )
-    both[:, TILE : 2 * TILE] = gmid[...].astype(BF16)
-    outs = hand_out(both.at[:, TILE : 2 * TILE], out_tok, tok_send, tok_here)
+
+    def store_tokens(at_rows, value):
+        sending[1, at_rows] = value.astype(BF16)
+
+    gain_one_back = norm_back(
+        lambda r: normed[r].astype(F32), inverse_own, 0, lambda r: gmid[r], store_tokens
+    )
+    pending += hand_out(sending.at[1], out_tok)
+    gain_one_back()
 
     for c in range(1, 4):
         small[c, 2:3] = small[0, 2:3]
@@ -1158,6 +1403,24 @@
     ]
     for copy in trio:
         copy.start()
+
+    main_back.total(add_tiles(plane))
+    back_send, back_here = marks.many(3), marks.many(3)
+    mine = lanes(plane * TILE)
+    back_to = out_ff.at[:, :, lanes(chip * TILE)]
+    backs = [
+        remote(
+            gout.at[:, block_rows(others[p]), mine], back_to, back_send(p), back_here(p), peers[p]
+        )
+        for p in range(3)
+    ]
+    backs.append(
+        pltpu.make_async_copy(gout.at[:, block_rows(chip), mine], back_to, marks.one())
+    )
+    for copy in backs:
+        copy.start()
+    pending += backs
+
     for copy in trio:
         copy.wait()
     small_b[0] = small[chip] + small_a[0] + small_a[1] + small_a[2]
@@ -1169,27 +1432,6 @@
     for copy in seven:
         copy.start()
 
-    add_own = add_tiles(plane)
-    for o in range(4):
-        main_back[o].total(add_own)
-    back_send, back_here = marks.many(3), marks.many(3)
-    mine = lanes(plane * TILE)
-    backs = [
-        remote(
-            gout.at[:, block_rows(others[p]), mine], out_ff.at[:, :, lanes(chip * TILE)],
-            back_send(p), back_here(p), peers[p],
-        )
-        for p in range(3)
-    ]
-    for copy in backs:
-        copy.start()
-    kept.append(
-        pltpu.make_async_copy(
-            gout.at[:, block_rows(chip), mine], out_ff.at[:, :, lanes(chip * TILE)], marks.one()
-        )
-    )
-    kept[-1].start()
-
     extra_back.total(add_tiles(4))
     last_send, last_here, last_local = marks.many(4), marks.one(), marks.one()
 
@@ -1215,30 +1457,35 @@
         def _():
             last_copy(c).start()
 
-    def add_head(a):
+    head_marks = marks.many(4)
+
+    def add_head(a, start, size):
         def add(source):
             loads = [
                 pltpu.make_async_copy(
-                    source.at[c], part.at[c * BLOCKROWS : (c + 1) * BLOCKROWS, 0:WIDE],
-                    load_marks(0),
+                    source.at[c], part.at[c * BLOCKROWS : c * BLOCKROWS + size, 0:WIDE],
+                    head_marks(c),
                 )
                 for c in range(4)
             ]
             for load in loads:
                 load.start()
+            for load in loads:
                 load.wait()
             for c in range(4):
-                gat[a, c] = (
-                    gat[a, c].astype(F32)
-                    + part[c * BLOCKROWS : (c + 1) * BLOCKROWS, 0:WIDE].astype(F32)
+                gat[a, c, start : start + size] = (
+                    gat[a, c, start : start + size].astype(F32)
+                    + part[c * BLOCKROWS : c * BLOCKROWS + size, 0:WIDE].astype(F32)
                 ).astype(BF16)
 
         return add
 
-    for a in range(2):
-        att_back[a].relay(add_head(a))
-    for a in range(2):
-        att_back[a].total(add_head(a))
+    for items, start, size in ((out_back, HEADROWS, HDIM), (in_back, 0, HEADROWS)):
+        for a in range(2):
+            items[a].relay(add_head(a, start, size))
+    for items, start, size in ((out_back, HEADROWS, HDIM), (in_back, 0, HEADROWS)):
+        for a in range(2):
+            items[a].total(add_head(a, start, size))
     head_send, head_here, head_local = marks.many(4), marks.many(2), marks.one()
 
     def head_copy(c):
@@ -1269,12 +1516,10 @@
     small_a[0] = total
     small_out = pltpu.make_async_copy(small_a.at[0], out_small, marks.one())
     small_out.start()
-    kept.append(small_out)
-    for item in att_line + main_line + [extra_line] + main_back + [extra_back] + att_back:
+    pending.append(small_out)
+    for item in in_line + out_line + [extra_line, main_back, extra_back] + out_back + in_back:
         item.finish()
-    for copy in outs + backs:
-        copy.wait()
-    for copy in kept[1:]:
+    for copy in pending:
         copy.wait()
     for c in range(4):
         for holds, same, local, away_copy in (
@@ -1303,7 +1548,7 @@
             ).wait_recv()
 
     pl.semaphore_wait(free_mate, 1)
-    pl.semaphore_wait(free_chips, 3)
+    pl.semaphore_wait(free_chips, 2)
     assert marks.used <= MARKS, marks.used
 
 
@@ -1348,7 +1593,8 @@
             vmem((3 * TILE, width), BF16),
             vmem((5 * TILE, seq), BF16),
             vmem((2 * TILE, seq), BF16),
-            vmem((width, TILE), BF16),
+            vmem((4, 16, WIDE), BF16),
+            vmem((width, TILE), F32),
             vmem((2, HDIM, seq), F32),
             vmem((2, FEAT, seq), BF16),
             vmem((2, FEAT, seq), BF16),
@@ -1358,7 +1604,9 @@
             vmem((2, HEADROWS, seq), BF16),
             vmem((width, TILE), F32),
             vmem((width, TILE), F32),
+            vmem((width, TILE), F32),
             vmem((width, TILE), BF16),
+            vmem((2, width, TILE), BF16),
             vmem((1, seq), F32),
             vmem((2, 1, seq), F32),
             vmem((4, 8, WIDE), F32),
@@ -1383,20 +1631,15 @@
     heads = 2
     pad = ((0, 0), (0, 5 * TILE - ffn_cols))
     wff = jnp.stack([jnp.pad(w, pad) for w in (w_gate, w_up, w_down)])
-    upper = jnp.pad(
-        w_qkv.T.reshape(heads, HEADROWS, rows), ((0, 0), (0, 0), (0, WIDE - rows))
-    )
-    lower = jnp.concatenate(
-        [
-            w_out.reshape(heads, HDIM, rows),
-            conv_weight.T.reshape(heads, HDIM, CONV),
-            jnp.zeros((heads, HDIM, WIDE - rows - CONV), BF16),
-        ],
-        2,
-    )
+    taps = jnp.pad(
+        conv_weight.T.reshape(heads, HDIM, CONV),
+        ((0, 0), (2 * FEAT, 0), (0, WIDE - rows - CONV)),
+    )
+    upper = jnp.concatenate([w_qkv.T.reshape(heads, HEADROWS, rows), taps], 2)
+    lower = jnp.pad(w_out.reshape(heads, HDIM, rows), ((0, 0), (0, 0), (0, WIDE - rows)))
     wat = jnp.concatenate([upper, lower], 1)
-    gains = jnp.concatenate(
-        [jnp.broadcast_to(g[:, None], (rows, TILE // 2)) for g in (gain_mix, gain_ffn)], 1
+    gains = jnp.pad(
+        jnp.stack([gain_mix, gain_ffn]), ((0, 14), (0, WIDE - rows))
     )
     out_ff, out_at, out_res, out_tok, small = run_layer(wff, wat, tokens, cotangent, gains)[:5]
     out_at = out_at.astype(F32)
@@ -1404,7 +1647,7 @@
         out_res,
         out_tok.astype(F32),
         out_at[:, :HEADROWS, :rows].reshape(heads * HEADROWS, rows).T,
-        out_at[:, HEADROWS:, rows : rows + CONV].reshape(heads * HDIM, CONV).T,
+        out_at[:, 2 * FEAT : HEADROWS, rows : rows + CONV].reshape(heads * HDIM, CONV).T,
         out_at[:, HEADROWS:, :rows].reshape(heads * HDIM, rows),
         out_ff[0, :, :ffn_cols].astype(F32),
         out_ff[1, :, :ffn_cols].astype(F32),

time: 525 us -> 345 us (0.66)
  Pallas kernels: 505 us -> 324 us
    pallas_call x1, Pallas kernels: 505 us -> 324 us  [run_layer(): pl.pallas_call(layer_kernel, out_shape=[shape((3, rows, 5 * TILE), BF16),...]
where the time goes in v3:
time: 345 us; the launch traced here: 344 us
  Pallas kernels  324 us (94%)
  local copies, waits for them, and re-layouts  11 us (3%)
  other arithmetic  8.16 us (2%)
    pallas_call x1, Pallas kernels, run_layer(): pl.pallas_call(layer_kernel, out_shape=[shape((3, rows, 5 * TILE), BF16),...  324 us

profile of v3, /device:TPU:4, one launch (start us, length us, event | category | flops | bytes accessed | tf_op | source)
XLA Modules:
  0.0 343.9 jit_solution(10362745472752342892)
XLA Ops:
  0.6 0.0 copy-start.1
  0.7 0.0 copy-start.2
  0.7 0.8 stack.25
  1.4 0.7 stack.26
  2.1 0.6 fusion.11.gains
  2.7 0.8 copy.21
  3.6 2.0 fusion.4.wat
  5.6 1.1 pad_bitcast_fusion.2
  6.7 0.0 copy-done.1
  6.7 0.0 copy-done.2
  6.7 0.1 pad_bitcast_fusion
  6.8 1.4 pad_maximum_fusion.wff
  8.2 324.0 %layer.1 = (bf16[3,448,640]{2,1,0:T(8,128)(2,1)}, bf16[2,256,512]{2,1,0:T(8,128)(2,1)}, bf16[448,512]{1,0:T(8,128)(2,1)}, bf16[448,512]{1,0:T(8,128)(2,1)}, f32[...) custom-call(bf16[3,448,640]{2,1,0:T(8,128)(2,1)} %pad_maximum_fusion, ...), custom_call_target="tpu_custom_call" | custom-call | tf_op jit(solution)/shard_map/layer/pallas_call | solution.py:1566
  332.2 0.0 copy-start.4
  332.2 1.3 sqrt_bitcast_fusion
  333.5 1.4 fusion.12
  334.9 0.9 slice.37
  335.8 0.7 copy.22
  336.5 0.0 copy-start
  336.5 1.9 slice.38
  338.4 1.8 slice.36
  340.2 0.0 copy-done.4
  340.2 1.0 convert_element_type.34
  341.2 0.0 copy-done
  341.2 0.0 copy-start.3
  341.2 1.8 bitcast_convert_fusion
  343.1 0.0 copy-done.3
  343.1 0.8 copy.24
Async XLA Ops:
  0.6 6.0 %copy-start.1 = (bf16[448,608]{1,0:T(8,128)(2,1)S(1)}, bf16[448,608]{1,0:T(8,128)(2,1)}, u32[]{:S(2)}) copy-start(bf16[448,608]{1,0:T(8,128)(2,1)} %param.19) | copy-start | bytes 1634308
  0.7 6.0 %copy-start.2 = (bf16[448,608]{1,0:T(8,128)(2,1)S(1)}, bf16[448,608]{1,0:T(8,128)(2,1)}, u32[]{:S(2)}) copy-start(bf16[448,608]{1,0:T(8,128)(2,1)} %param.18) | copy-start | bytes 1634308
  332.2 8.0 %copy-start.4 = (bf16[448,512]{1,0:T(8,128)(2,1)S(1)}, bf16[448,512]{1,0:T(8,128)(2,1)}, u32[]{:S(2)}) copy-start(bf16[448,512]{1,0:T(8,128)(2,1)} %get-tuple-element.17) | copy-start | bytes 1376260
  336.5 4.8 %copy-start = (bf16[3,448,640]{2,1,0:T(8,128)(2,1)S(1)}, bf16[3,448,640]{2,1,0:T(8,128)(2,1)}, u32[]{:S(2)}) copy-start(bf16[3,448,640]{2,1,0:T(8,128)(2,1)} %get-tuple-element.19) | copy-start | bytes 5160964
  341.2 1.8 copy-start.3

commit v4 on v3

--- a/solution.py
+++ b/solution.py
@@ -437,13 +437,16 @@
 
 
 class Spread:
-    def __init__(self, ref, owner, chip, plane, core, marks, forward):
-        self.ref, self.owner, self.spot = ref, owner, (chip, plane, core)
-        self.sends = marks.many(4)
+    def __init__(self, ref, owner, chip, plane, core, marks):
+        self.ref, self.spot = ref, (chip, plane, core)
+        self.sends = marks.many(3)
         self.arrived = marks.one()
+        inner = is_inner(plane)
         self.mine = plane == owner
-        self.forward = forward
-        self.relays = is_inner(plane) & (plane == away(owner, 2))
+        self.outer_owner = self.mine & no(inner)
+        self.inner_owner = self.mine & inner
+        far = (plane == away(owner, 2)) | ((plane == away(owner, 3)) & is_inner(owner))
+        self.relays = inner & far
 
     def copy(self, step, send):
         chip, plane, core = self.spot
@@ -452,53 +455,76 @@
             device(chip, away(plane, step), core),
         )
 
-    def far(self):
-        return self.mine & is_inner(self.spot[1]) if self.forward else self.mine
-
     def start(self):
-        @pl.when(self.far())
-        def _():
-            self.copy(3, 2).start()
-
-        @pl.when(self.mine)
-        def _():
-            self.copy(2, 1).start()
-            self.copy(1, 0).start()
+        pl.when(self.outer_owner)(lambda: self.copy(2, 1).start())
+        pl.when(self.inner_owner)(lambda: self.copy(3, 1).start())
+        pl.when(self.mine)(lambda: self.copy(1, 0).start())
 
     def relay(self):
         @pl.when(self.relays)
         def _():
-            self.copy(1, 3).wait_recv()
-            self.copy(1, 3).start()
+            self.copy(1, 2).wait_recv()
+            self.copy(1, 2).start()
 
     def arrive(self):
-        done = self.mine | self.relays if self.forward else self.mine
-
-        @pl.when(no(done))
-        def _():
-            self.copy(1, 3).wait_recv()
+        pl.when(no(self.mine | self.relays))(lambda: self.copy(1, 2).wait_recv())
 
     def finish(self):
         @pl.when(self.mine)
         def _():
             self.copy(1, 0).wait_send()
-            self.copy(2, 1).wait_send()
-
-        @pl.when(self.far())
-        def _():
-            self.copy(3, 2).wait_send()
-
-        if self.forward:
-
-            @pl.when(self.relays)
-            def _():
-                self.copy(1, 3).wait_send()
+            self.copy(1, 1).wait_send()
+
+        pl.when(self.relays)(lambda: self.copy(1, 2).wait_send())
+
+
+class Chain:
+    def __init__(self, ref, owner, chip, plane, core, marks):
+        self.ref, self.spot = ref, (chip, plane, core)
+        self.sends = marks.many(2)
+        self.arrived = marks.one()
+        inner = is_inner(plane)
+        self.mine = plane == owner
+        self.mine_inner = self.mine & inner
+        self.from_end = inner & (plane == away(owner, 1))
+        self.from_inner = inner & (plane == away(owner, 3))
+        self.from_far = inner & (plane == away(owner, 2))
+        self.waits = no(inner) & no(self.mine)
+
+    def copy(self, step, send):
+        chip, plane, core = self.spot
+        return remote(
+            self.ref, self.ref, self.sends(send), self.arrived,
+            device(chip, away(plane, step), core),
+        )
+
+    def start(self):
+        pl.when(self.mine)(lambda: self.copy(1, 0).start())
+        pl.when(self.mine_inner)(lambda: self.copy(3, 1).start())
+
+    def relay(self):
+        pl.when(self.from_end | self.from_inner)(lambda: self.copy(1, 0).wait_recv())
+        pl.when(self.from_end)(lambda: self.copy(3, 0).start())
+        pl.when(self.from_inner)(lambda: self.copy(1, 0).start())
+
+    def relay_far(self):
+        @pl.when(self.from_far)
+        def _():
+            self.copy(1, 0).wait_recv()
+            self.copy(1, 0).start()
+
+    def arrive(self):
+        pl.when(self.waits)(lambda: self.copy(1, 0).wait_recv())
+
+    def finish(self):
+        pl.when(no(self.waits))(lambda: self.copy(1, 0).wait_send())
+        pl.when(self.mine_inner)(lambda: self.copy(3, 1).wait_send())
 
 
 class MainTiles:
     def __init__(self, ff, chip, plane, core, marks):
         self.ff, self.spot = ff, (chip, plane, core)
-        self.sends, self.here = marks.many(4), marks.many(3)
+        self.sends, self.here = marks.many(5), marks.many(3)
         self.inner = is_inner(plane)
 
     def copy(self, slot, to_step, send, receive):
@@ -509,49 +535,48 @@
             device(chip, away(plane, to_step), core),
         )
 
-    def start_all(self):
-        near, next_on, far = [
-            self.copy(self.spot[1], step, step - 1, step - 1) for step in (1, 2, 3)
-        ]
+    def got(self, step):
+        self.copy(self.spot[1], 1, 0, step - 1).wait_recv()
+
+    def start(self):
+        plane = self.spot[1]
+        self.copy(plane, 1, 0, 0).start()
+        pl.when(self.inner)(lambda: self.copy(plane, 3, 2, 2).start())
+
+    def relay(self):
+        plane = self.spot[1]
 
         @pl.when(self.inner)
         def _():
-            near.start()
-            next_on.start()
-            far.start()
-
-        @pl.when(no(self.inner))
-        def _():
-            next_on.start()
-            near.start()
-
-    def relay(self):
+            self.got(1)
+            self.copy(away(plane, 1), 3, 1, 1).start()
+            self.got(3)
+            self.copy(away(plane, 3), 1, 3, 1).start()
+
+    def relay_far(self):
+        plane = self.spot[1]
+
         @pl.when(self.inner)
         def _():
-            self.copy(self.spot[1], 1, 0, 1).wait_recv()
-            self.copy(away(self.spot[1], 2), 1, 3, 2).start()
+            self.got(2)
+            self.copy(away(plane, 2), 1, 4, 2).start()
 
     def arrive(self, step):
-        copy = self.copy(self.spot[1], 1, 0, step - 1)
-        if step == 2:
-            pl.when(no(self.inner))(copy.wait_recv)
-        else:
-            copy.wait_recv()
+        pl.when(no(self.inner))(lambda: self.got(step))
 
     def finish(self):
-        for step in (1, 2):
-            self.copy(self.spot[1], 1, step - 1, 0).wait_send()
+        self.copy(self.spot[1], 1, 0, 0).wait_send()
 
         @pl.when(self.inner)
         def _():
-            self.copy(self.spot[1], 1, 2, 0).wait_send()
-            self.copy(self.spot[1], 1, 3, 0).wait_send()
+            for send in range(1, 5):
+                self.copy(self.spot[1], 1, send, 0).wait_send()
 
 
 class MainGrads:
     def __init__(self, gout, slots, chip, plane, core, marks):
         self.gout, self.slots, self.spot = gout, slots, (chip, plane, core)
-        self.sends, self.here = marks.many(3), marks.many(4)
+        self.sends, self.here = marks.many(3), marks.many(5)
         self.inner = is_inner(plane)
 
     def copy(self, slot, to_step, send, receive):
@@ -562,34 +587,32 @@
         )
 
     def start(self, step):
-        plane = self.spot[1]
-        if step == 1:
-            self.copy(away(plane, 1), 1, 0, 0).start()
-        if step == 2:
-            pl.when(no(self.inner))(self.copy(away(plane, 2), 2, 1, 1).start)
-        if step == 3:
-            pl.when(self.inner)(self.copy(away(plane, 3), 3, 2, 2).start)
-            pl.when(no(self.inner))(self.copy(away(plane, 3), 1, 2, 3).start)
-
-    def relay(self, add):
-        plane = self.spot[1]
-
+        receive = {1: 0, 2: 4, 3: 3}[step]
+        self.copy(away(self.spot[1], step), 1, step - 1, receive).start()
+
+    def relay(self, step, add):
         @pl.when(self.inner)
         def _():
-            self.copy(plane, 1, 0, 3).wait_recv()
-            add(self.slots.at[3])
-            self.copy(away(plane, 2), 2, 1, 1).start()
+            receive = {2: 3, 3: 4}[step]
+            self.copy(self.spot[1], 1, 0, receive).wait_recv()
+            slot = away(self.spot[1], step)
+            add(slot, self.slots.at[receive])
+            self.copy(slot, step, step - 1, step - 1).start()
 
     def total(self, add):
         plane = self.spot[1]
-        for receive in range(2):
-            self.copy(plane, 1, 0, receive).wait_recv()
-            add(self.slots.at[receive])
+        self.copy(plane, 1, 0, 0).wait_recv()
+        add(plane, self.slots.at[0])
+
+        @pl.when(no(self.inner))
+        def _():
+            self.copy(plane, 1, 0, 1).wait_recv()
+            add(plane, self.slots.at[1])
 
         @pl.when(self.inner)
         def _():
             self.copy(plane, 1, 0, 2).wait_recv()
-            add(self.slots.at[2])
+            add(plane, self.slots.at[2])
 
     def finish(self):
         for send in range(3):
@@ -598,15 +621,18 @@
 
 class Collect:
     def __init__(self, ref, slots, owner, chip, plane, core, marks):
-        self.ref, self.slots, self.owner, self.spot = ref, slots, owner, (chip, plane, core)
+        self.ref, self.slots, self.spot = ref, slots, (chip, plane, core)
         self.send = marks.one()
-        self.arrived = marks.many(4)
-        outer = no(is_inner(owner))
+        self.arrived = marks.many(3)
+        inner, inner_owner = is_inner(plane), is_inner(owner)
         self.mine = plane == owner
-        self.first = plane == away(owner, 1)
-        self.second = plane == away(owner, 2)
-        self.third = plane == away(owner, 3)
-        self.outer = outer
+        self.mine_outer = self.mine & no(inner)
+        self.mine_inner = self.mine & inner
+        self.near = plane == away(owner, 1)
+        second, third = plane == away(owner, 2), plane == away(owner, 3)
+        self.hands = no(inner) & (second | third) & no(self.near)
+        self.adds_second = inner & second & no(inner_owner)
+        self.adds_third = inner & third & inner_owner
 
     def copy(self, step, slot):
         chip, plane, core = self.spot
@@ -615,47 +641,28 @@
             device(chip, away(plane, step), core),
         )
 
-    def start(self, add):
-        @pl.when(self.first)
-        def _():
-            self.copy(1, 0).start()
-
-        @pl.when(self.third & self.outer)
-        def _():
-            self.copy(1, 3).start()
-
-        @pl.when(self.third & no(self.outer))
-        def _():
-            self.copy(3, 2).start()
-
-        @pl.when(self.second & no(self.outer))
-        def _():
-            self.copy(2, 1).start()
+    def start(self):
+        pl.when(self.near)(lambda: self.copy(1, 0).start())
+        pl.when(self.hands)(lambda: self.copy(1, 2).start())
 
     def relay(self, add):
-        @pl.when(self.second & self.outer)
-        def _():
-            self.copy(1, 3).wait_recv()
-            add(self.slots.at[3])
-            self.copy(2, 1).start()
+        @pl.when(self.adds_second | self.adds_third)
+        def _():
+            self.copy(1, 2).wait_recv()
+            add(self.slots.at[2])
+
+        pl.when(self.adds_second)(lambda: self.copy(2, 1).start())
+        pl.when(self.adds_third)(lambda: self.copy(3, 1).start())
 
     def total(self, add):
         @pl.when(self.mine)
         def _():
-            self.copy(1, 0).wait_recv()
-            add(self.slots.at[0])
-            self.copy(1, 1).wait_recv()
-            add(self.slots.at[1])
-
-        @pl.when(self.mine & no(self.outer))
-        def _():
-            self.copy(1, 2).wait_recv()
-            add(self.slots.at[2])
+            for slot in range(2):
+                self.copy(1, slot).wait_recv()
+                add(self.slots.at[slot])
 
     def finish(self):
-        @pl.when(no(self.mine))
-        def _():
-            self.copy(1, 0).wait_send()
+        pl.when(no(self.mine))(lambda: self.copy(1, 0).wait_send())
 
 
 def layer_kernel(
@@ -799,7 +806,7 @@
     out_rows, in_rows = pl.ds(HEADROWS, HDIM), pl.ds(0, HEADROWS)
     in_line, out_line = [
         [
-            Spread(at.at[a, :, span], 2 * core + a, chip, plane, core, marks, forward=True)
+            Spread(at.at[a, :, span], 2 * core + a, chip, plane, core, marks)
             for a in range(2)
         ]
         for span in (in_rows, out_rows)
@@ -877,33 +884,6 @@
 
     for item in out_line:
         item.relay()
-    main_keep.wait()
-    for copy in mains:
-        copy.wait()
-    main_line = MainTiles(ff, chip, plane, core, marks)
-    main_line.start_all()
-
-    @pl.when(extra_self)
-    def _():
-        extra_keep().wait()
-
-    @pl.when(no(extra_self))
-    def _():
-        extra_copy().wait_send()
-
-    for c in range(4):
-
-        @pl.when(holds_extra & no((c == chip) & (core == chip % 2)))
-        def _():
-            remote(
-                wff.at[:, :, last], ff.at[:, block_rows(c), last], extra_send, extra_here(c), mate
-            ).wait_recv()
-
-    extra_line = Spread(ff.at[:, :, last], extra_plane, chip, plane, core, marks, forward=True)
-    extra_line.start()
-
-    cot_in.pass_on()
-
     for item in in_line:
         item.arrive()
 
@@ -948,6 +928,33 @@
             inv_sum[h, :, b * SPAN : seen] = inverse
             weights = (kernel * inverse).astype(BF16)
             att[h, :, b * SPAN : seen] = dot(vs[h, :, :seen], weights, 1, 0).astype(BF16)
+
+    main_keep.wait()
+    for copy in mains:
+        copy.wait()
+    main_line = MainTiles(ff, chip, plane, core, marks)
+    main_line.start()
+
+    @pl.when(extra_self)
+    def _():
+        extra_keep().wait()
+
+    @pl.when(no(extra_self))
+    def _():
+        extra_copy().wait_send()
+
+    for c in range(4):
+
+        @pl.when(holds_extra & no((c == chip) & (core == chip % 2)))
+        def _():
+            remote(
+                wff.at[:, :, last], ff.at[:, block_rows(c), last], extra_send, extra_here(c), mate
+            ).wait_recv()
+
+    extra_line = Chain(ff.at[:, :, last], extra_plane, chip, plane, core, marks)
+    extra_line.start()
+
+    cot_in.pass_on()
 
     for item in out_line:
         item.arrive()
@@ -1094,8 +1101,9 @@
     low_in.pass_on()
     low_in.arrive()
     low_in.finish()
+
     extra_line.relay()
-
+    main_line.relay_far()
     def feed(slot):
         where = lanes(slot * TILE)
         unit_rows = rows_at(slot * TILE, TILE, TILE)
@@ -1130,34 +1138,36 @@
     extra_back = Collect(gout.at[:, :, last], extra_got, extra_plane, chip, plane, core, marks)
     load_marks = marks.many(3)
 
-    def add_tiles(slot):
-        def add(source):
-            loads = [
-                pltpu.make_async_copy(source.at[m], part.at[:, lanes(m * TILE)], load_marks(m))
-                for m in range(3)
-            ]
-            for load in loads:
-                load.start()
-            for load in loads:
-                load.wait()
-            where = lanes(slot * TILE)
-
-            @pl.loop(0, 4)
-            def _(c):
-                at_rows = block_rows(c)
-                for m in range(3):
-                    gout[m, at_rows, where] = (
-                        gout[m, at_rows, where].astype(F32)
-                        + part[at_rows, m * TILE : (m + 1) * TILE].astype(F32)
-                    ).astype(BF16)
-
-        return add
+    def add_tiles(slot, source):
+        loads = [
+            pltpu.make_async_copy(source.at[m], ff.at[2, :, lanes(m * TILE)], load_marks(m))
+            for m in range(3)
+        ]
+        for load in loads:
+            load.start()
+        for load in loads:
+            load.wait()
+        where = lanes(slot * TILE)
+
+        @pl.loop(0, 4)
+        def _(c):
+            at_rows = block_rows(c)
+            for m in range(3):
+                gout[m, at_rows, where] = (
+                    gout[m, at_rows, where].astype(F32)
+                    + ff[2, at_rows, m * TILE : (m + 1) * TILE].astype(F32)
+                ).astype(BF16)
+
+    def add_extra(source):
+        add_tiles(4, source)
 
     slots = [away(plane, 1), plane, away(plane, 2), away(plane, 3), 4]
     inner = is_inner(plane)
 
     @pl.loop(0, 5)
     def _(turn):
+        pl.when(turn == 2)(lambda: extra_line.relay_far())
+
         for i, step in ((0, 1), (2, 2), (3, 3)):
 
             @pl.when(turn == i)
@@ -1171,21 +1181,15 @@
         slot = sum((turn == i).astype(jnp.int32) * slots[i] for i in range(5))
         feed(slot)
 
-        @pl.when((turn == 0) & no(inner))
-        def _():
-            main_back.start(1)
-
-        @pl.when((turn == 3) & no(inner))
-        def _():
-            main_back.start(3)
-            main_back.start(2)
-
-    @pl.when(inner)
-    def _():
-        main_back.start(1)
-        main_back.start(3)
-
-    extra_back.start(None)
+        for i, step in ((0, 1), (2, 2), (3, 3)):
+
+            @pl.when((turn == i) & no(inner))
+            def _():
+                main_back.start(step)
+
+    pl.when(inner)(lambda: main_back.start(1))
+
+    extra_back.start()
     main_line.finish()
 
     def fill_grad_two(start):
@@ -1218,6 +1222,7 @@
     ffn_sum.begin(fill_ffn)
     two_sum.finish(store_gsum)
 
+    main_back.relay(3, add_tiles)
     def norm_back(source, inverse, gain_lane, base, store):
         def add_dots(c, total):
             at_rows = block_rows(c)
@@ -1264,7 +1269,33 @@
             total += dot(at[h, c, HEADROWS:, :rows], low2[c * rows : (c + 1) * rows], 1, 0)
         gatt[h] = total.astype(BF16)
 
-    main_back.relay(add_tiles(away(plane, 2)))
+    main_back.relay(2, add_tiles)
+
+    out_back, in_back = [
+        [
+            Collect(
+                gat.at[a, :, span], att_got.at[a, :, :, span], 2 * core + a,
+                chip, plane, core, marks,
+            )
+            for a in range(2)
+        ]
+        for span in (out_rows, in_rows)
+    ]
+
+    def head_grads(left, right, start, size):
+        whole = rows // TILE * TILE
+
+        @pl.loop(0, 2)
+        def _(h):
+            for c in range(4):
+                grad = dot(left[h], right[c * rows : (c + 1) * rows], 1, 1).astype(BF16)
+                gat[h, c, start : start + size, :whole] = grad[:, :whole]
+                gat[h, c, start : start + size, whole:rows] = grad[:, whole:]
+
+    head_grads(att, low2, HEADROWS, HDIM)
+    for item in out_back:
+        item.start()
+
 
     @pl.loop(0, 2)
     def _(h):
@@ -1307,6 +1338,10 @@
         for c in range(4):
             gat[h, c, 2 * FEAT : HEADROWS, WIDE - TILE :] = columns.astype(BF16)
 
+    head_grads(gproj, xs, 0, HEADROWS)
+    for item in in_back:
+        item.start()
+
     ffn_sum.pass_on()
     mid_in.finish()
 
@@ -1322,34 +1357,7 @@
     one_sum.begin(fill_grad_one)
     one_sum.combine()
     one_sum.send()
-
-    out_back, in_back = [
-        [
-            Collect(
-                gat.at[a, :, span], att_got.at[a, :, :, span], 2 * core + a,
-                chip, plane, core, marks,
-            )
-            for a in range(2)
-        ]
-        for span in (out_rows, in_rows)
-    ]
-
-    def head_grads(left, right, start, size):
-        whole = rows // TILE * TILE
-
-        @pl.loop(0, 2)
-        def _(h):
-            for c in range(4):
-                grad = dot(left[h], right[c * rows : (c + 1) * rows], 1, 1).astype(BF16)
-                gat[h, c, start : start + size, :whole] = grad[:, :whole]
-                gat[h, c, start : start + size, whole:rows] = grad[:, whole:]
-
-    head_grads(att, low2, HEADROWS, HDIM)
-    for item in out_back:
-        item.start(None)
-    head_grads(gproj, xs, 0, HEADROWS)
-    for item in in_back:
-        item.start(None)
+    extra_back.relay(add_extra)
 
     def store_result(at_rows, total):
         note_square(1, total)
@@ -1380,7 +1388,6 @@
     ffn_sum.finish(store_result)
     pending = hand_out(sending.at[0], out_res)
 
-    extra_back.relay(add_tiles(4))
 
     one_sum.finish(store_gsum)
     inverse_own = inv_all[:, lanes(first)]
@@ -1404,7 +1411,7 @@
     for copy in trio:
         copy.start()
 
-    main_back.total(add_tiles(plane))
+    main_back.total(add_tiles)
     back_send, back_here = marks.many(3), marks.many(3)
     mine = lanes(plane * TILE)
     back_to = out_ff.at[:, :, lanes(chip * TILE)]
@@ -1432,7 +1439,7 @@
     for copy in seven:
         copy.start()
 
-    extra_back.total(add_tiles(4))
+    extra_back.total(add_extra)
     last_send, last_here, last_local = marks.many(4), marks.one(), marks.one()
 
     def last_copy(c):
@@ -1571,7 +1578,7 @@
             shape((rows, half), BF16),
             shape((rows, half), BF16),
             shape((8, WIDE), F32),
-            shape((4,) + tiles, BF16),
+            shape((5,) + tiles, BF16),
             shape((4,) + tiles, BF16),
             shape((2, 4) + head, BF16),
         ],

time: 345 us -> 328 us (0.951)
  Pallas kernels: 324 us -> 307 us
    pallas_call x1, Pallas kernels: 324 us -> 307 us  [run_layer(): pl.pallas_call(layer_kernel, out_shape=[shape((3, rows, 5 * TILE), BF16),...]
where the time goes in v4:
time: 328 us; the launch traced here: 327 us
  Pallas kernels  307 us (94%)
  local copies, waits for them, and re-layouts  11 us (3%)
  other arithmetic  8.17 us (2%)
    pallas_call x1, Pallas kernels, run_layer(): pl.pallas_call(layer_kernel, out_shape=[shape((3, rows, 5 * TILE), BF16),...  307 us

profile of v4, /device:TPU:4, one launch (start us, length us, event | category | flops | bytes accessed | tf_op | source)
XLA Modules:
  0.0 327.3 jit_solution(14762812022925473)
XLA Ops:
  0.6 0.0 copy-start.1
  0.7 0.0 copy-start.2
  0.7 0.8 stack.25
  1.4 0.7 stack.26
  2.1 0.6 fusion.11.gains
  2.7 0.8 copy.21
  3.6 2.0 fusion.4.wat
  5.6 1.1 pad_bitcast_fusion.2
  6.7 0.0 copy-done.1
  6.7 0.0 copy-done.2
  6.7 0.1 pad_bitcast_fusion
  6.8 1.4 pad_maximum_fusion.wff
  8.3 307.4 %layer.1 = (bf16[3,448,640]{2,1,0:T(8,128)(2,1)}, bf16[2,256,512]{2,1,0:T(8,128)(2,1)}, bf16[448,512]{1,0:T(8,128)(2,1)}, bf16[448,512]{1,0:T(8,128)(2,1)}, f32[...) custom-call(bf16[3,448,640]{2,1,0:T(8,128)(2,1)} %pad_maximum_fusion, ...), custom_call_target="tpu_custom_call" | custom-call | tf_op jit(solution)/shard_map/layer/pallas_call | solution.py:1573
  315.7 0.0 copy-start.4
  315.7 1.3 sqrt_bitcast_fusion
  317.0 1.4 fusion.12
  318.4 0.9 slice.37
  319.3 0.7 copy.22
  319.9 0.0 copy-start
  319.9 1.9 slice.38
  321.8 1.8 slice.36
  323.7 0.0 copy-done.4
  323.7 1.0 convert_element_type.34
  324.7 0.0 copy-done
  324.7 0.0 copy-start.3
  324.7 1.8 bitcast_convert_fusion
  326.6 0.0 copy-done.3
  326.6 0.8 copy.24
Async XLA Ops:
  0.6 6.0 %copy-start.1 = (bf16[448,608]{1,0:T(8,128)(2,1)S(1)}, bf16[448,608]{1,0:T(8,128)(2,1)}, u32[]{:S(2)}) copy-start(bf16[448,608]{1,0:T(8,128)(2,1)} %param.19) | copy-start | bytes 1634308
  0.7 6.0 %copy-start.2 = (bf16[448,608]{1,0:T(8,128)(2,1)S(1)}, bf16[448,608]{1,0:T(8,128)(2,1)}, u32[]{:S(2)}) copy-start(bf16[448,608]{1,0:T(8,128)(2,1)} %param.18) | copy-start | bytes 1634308
  315.7 8.0 %copy-start.4 = (bf16[448,512]{1,0:T(8,128)(2,1)S(1)}, bf16[448,512]{1,0:T(8,128)(2,1)}, u32[]{:S(2)}) copy-start(bf16[448,512]{1,0:T(8,128)(2,1)} %get-tuple-element.17) | copy-start | bytes 1376260
  319.9 4.8 %copy-start = (bf16[3,448,640]{2,1,0:T(8,128)(2,1)S(1)}, bf16[3,448,640]{2,1,0:T(8,128)(2,1)}, u32[]{:S(2)}) copy-start(bf16[3,448,640]{2,1,0:T(8,128)(2,1)} %get-tuple-element.19) | copy-start | bytes 5160964
  324.7 1.8 copy-start.3

commit v5 on v4

--- a/solution.py
+++ b/solution.py
@@ -1,3 +1,5 @@
+import functools
+
 import jax
 import jax.numpy as jnp
 from jax import lax
@@ -361,7 +363,7 @@
 TILE = 128
 WIDE = 512
 SPAN = 256
-MARKS = 320
+MARKS = 420
 MESH = pl.DeviceIdType.MESH
 ANY = pl.BlockSpec(memory_space=pl.ANY)
 F32, BF16 = jnp.float32, jnp.bfloat16
@@ -485,7 +487,7 @@
         self.arrived = marks.one()
         inner = is_inner(plane)
         self.mine = plane == owner
-        self.mine_inner = self.mine & inner
+        self.mine_inner, self.mine_outer = self.mine & inner, self.mine & no(inner)
         self.from_end = inner & (plane == away(owner, 1))
         self.from_inner = inner & (plane == away(owner, 3))
         self.from_far = inner & (plane == away(owner, 2))
@@ -499,8 +501,13 @@
         )
 
     def start(self):
-        pl.when(self.mine)(lambda: self.copy(1, 0).start())
-        pl.when(self.mine_inner)(lambda: self.copy(3, 1).start())
+        pl.when(self.mine_outer)(lambda: self.copy(1, 0).start())
+
+    def start_inner(self):
+        @pl.when(self.mine_inner)
+        def _():
+            self.copy(3, 1).start()
+            self.copy(1, 0).start()
 
     def relay(self):
         pl.when(self.from_end | self.from_inner)(lambda: self.copy(1, 0).wait_recv())
@@ -666,11 +673,12 @@
 
 
 def layer_kernel(
-    wff, wat, tok, cot, gains,
+    w_gate, w_up, w_down, w_qkv, w_out, conv, gain_mix, gain_ffn, tok, cot,
     out_ff, out_at, out_res, out_tok, out_small, main_got, extra_got, att_got,
     ff, at, xs, gs, low2, part, acc3, gout, gat, from_mate, both, got, turned, hid, gg,
     gn, gcol, raw, qs, ks, vs, att, gatt, gproj, mid, gmid, gsum, normed, sending, inv_all,
-    inv_sum, small, small_a, small_b, sem, free_mate, free_chips,
+    inv_sum, small, small_a, small_b, raw_ff, raw_qkv, raw_out, raw_conv, tapped, last_tile, wat,
+    gains, gain_rows, sem, free_mate, free_chips,
 ):
     chip, plane, core = place()
     others = other_chips(chip)
@@ -691,50 +699,118 @@
     partners = peers + [mate] + sides + line + line_mates
     for partner in partners:
         pl.semaphore_signal(barrier, inc=1, device_id=partner, device_id_type=MESH)
-    pl.semaphore_wait(barrier, len(partners))
 
     def block_rows(c):
         return rows_at(c * rows, rows, rows)
+
+    ffn_weights = (w_gate, w_up, w_down)
+    ffn_cols = w_gate.shape[1]
+    early = marks.many(8)
+    loads = [
+        pltpu.make_async_copy(source, target, early(i))
+        for i, (source, target) in enumerate(
+            (
+                (w_qkv, raw_qkv), (w_out, raw_out), (conv, raw_conv),
+                (gain_mix, gain_rows[0]), (gain_ffn, gain_rows[1]),
+            )
+        )
+    ]
+    ffn_loads = [
+        pltpu.make_async_copy(ffn_weights[m], raw_ff.at[m], early(5 + m)) for m in range(3)
+    ]
+    for load in loads + ffn_loads:
+        load.start()
+    for load in loads:
+        load.wait()
+    for i in range(2):
+        gains[i] = gain_rows[i][...].reshape(1, rows)
+    tapped[...] = jnp.zeros(tapped.shape, F32)
+    tapped[0:CONV, 0 : 2 * HDIM] = raw_conv[...].astype(F32)
+    tap_rows = tapped[...].T
+    tail = lax.broadcasted_iota(jnp.int32, (HDIM, TILE), 1)
+    spare = rows % TILE
+    for h in range(2):
+        wat[h, :HEADROWS, :rows] = raw_qkv[h * HEADROWS : (h + 1) * HEADROWS]
+        wat[h, HEADROWS:, :rows] = raw_out[h * HDIM : (h + 1) * HDIM]
+        columns = wat[h, 2 * FEAT : HEADROWS, WIDE - TILE :].astype(F32)
+        for j in range(CONV):
+            column = tap_rows[h * HDIM : (h + 1) * HDIM, j : j + 1]
+            columns = jnp.where(tail == spare + j, column, columns)
+        wat[h, 2 * FEAT : HEADROWS, WIDE - TILE :] = columns.astype(BF16)
+    for load in ffn_loads:
+        load.wait()
+    short = ffn_cols - 4 * TILE
+    for m in range(3):
+        last_tile[m, :, 0:short] = raw_ff[m, :, 4 * TILE :]
+        last_tile[m, :, short:] = jnp.zeros((rows, TILE - short), BF16)
+
+    pl.semaphore_wait(barrier, len(partners))
 
     far_core = plane // 2
     holds_att = core == far_core
     holds_extra = holds_att & (chip // 2 == plane % 2)
     extra_plane = 2 * core + chip // 2
     extra_chip = (plane % 2) * 2 + core
-    att_send, att_here = marks.many(2), marks.many(4)
-    att_local = marks.one()
-
-    def att_copy(h):
-        return remote(
-            wat.at[h], at.at[plane % 2, chip], att_send(h), att_here(chip),
-            device(2 * core + h, plane, far_core),
-        )
-
-    def att_keep(h):
-        return pltpu.make_async_copy(wat.at[h], at.at[plane % 2, chip], att_local)
-
+    out_rows, in_rows = pl.ds(HEADROWS, HDIM), pl.ds(0, HEADROWS)
     att_self = [(2 * core + h == chip) & holds_att for h in range(2)]
-    for h in range(2):
-
-        @pl.when(att_self[h])
-        def _():
-            att_keep(h).start()
-
-        @pl.when(no(att_self[h]))
-        def _():
-            att_copy(h).start()
+
+    class Heads:
+        def __init__(self, span):
+            self.span, self.local = span, marks.one()
+            self.send, self.here = marks.many(2), marks.many(4)
+
+        def copy(self, h):
+            return remote(
+                wat.at[h, self.span], at.at[plane % 2, chip, self.span], self.send(h),
+                self.here(chip), device(2 * core + h, plane, far_core),
+            )
+
+        def keep(self, h):
+            return pltpu.make_async_copy(
+                wat.at[h, self.span], at.at[plane % 2, chip, self.span], self.local
+            )
+
+        def start(self):
+            for h in range(2):
+                pl.when(att_self[h])(lambda: self.keep(h).start())
+                pl.when(no(att_self[h]))(lambda: self.copy(h).start())
+
+        def arrive(self):
+            for h in range(2):
+                pl.when(att_self[h])(lambda: self.keep(h).wait())
+
+            for c in range(4):
+
+                @pl.when(holds_att & no((c == chip) & (core == chip // 2)))
+                def _():
+                    remote(
+                        wat.at[0, self.span], at.at[plane % 2, c, self.span], self.send(0),
+                        self.here(c), mate,
+                    ).wait_recv()
+
+        def finish(self):
+            for h in range(2):
+                pl.when(no(att_self[h]))(lambda: self.copy(h).wait_send())
+
+    heads_in, heads_out = Heads(in_rows), Heads(out_rows)
+    heads_in.start()
+    heads_out.start()
 
     class Gather:
         def __init__(self, source, target_of):
             self.source, self.target_of = source, target_of
-            self.send, self.here = marks.many(4), marks.many(4)
+            self.send, self.here = marks.many(6), marks.many(6)
             self.mate_send, self.mate_here = marks.many(4), marks.many(4)
             self.keep = pltpu.make_async_copy(source, target_of(chip), marks.one())
-            self.copies = [
-                remote(source, target_of(chip), self.send(p), self.here(p), peers[p])
-                for p in range(2)
-            ]
-            for copy in self.copies:
+            mine = self.halves(source)
+            there = self.halves(target_of(chip))
+            self.copies = {
+                mark: remote(
+                    mine[half], there[half], self.send(mark), self.here(mark), peers[p]
+                )
+                for mark, half, p in ((0, 0, 0), (3, 1, 1), (1, 1, 0), (2, 0, 1))
+            }
+            for copy in self.copies.values():
                 copy.start()
             self.keep.start()
             self.crossing = []
@@ -747,33 +823,32 @@
             copy.start()
             self.crossing.append(copy)
 
-        def halves(self, c):
-            block = self.target_of(c)
+        def halves(self, block):
             size = block.shape[0] // 2
             return block.at[0:size], block.at[size : 2 * size]
 
         def pass_on(self):
-            self.copies[0].wait_recv()
-            part_a = self.halves(others[0])[0]
-            self.copies.append(remote(part_a, part_a, self.send(2), self.here(2), peers[1]))
-            self.copies[2].start()
-            self.cross(self.target_of(others[0]), others[0], 0)
-            self.copies[1].wait_recv()
-            part_b = self.halves(others[1])[1]
-            self.copies.append(remote(part_b, part_b, self.send(3), self.here(3), peers[0]))
-            self.copies[3].start()
-            self.cross(self.target_of(others[1]), others[1], 1)
+            for mark, half, p, onward in ((0, 0, 0, 4), (3, 1, 1, 5)):
+                self.copies[mark].wait_recv()
+                block = self.halves(self.target_of(others[p]))[half]
+                self.copies[onward] = remote(
+                    block, block, self.send(onward), self.here(onward), peers[1 - p]
+                )
+                self.copies[onward].start()
+            for mark, p in ((1, 0), (2, 1)):
+                self.copies[mark].wait_recv()
+                self.cross(self.target_of(others[p]), others[p], p)
 
         def arrive(self):
-            for copy in self.copies[2:]:
-                copy.wait_recv()
+            for mark in (4, 5):
+                self.copies[mark].wait_recv()
             self.cross(self.target_of(others[2]), others[2], 2)
             for copy in self.crossing:
                 copy.wait_recv()
             self.keep.wait()
 
         def finish(self):
-            for copy in self.copies + self.crossing:
+            for copy in list(self.copies.values()) + self.crossing:
                 copy.wait_send()
 
     tokens_in = Gather(tok, lambda c: xs.at[block_rows(c), own_half])
@@ -785,25 +860,6 @@
     for copy in gain_copies + [gain_keep]:
         copy.start()
 
-    for h in range(2):
-
-        @pl.when(att_self[h])
-        def _():
-            att_keep(h).wait()
-
-        @pl.when(no(att_self[h]))
-        def _():
-            att_copy(h).wait_send()
-
-    for c in range(4):
-
-        @pl.when(holds_att & no((c == chip) & (core == chip // 2)))
-        def _():
-            remote(
-                wat.at[0], at.at[plane % 2, c], att_send(0), att_here(c), mate
-            ).wait_recv()
-
-    out_rows, in_rows = pl.ds(HEADROWS, HDIM), pl.ds(0, HEADROWS)
     in_line, out_line = [
         [
             Spread(at.at[a, :, span], 2 * core + a, chip, plane, core, marks)
@@ -811,23 +867,34 @@
         ]
         for span in (in_rows, out_rows)
     ]
-    for item in in_line + out_line:
+    heads_in.arrive()
+    for item in in_line:
         item.start()
+    heads_out.arrive()
+    for item in out_line:
+        item.start()
+    heads_in.finish()
+    heads_out.finish()
 
     tokens_in.pass_on()
-    main_send, main_here, main_local = marks.many(3), marks.many(3), marks.one()
-    main_here_at = ff.at[:, block_rows(chip), lanes(plane * TILE)]
+    main_send, main_here, main_local = marks.many(9), marks.many(9), marks.many(3)
+    main_here_at = [ff.at[m, block_rows(chip), lanes(plane * TILE)] for m in range(3)]
     mains = [
         remote(
-            wff.at[:, :, lanes(others[p] * TILE)], main_here_at,
-            main_send(p), main_here(p), peers[p],
+            ffn_weights[m].at[:, lanes(others[p] * TILE)], main_here_at[m],
+            main_send(3 * p + m), main_here(3 * p + m), peers[p],
         )
         for p in range(3)
+        for m in range(3)
+    ]
+    mains += [
+        pltpu.make_async_copy(
+            ffn_weights[m].at[:, lanes(chip * TILE)], main_here_at[m], main_local(m)
+        )
+        for m in range(3)
     ]
     for copy in mains:
         copy.start()
-    main_keep = pltpu.make_async_copy(wff.at[:, :, lanes(chip * TILE)], main_here_at, main_local)
-    main_keep.start()
 
     extra_send, extra_here, extra_local = marks.one(), marks.many(4), marks.one()
     extra_self = (extra_chip == chip) & holds_att
@@ -835,13 +902,13 @@
 
     def extra_copy():
         return remote(
-            wff.at[:, :, last], ff.at[:, block_rows(chip), last], extra_send, extra_here(chip),
+            last_tile, ff.at[:, block_rows(chip), last], extra_send, extra_here(chip),
             device(extra_chip, plane, far_core),
         )
 
     def extra_keep():
         return pltpu.make_async_copy(
-            wff.at[:, :, last], ff.at[:, block_rows(chip), last], extra_local
+            last_tile, ff.at[:, block_rows(chip), last], extra_local
         )
 
     @pl.when(extra_self)
@@ -852,17 +919,21 @@
     def _():
         extra_copy().start()
 
+    for item in in_line:
+        item.relay()
     tokens_in.arrive()
     cot_in = Gather(cot, lambda c: gs.at[block_rows(c), own_half])
     for copy in gain_copies + [gain_keep]:
         copy.wait()
 
-    for item in in_line:
+    for item in out_line:
         item.relay()
     @pl.loop(0, 4)
     def _(c):
-        columns = gn[c].astype(F32).T
-        gcol[block_rows(c), 0:16] = columns[:rows]
+        pair = jnp.concatenate(
+            [gn[c, 0].astype(F32), gn[c, 1].astype(F32), jnp.zeros((6, rows), F32)], 0
+        )
+        gcol[block_rows(c), 0:8] = pair.T
 
     step_rows = 64
 
@@ -882,13 +953,10 @@
             xs[at_rows].astype(F32) * inv_all[...] * gcol[at_rows, 0:1]
         ).astype(BF16)
 
-    for item in out_line:
-        item.relay()
     for item in in_line:
         item.arrive()
 
     position = lax.broadcasted_iota(jnp.int32, (1, seq), 1)
-    tail = lax.broadcasted_iota(jnp.int32, (HDIM, TILE), 1)
 
     def taps(h):
         columns = at[h, 0, 2 * FEAT : HEADROWS, WIDE - TILE : WIDE].astype(F32)
@@ -929,7 +997,6 @@
             weights = (kernel * inverse).astype(BF16)
             att[h, :, b * SPAN : seen] = dot(vs[h, :, :seen], weights, 1, 0).astype(BF16)
 
-    main_keep.wait()
     for copy in mains:
         copy.wait()
     main_line = MainTiles(ff, chip, plane, core, marks)
@@ -948,14 +1015,12 @@
         @pl.when(holds_extra & no((c == chip) & (core == chip % 2)))
         def _():
             remote(
-                wff.at[:, :, last], ff.at[:, block_rows(c), last], extra_send, extra_here(c), mate
+                last_tile, ff.at[:, block_rows(c), last], extra_send, extra_here(c), mate
             ).wait_recv()
 
     extra_line = Chain(ff.at[:, :, last], extra_plane, chip, plane, core, marks)
     extra_line.start()
 
-    cot_in.pass_on()
-
     for item in out_line:
         item.arrive()
 
@@ -963,66 +1028,82 @@
         return got.at[i]
 
     class Sum:
-        def __init__(self, guard, both=both, got=None, share=True):
-            self.guard, self.both, self.share = guard, both, share
+        def __init__(self, guard, both=both, got=None, share=True, at_once=True):
+            self.guard, self.both, self.share, self.at_once = guard, both, share, at_once
             self.got = got or default_got
 
         def begin(self, fill):
             fill((1 - core) * half)
-            self.to_mate = remote(
-                part.at[:, lanes((1 - core) * half, half)], from_mate,
-                marks.one(), marks.one(), mate,
-            )
+            send, here = marks.many(4), marks.many(4)
+            self.order = (others[2], others[0], others[1], chip)
+            self.to_mate = [
+                remote(
+                    part.at[:, lanes((1 - core) * half + c * TILE)],
+                    from_mate.at[:, lanes(c * TILE)], send(i), here(i), mate,
+                )
+                for i, c in enumerate(self.order)
+            ]
             if self.guard:
                 pl.semaphore_wait(free_mate, 1)
-            self.to_mate.start()
+            for copy in self.to_mate:
+                copy.start()
             fill(core * half)
 
         def combine(self):
-            self.to_mate.wait_recv()
-
-            @pl.loop(0, 4)
-            def _(c):
-                self.both[block_rows(c)] = (
-                    part[block_rows(c), own_half].astype(F32)
-                    + from_mate[block_rows(c)].astype(F32)
-                ).astype(BF16)
-
+            self.prepare()
+            for i, c in enumerate(self.order):
+                self.to_mate[i].wait_recv()
+                where, own = lanes(c * TILE), lanes(core * half + c * TILE)
+
+                @pl.loop(0, 4)
+                def _(b):
+                    at_rows = block_rows(b)
+                    self.both[at_rows, where] = (
+                        part[at_rows, own].astype(F32) + from_mate[at_rows, where].astype(F32)
+                    ).astype(BF16)
+
+                if self.at_once:
+                    self.send(i)
             pl.semaphore_signal(free_mate, inc=1, device_id=mate, device_id_type=MESH)
-            self.to_mate.wait_send()
+            for copy in self.to_mate:
+                copy.wait_send()
 
         def piece(self, upper, c):
             size = width // 2
             return self.both.at[pl.ds(0 if upper else size, size), lanes(c * TILE)]
 
-        def send(self):
-            if self.guard and self.share:
-                pl.semaphore_wait(free_chips, 2)
+        def prepare(self):
             size = width // 2
             top, bottom = pl.ds(0, size), pl.ds(size, size)
             send, here = marks.many(6), marks.many(6)
+            x, y, across = others
             self.across = [
-                remote(self.piece(True, others[2]), self.got(2).at[top], send(0), here(0), peers[0]),
+                remote(self.piece(True, across), self.got(2).at[top], send(0), here(0), peers[0]),
                 remote(
-                    self.piece(False, others[2]), self.got(2).at[bottom], send(1), here(1), peers[1]
+                    self.piece(False, across), self.got(2).at[bottom], send(1), here(1), peers[1]
                 ),
             ]
             self.plain = [
-                remote(self.piece(True, others[0]), self.got(0).at[top], send(2), here(2), peers[0]),
-                remote(
-                    self.piece(False, others[1]), self.got(1).at[bottom], send(3), here(3), peers[1]
-                ),
+                remote(self.piece(True, x), self.got(0).at[top], send(2), here(2), peers[0]),
+                remote(self.piece(False, y), self.got(1).at[bottom], send(3), here(3), peers[1]),
             ]
             self.added = [
-                remote(
-                    self.piece(True, others[1]), self.got(1).at[top], send(4), here(4), peers[1]
-                ),
-                remote(
-                    self.piece(False, others[0]), self.got(0).at[bottom], send(5), here(5), peers[0]
-                ),
+                remote(self.piece(True, y), self.got(1).at[top], send(4), here(4), peers[1]),
+                remote(self.piece(False, x), self.got(0).at[bottom], send(5), here(5), peers[0]),
             ]
-            for copy in self.across + self.plain:
-                copy.start()
+
+        def send(self, i):
+            if i == 0:
+                if self.guard and self.share:
+                    pl.semaphore_wait(free_chips, 2)
+                for copy in self.across:
+                    copy.start()
+            elif i < 3:
+                self.plain[i - 1].start()
+
+        def send_all(self):
+            for i in range(3):
+                self.send(i)
 
         def pass_on(self):
             size = width // 2
@@ -1074,12 +1155,13 @@
 
     branch_sum = Sum(guard=False)
     branch_sum.begin(fill_branch)
+    cot_in.pass_on()
     cot_in.arrive()
     branch_sum.combine()
-    branch_sum.send()
     branch_sum.pass_on()
+    main_line.relay()
+    extra_line.start_inner()
     branch_sum.finish(store_branch)
-    main_line.relay()
     middle = mid[...]
     inverse_two = lax.rsqrt(jnp.sum(middle * middle, 0, keepdims=True) / D + EPSILON)
 
@@ -1102,8 +1184,8 @@
     low_in.arrive()
     low_in.finish()
 
+    main_line.relay_far()
     extra_line.relay()
-    main_line.relay_far()
     def feed(slot):
         where = lanes(slot * TILE)
         unit_rows = rows_at(slot * TILE, TILE, TILE)
@@ -1204,7 +1286,6 @@
     two_sum = Sum(guard=True)
     two_sum.begin(fill_grad_two)
     two_sum.combine()
-    two_sum.send()
     two_sum.pass_on()
 
     def fill_ffn(start):
@@ -1218,6 +1299,7 @@
     ffn_sum = Sum(
         guard=True, both=ff.at[1, :, lanes(0, half)],
         got=lambda i: ff.at[0, :, lanes(i * TILE)], share=False,
+        at_once=False,
     )
     ffn_sum.begin(fill_ffn)
     two_sum.finish(store_gsum)
@@ -1259,7 +1341,7 @@
     gain_two_back()
     ffn_sum.combine()
     mid_in.pass_on()
-    ffn_sum.send()
+    ffn_sum.send_all()
     mid_in.arrive()
 
     @pl.loop(0, 2)
@@ -1356,7 +1438,6 @@
     one_sum = Sum(guard=True)
     one_sum.begin(fill_grad_one)
     one_sum.combine()
-    one_sum.send()
     extra_back.relay(add_extra)
 
     def store_result(at_rows, total):
@@ -1490,30 +1571,50 @@
     for items, start, size in ((out_back, HEADROWS, HDIM), (in_back, 0, HEADROWS)):
         for a in range(2):
             items[a].relay(add_head(a, start, size))
+    class HeadsBack:
+        def __init__(self, span):
+            self.span, self.local = span, marks.one()
+            self.send, self.here = marks.many(4), marks.many(2)
+
+        def same(self, c):
+            return (c == chip) & (core == chip // 2)
+
+        def copy(self, c):
+            return remote(
+                gat.at[plane % 2, c, self.span], out_at.at[chip % 2, self.span], self.send(c),
+                self.here(chip % 2), device(c, plane, chip // 2),
+            )
+
+        def keep(self):
+            return pltpu.make_async_copy(
+                gat.at[plane % 2, chip, self.span], out_at.at[chip % 2, self.span], self.local
+            )
+
+        def start(self):
+            for c in range(4):
+                pl.when(holds_att & self.same(c))(lambda: self.keep().start())
+                pl.when(holds_att & no(self.same(c)))(lambda: self.copy(c).start())
+
+        def finish(self):
+            for c in range(4):
+                pl.when(holds_att & self.same(c))(lambda: self.keep().wait())
+                pl.when(holds_att & no(self.same(c)))(lambda: self.copy(c).wait_send())
+
+            for h in range(2):
+
+                @pl.when(no(att_self[h]))
+                def _():
+                    remote(
+                        gat.at[0, 0, self.span], out_at.at[h, self.span], self.send(0),
+                        self.here(h), mate,
+                    ).wait_recv()
+
+    heads_back = []
     for items, start, size in ((out_back, HEADROWS, HDIM), (in_back, 0, HEADROWS)):
         for a in range(2):
             items[a].total(add_head(a, start, size))
-    head_send, head_here, head_local = marks.many(4), marks.many(2), marks.one()
-
-    def head_copy(c):
-        return remote(
-            gat.at[plane % 2, c], out_at.at[chip % 2], head_send(c), head_here(chip % 2),
-            device(c, plane, chip // 2),
-        )
-
-    def head_keep():
-        return pltpu.make_async_copy(gat.at[plane % 2, chip], out_at.at[chip % 2], head_local)
-
-    for c in range(4):
-        same = (c == chip) & (core == chip // 2)
-
-        @pl.when(holds_att & same)
-        def _():
-            head_keep().start()
-
-        @pl.when(holds_att & no(same))
-        def _():
-            head_copy(c).start()
+        heads_back.append(HeadsBack(pl.ds(start, size)))
+        heads_back[-1].start()
 
     for copy in seven:
         copy.wait()
@@ -1529,30 +1630,16 @@
     for copy in pending:
         copy.wait()
     for c in range(4):
-        for holds, same, local, away_copy in (
-            (holds_extra, (c == chip) & (core == chip % 2), last_keep, last_copy),
-            (holds_att, (c == chip) & (core == chip // 2), head_keep, head_copy),
-        ):
-
-            @pl.when(holds & same)
-            def _():
-                local().wait()
-
-            @pl.when(holds & no(same))
-            def _():
-                away_copy(c).wait_send()
+        same = (c == chip) & (core == chip % 2)
+        pl.when(holds_extra & same)(lambda: last_keep().wait())
+        pl.when(holds_extra & no(same))(lambda: last_copy(c).wait_send())
 
     @pl.when(no(extra_self))
     def _():
         last_copy(0).wait_recv()
 
-    for h in range(2):
-
-        @pl.when(no(att_self[h]))
-        def _():
-            remote(
-                gat.at[0, 0], out_at.at[h], head_send(0), head_here(h), mate
-            ).wait_recv()
+    for item in heads_back:
+        item.finish()
 
     pl.semaphore_wait(free_mate, 1)
     pl.semaphore_wait(free_chips, 2)
@@ -1563,7 +1650,7 @@
     return pltpu.SemaphoreType.DMA(shape)
 
 
-def run_layer(wff, wat, tok, cot, gains):
+def run_layer(w_gate, w_up, w_down, w_qkv, w_out, conv, gain_mix, gain_ffn, tok, cot):
     rows, half = tok.shape
     width, seq = 4 * rows, 2 * half
     shape = jax.ShapeDtypeStruct
@@ -1582,7 +1669,7 @@
             shape((4,) + tiles, BF16),
             shape((2, 4) + head, BF16),
         ],
-        in_specs=[ANY] * 5,
+        in_specs=[ANY] * 10,
         out_specs=[ANY] * 8,
         scratch_shapes=[
             vmem((3, width, 5 * TILE), BF16),
@@ -1600,7 +1687,7 @@
             vmem((3 * TILE, width), BF16),
             vmem((5 * TILE, seq), BF16),
             vmem((2 * TILE, seq), BF16),
-            vmem((4, 16, WIDE), BF16),
+            vmem((4, 2, 1, rows), BF16),
             vmem((width, TILE), F32),
             vmem((2, HDIM, seq), F32),
             vmem((2, FEAT, seq), BF16),
@@ -1619,6 +1706,15 @@
             vmem((4, 8, WIDE), F32),
             vmem((3, 8, WIDE), F32),
             vmem((8, 8, WIDE), F32),
+            vmem((3,) + w_gate.shape, BF16),
+            vmem(w_qkv.shape, BF16),
+            vmem(w_out.shape, BF16),
+            vmem(conv.shape, BF16),
+            vmem((8, 2 * TILE), F32),
+            vmem((3, rows, TILE), BF16),
+            vmem((2, BLOCKROWS, WIDE), BF16),
+            vmem((2, 1, rows), BF16),
+            [vmem((rows,), BF16)] * 2,
             dma(MARKS),
             pltpu.SemaphoreType.REGULAR,
             pltpu.SemaphoreType.REGULAR,
@@ -1627,7 +1723,81 @@
             collective_id=0, has_side_effects=True, vmem_limit_bytes=63 * 2**20
         ),
         name="layer",
-    )(wff, wat, tok, cot, gains)
+    )(w_gate, w_up, w_down, w_qkv, w_out, conv, gain_mix, gain_ffn, tok, cot)
+
+
+def outputs_kernel(
+    count, ff, at, tok, small, to_tok, to_qkv, to_conv, to_out, to_gate, to_up, to_down,
+    to_mix, to_ffn, to_rms, ff_in, at_in, tok_in, small_in, tok_out, qkv_out, conv_out, out_out,
+    ff_out, rms_out, sem,
+):
+    rows, cols = to_gate.shape
+    marks = Marks(sem)
+    loads = [
+        pltpu.make_async_copy(source, target, marks.one())
+        for source, target in (
+            [(tok, tok_in), (at, at_in)] + [(ff.at[m], ff_in.at[m]) for m in range(3)]
+            + [(small, small_in)]
+        )
+    ]
+    for load in loads:
+        load.start()
+    stores = []
+
+    def store(source, target):
+        stores.append(pltpu.make_async_copy(source, target, marks.one()))
+        stores[-1].start()
+
+    loads[0].wait()
+    tok_out[...] = tok_in[...].astype(F32)
+    store(tok_out, to_tok)
+    loads[1].wait()
+    for h in range(2):
+        qkv_out[h * HEADROWS : (h + 1) * HEADROWS] = at_in[h, :HEADROWS, :rows].astype(F32)
+        out_out[h * HDIM : (h + 1) * HDIM] = at_in[h, HEADROWS:, :rows].astype(F32)
+    store(qkv_out, to_qkv)
+    store(out_out, to_out)
+    taps = jnp.concatenate(
+        [at_in[h, 2 * FEAT : HEADROWS, WIDE - TILE :].astype(F32) for h in range(2)], 0
+    )
+    conv_out[...] = taps.T[rows % TILE : rows % TILE + CONV]
+    store(conv_out, to_conv)
+    for m, target in enumerate((to_gate, to_up, to_down)):
+        loads[2 + m].wait()
+        ff_out[m] = ff_in[m, :, :cols].astype(F32)
+        store(ff_out.at[m], target)
+    loads[5].wait()
+    rms_out[0] = small_in[0:1, :rows]
+    rms_out[1] = small_in[1:2, :rows]
+    rms_out[2] = jnp.sqrt(small_in[2:3, :rows] / count)
+    for i, target in enumerate((to_mix, to_ffn, to_rms)):
+        store(rms_out.at[i], target)
+    for copy in stores:
+        copy.wait()
+
+
+def outputs(ff, at, tok, small, ffn_cols, count):
+    rows, half = tok.shape
+    shape = jax.ShapeDtypeStruct
+    shapes = [
+        (rows, half), (2 * HEADROWS, rows), (CONV, 2 * HDIM), (2 * HDIM, rows),
+        (rows, ffn_cols), (rows, ffn_cols), (rows, ffn_cols), (1, rows), (1, rows), (1, rows),
+    ]
+    vmem = pltpu.VMEM
+    return pl.pallas_call(
+        functools.partial(outputs_kernel, count),
+        out_shape=[shape(s, F32) for s in shapes],
+        in_specs=[ANY] * 4,
+        out_specs=[ANY] * 10,
+        scratch_shapes=[
+            vmem(ff.shape, BF16), vmem(at.shape, BF16), vmem(tok.shape, BF16),
+            vmem(small.shape, F32), vmem(shapes[0], F32), vmem(shapes[1], F32),
+            vmem(shapes[2], F32), vmem(shapes[3], F32), vmem((3,) + shapes[4], F32),
+            vmem((3,) + shapes[7], F32), dma(24),
+        ],
+        compiler_params=pltpu.CompilerParams(vmem_limit_bytes=60 * 2**20),
+        name="outputs",
+    )(ff, at, tok, small)
 
 
 def on_device_full(
@@ -1635,33 +1805,15 @@
 ):
     rows, half = tokens.shape
     ffn_cols = w_gate.shape[1]
-    heads = 2
-    pad = ((0, 0), (0, 5 * TILE - ffn_cols))
-    wff = jnp.stack([jnp.pad(w, pad) for w in (w_gate, w_up, w_down)])
-    taps = jnp.pad(
-        conv_weight.T.reshape(heads, HDIM, CONV),
-        ((0, 0), (2 * FEAT, 0), (0, WIDE - rows - CONV)),
-    )
-    upper = jnp.concatenate([w_qkv.T.reshape(heads, HEADROWS, rows), taps], 2)
-    lower = jnp.pad(w_out.reshape(heads, HDIM, rows), ((0, 0), (0, 0), (0, WIDE - rows)))
-    wat = jnp.concatenate([upper, lower], 1)
-    gains = jnp.pad(
-        jnp.stack([gain_mix, gain_ffn]), ((0, 14), (0, WIDE - rows))
-    )
-    out_ff, out_at, out_res, out_tok, small = run_layer(wff, wat, tokens, cotangent, gains)[:5]
-    out_at = out_at.astype(F32)
+    out_ff, out_at, out_res, out_tok, small = run_layer(
+        w_gate, w_up, w_down, w_qkv.T, w_out, conv_weight, gain_mix, gain_ffn,
+        tokens, cotangent,
+    )[:5]
+    grads = outputs(out_ff, out_at, out_tok, small, ffn_cols, 8 * half * 4 * rows)
+    to_tok, to_qkv, to_conv, to_out, to_gate, to_up, to_down, to_mix, to_ffn, to_rms = grads
     return (
-        out_res,
-        out_tok.astype(F32),
-        out_at[:, :HEADROWS, :rows].reshape(heads * HEADROWS, rows).T,
-        out_at[:, 2 * FEAT : HEADROWS, rows : rows + CONV].reshape(heads * HDIM, CONV).T,
-        out_at[:, HEADROWS:, :rows].reshape(heads * HDIM, rows),
-        out_ff[0, :, :ffn_cols].astype(F32),
-        out_ff[1, :, :ffn_cols].astype(F32),
-        out_ff[2, :, :ffn_cols].astype(F32),
-        small[0, :rows],
-        small[1, :rows],
-        jnp.sqrt(small[2, :3] / (8 * half * 4 * rows)),
+        out_res, to_tok, to_qkv.T, to_conv, to_out, to_gate, to_up, to_down,
+        to_mix[0], to_ffn[0], to_rms[0, :3],
     )
 
 

time: 328 us -> 301 us (0.918)
  Pallas kernels: 307 us -> 296 us
  local copies, waits for them, and re-layouts: 11 us -> 1.94 us
  other arithmetic: 8.17 us -> 0 us
    pallas_call x1, Pallas kernels: 307 us -> 292 us  [run_layer(): pl.pallas_call(layer_kernel, out_shape=[shape((3, rows, 5 * TILE), BF16),...]
    slice x4 -> x0, local copies, waits for them, and re-layouts: 6.01 us -> none  [the longest x1 1.89 us: on_device_full(): out_at[:, HEADROWS:, :rows].reshape(heads * HDIM, rows)]
    pallas_call x0 -> x1, Pallas kernels: none -> 3.76 us  [outputs(): pl.pallas_call(functools.partial(outputs_kernel, count), out_shape=[shape...]
where the time goes in v5:
time: 301 us; the launch traced here: 298 us
  Pallas kernels  296 us (98%)
    pallas_call x1, Pallas kernels, run_layer(): pl.pallas_call(layer_kernel, out_shape=[shape((3, rows, 5 * TILE), BF16),...  292 us

profile of v5, /device:TPU:4, one launch (start us, length us, event | category | flops | bytes accessed | tf_op | source)
XLA Modules:
  0.0 298.5 jit_solution(14763961456613828423)
XLA Ops:
  0.6 292.1 %layer.1 = (bf16[3,448,640]{2,1,0:T(8,128)(2,1)}, bf16[2,256,512]{2,1,0:T(8,128)(2,1)}, bf16[448,512]{1,0:T(8,128)(2,1)}, bf16[448,512]{1,0:T(8,128)(2,1)}, f32[...) custom-call(bf16[448,608]{1,0:T(8,128)(2,1)} %w_gate.1, ...), custom_call_target="tpu_custom_call" | custom-call | tf_op jit(solution)/shard_map/layer/pallas_call | solution.py:1660
  292.8 0.0 copy-start
  292.8 3.8 %outputs.1 = (f32[448,512]{1,0:T(8,128)}, f32[288,448]{1,0:T(8,128)}, f32[3,224]{1,0:T(4,128)}, f32[224,448]{1,0:T(8,128)}, f32[448,608]{1,0:T(8,128)}, /*index=...) custom-call(bf16[3,448,640]{2,1,0:T(8,128)(2,1)} %get-tuple-element.27.ff, ...), custom_call_target="tpu_custom_call" | custom-call | tf_op jit(solution)/shard_map/outputs/pallas_call | solution.py:1787
  296.6 1.2 slice_bitcast_fusion
  297.7 0.0 copy-done
  297.7 0.8 copy.22
Async XLA Ops:
  292.8 4.9 %copy-start = (bf16[448,512]{1,0:T(8,128)(2,1)S(1)}, bf16[448,512]{1,0:T(8,128)(2,1)}, u32[]{:S(2)}) copy-start(bf16[448,512]{1,0:T(8,128)(2,1)} %get-tuple-element.52) | copy-start | bytes 1376260

commit v6 on v5

--- a/solution.py
+++ b/solution.py
@@ -363,7 +363,7 @@
 TILE = 128
 WIDE = 512
 SPAN = 256
-MARKS = 420
+MARKS = 292
 MESH = pl.DeviceIdType.MESH
 ANY = pl.BlockSpec(memory_space=pl.ANY)
 F32, BF16 = jnp.float32, jnp.bfloat16
@@ -674,11 +674,11 @@
 
 def layer_kernel(
     w_gate, w_up, w_down, w_qkv, w_out, conv, gain_mix, gain_ffn, tok, cot,
-    out_ff, out_at, out_res, out_tok, out_small, main_got, extra_got, att_got,
+    out_ff, out_at, out_res, out_tok, out_small, main_got, extra_got, att_got, tail_got,
     ff, at, xs, gs, low2, part, acc3, gout, gat, from_mate, both, got, turned, hid, gg,
     gn, gcol, raw, qs, ks, vs, att, gatt, gproj, mid, gmid, gsum, normed, sending, inv_all,
-    inv_sum, small, small_a, small_b, raw_ff, raw_qkv, raw_out, raw_conv, tapped, last_tile, wat,
-    gains, gain_rows, sem, free_mate, free_chips,
+    inv_sum, small, small_a, small_b, raw_ff, raw_qkv, raw_out, raw_conv, tapped,
+    gains, gain_rows, packed, packed_back, at_tail, gat_tail, sem, free_mate, free_chips,
 ):
     chip, plane, core = place()
     others = other_chips(chip)
@@ -705,7 +705,8 @@
 
     ffn_weights = (w_gate, w_up, w_down)
     ffn_cols = w_gate.shape[1]
-    early = marks.many(8)
+    wat, last_tile = gat.at[:, 0], packed_back.at[:, 0:rows]
+    early = marks.many(6)
     loads = [
         pltpu.make_async_copy(source, target, early(i))
         for i, (source, target) in enumerate(
@@ -715,10 +716,7 @@
             )
         )
     ]
-    ffn_loads = [
-        pltpu.make_async_copy(ffn_weights[m], raw_ff.at[m], early(5 + m)) for m in range(3)
-    ]
-    for load in loads + ffn_loads:
+    for load in loads:
         load.start()
     for load in loads:
         load.wait()
@@ -737,13 +735,6 @@
             column = tap_rows[h * HDIM : (h + 1) * HDIM, j : j + 1]
             columns = jnp.where(tail == spare + j, column, columns)
         wat[h, 2 * FEAT : HEADROWS, WIDE - TILE :] = columns.astype(BF16)
-    for load in ffn_loads:
-        load.wait()
-    short = ffn_cols - 4 * TILE
-    for m in range(3):
-        last_tile[m, :, 0:short] = raw_ff[m, :, 4 * TILE :]
-        last_tile[m, :, short:] = jnp.zeros((rows, TILE - short), BF16)
-
     pl.semaphore_wait(barrier, len(partners))
 
     far_core = plane // 2
@@ -752,6 +743,74 @@
     extra_plane = 2 * core + chip // 2
     extra_chip = (plane % 2) * 2 + core
     out_rows, in_rows = pl.ds(HEADROWS, HDIM), pl.ds(0, HEADROWS)
+    whole = rows // TILE * TILE
+    lead = 16
+    tail_in, tail_out = pl.ds(0, lead + HEADROWS), pl.ds(lead + HEADROWS, HDIM)
+
+    def leftover(ref, p):
+        pair = [ref[c * rows + whole : (c + 1) * rows] for c in (2 * p, 2 * p + 1)]
+        return jnp.concatenate(pair, 0)
+
+    def heads_times(h, start, size, right):
+        tails = slice(lead + start, lead + start + size)
+        total = dot(at_tail[h, 0, tails], leftover(right, 0), 1, 0)
+        total += dot(at_tail[h, 1, tails], leftover(right, 1), 1, 0)
+        for c in range(4):
+            total += dot(
+                at[h, c, start : start + size, :whole], right[c * rows : c * rows + whole], 1, 0
+            )
+        return total
+
+    def heads_spread(start, size, left, where, target):
+        tails = slice(lead + start, lead + start + size)
+
+        @pl.loop(0, 4)
+        def _(c):
+            total = dot(at[0, c, start : start + size, :whole], left[0, :, where], 0, 0)
+            total += dot(at[1, c, start : start + size, :whole], left[1, :, where], 0, 0)
+            target[rows_at(c * rows, whole, 16), where] = total.astype(BF16)
+
+        for p in range(2):
+            total = dot(at_tail[0, p, tails], left[0, :, where], 0, 0)
+            total += dot(at_tail[1, p, tails], left[1, :, where], 0, 0)
+            for i, c in enumerate((2 * p, 2 * p + 1)):
+                size_left = rows - whole
+                target[c * rows + whole : (c + 1) * rows, where] = total[
+                    i * size_left : (i + 1) * size_left
+                ].astype(BF16)
+
+    lane_at = lax.broadcasted_iota(jnp.int32, (1, TILE), 1)
+
+    def pack_heads(start, size):
+        a = plane % 2
+        for p in range(2):
+            even, odd = [
+                at[a, 2 * p + i, start : start + size, whole:].astype(F32) for i in range(2)
+            ]
+            tile = jnp.where(lane_at < spare, even, pltpu.roll(odd, spare, 1))
+            at_tail[a, p, lead + start : lead + start + size] = tile.astype(BF16)
+
+    def pack_taps():
+        a = plane % 2
+        columns = at[a, 0, 2 * FEAT : HEADROWS, whole:].astype(F32).T
+        at_tail[a, 0, 0:lead, 0:HDIM] = columns[spare : spare + lead].astype(BF16)
+
+    def unpack_heads(start, size):
+        a = plane % 2
+        for p in range(2):
+            tile = gat_tail[a, p, lead + start : lead + start + size].astype(F32)
+            for i, half_tile in enumerate((tile, pltpu.roll(tile, spare, 1))):
+                gat[a, 2 * p + i, start : start + size, whole:] = half_tile.astype(BF16)
+
+    def unpack_taps():
+        a = plane % 2
+        columns = gat_tail[a, 0, 0:lead, 0:HDIM].astype(F32).T
+        for c in range(4):
+            tile = gat[a, c, 2 * FEAT : HEADROWS, whole:].astype(F32)
+            for j in range(CONV):
+                tile = jnp.where(tail == spare + j, columns[:, j : j + 1], tile)
+            gat[a, c, 2 * FEAT : HEADROWS, whole:] = tile.astype(BF16)
+
     att_self = [(2 * core + h == chip) & holds_att for h in range(2)]
 
     class Heads:
@@ -797,11 +856,13 @@
     heads_out.start()
 
     class Gather:
-        def __init__(self, source, target_of):
+        def __init__(self, source, target_of, earlier=None):
             self.source, self.target_of = source, target_of
-            self.send, self.here = marks.many(6), marks.many(6)
-            self.mate_send, self.mate_here = marks.many(4), marks.many(4)
-            self.keep = pltpu.make_async_copy(source, target_of(chip), marks.one())
+            self.marks = earlier.marks if earlier else [marks.many(6), marks.many(6)] + [
+                marks.many(4), marks.many(4), marks.one()
+            ]
+            self.send, self.here, self.mate_send, self.mate_here, kept = self.marks
+            self.keep = pltpu.make_async_copy(source, target_of(chip), kept)
             mine = self.halves(source)
             there = self.halves(target_of(chip))
             self.copies = {
@@ -862,15 +923,23 @@
 
     in_line, out_line = [
         [
-            Spread(at.at[a, :, span], 2 * core + a, chip, plane, core, marks)
+            Spread(ref, 2 * core + a, chip, plane, core, marks)
             for a in range(2)
+            for ref in (at.at[a, :, span, 0:whole], at_tail.at[a, :, tail_span])
         ]
-        for span in (in_rows, out_rows)
+        for span, tail_span in ((in_rows, tail_in), (out_rows, tail_out))
     ]
     heads_in.arrive()
+
+    @pl.when(holds_att)
+    def _():
+        pack_heads(0, HEADROWS)
+        pack_taps()
+
     for item in in_line:
         item.start()
     heads_out.arrive()
+    pl.when(holds_att)(lambda: pack_heads(HEADROWS, HDIM))
     for item in out_line:
         item.start()
     heads_in.finish()
@@ -896,6 +965,14 @@
     for copy in mains:
         copy.start()
 
+    short = ffn_cols - 4 * TILE
+    for m in range(3):
+        load = pltpu.make_async_copy(ffn_weights[m], raw_ff, early(5))
+        load.start()
+        load.wait()
+        last_tile[m, :, 0:short] = raw_ff[:, 4 * TILE :]
+        last_tile[m, :, short:] = jnp.zeros((rows, TILE - short), BF16)
+
     extra_send, extra_here, extra_local = marks.one(), marks.many(4), marks.one()
     extra_self = (extra_chip == chip) & holds_att
     last = lanes(4 * TILE)
@@ -933,7 +1010,7 @@
         pair = jnp.concatenate(
             [gn[c, 0].astype(F32), gn[c, 1].astype(F32), jnp.zeros((6, rows), F32)], 0
         )
-        gcol[block_rows(c), 0:8] = pair.T
+        gcol[block_rows(c), 0:8] = pair.T.astype(BF16)
 
     step_rows = 64
 
@@ -950,7 +1027,7 @@
     def _(i):
         at_rows = rows_at(i * step_rows, step_rows, step_rows)
         xs[at_rows] = (
-            xs[at_rows].astype(F32) * inv_all[...] * gcol[at_rows, 0:1]
+            xs[at_rows].astype(F32) * inv_all[...] * gcol[at_rows, 0:1].astype(F32)
         ).astype(BF16)
 
     for item in in_line:
@@ -959,14 +1036,12 @@
     position = lax.broadcasted_iota(jnp.int32, (1, seq), 1)
 
     def taps(h):
-        columns = at[h, 0, 2 * FEAT : HEADROWS, WIDE - TILE : WIDE].astype(F32)
-        return [columns[:, rows % TILE + j : rows % TILE + j + 1] for j in range(CONV)]
+        columns = at_tail[h, 0, 0:lead, 0:HDIM].astype(F32).T
+        return [columns[:, j : j + 1] for j in range(CONV)]
 
     @pl.loop(0, 2)
     def _(h):
-        projected = dot(at[h, 0, :HEADROWS, :rows], xs[0:rows], 1, 0)
-        for c in range(1, 4):
-            projected += dot(at[h, c, :HEADROWS, :rows], xs[c * rows : (c + 1) * rows], 1, 0)
+        projected = heads_times(h, 0, HEADROWS, xs)
         qs[h] = (projected[:FEAT].astype(BF16).astype(F32) * FEAT**-0.5).astype(BF16)
         ks[h] = projected[FEAT : 2 * FEAT].astype(BF16)
         values = projected[2 * FEAT :]
@@ -1018,7 +1093,36 @@
                 last_tile, ff.at[:, block_rows(c), last], extra_send, extra_here(c), mate
             ).wait_recv()
 
-    extra_line = Chain(ff.at[:, :, last], extra_plane, chip, plane, core, marks)
+    third = short // 3
+    unit_at = lax.broadcasted_iota(jnp.int32, (rows, TILE), 1)
+
+    def pack(source, target):
+        @pl.loop(0, 3)
+        def _(m):
+            fourth = source[m, 3 * rows :, last].astype(F32)
+            for b in range(3):
+                own = source[m, b * rows : (b + 1) * rows, last].astype(F32)
+                moved = pltpu.roll(fourth, (short - b * third) % TILE, 1)
+                target[m, b * rows : (b + 1) * rows] = jnp.where(
+                    unit_at < short, own, moved
+                ).astype(BF16)
+
+    def unpack(source, target):
+        @pl.loop(0, 3)
+        def _(m):
+            fourth = jnp.zeros((rows, TILE), F32)
+            for b in range(3):
+                block = source[m, b * rows : (b + 1) * rows].astype(F32)
+                target[m, b * rows : (b + 1) * rows, last] = jnp.where(
+                    unit_at < short, block, 0.0
+                ).astype(BF16)
+                moved = pltpu.roll(block, (b * third - short) % TILE, 1)
+                here = (unit_at >= b * third) & (unit_at < (b + 1) * third)
+                fourth = jnp.where(here, moved, fourth)
+            target[m, 3 * rows :, last] = fourth.astype(BF16)
+
+    pl.when(holds_extra)(lambda: pack(ff, packed))
+    extra_line = Chain(packed, extra_plane, chip, plane, core, marks)
     extra_line.start()
 
     for item in out_line:
@@ -1028,13 +1132,18 @@
         return got.at[i]
 
     class Sum:
-        def __init__(self, guard, both=both, got=None, share=True, at_once=True):
+        def __init__(
+            self, guard, earlier=None, both=both, got=None, share=True, at_once=True
+        ):
+            self.marks = earlier.marks if earlier else [marks.many(4), marks.many(4)] + [
+                marks.many(6), marks.many(6)
+            ]
             self.guard, self.both, self.share, self.at_once = guard, both, share, at_once
             self.got = got or default_got
 
         def begin(self, fill):
             fill((1 - core) * half)
-            send, here = marks.many(4), marks.many(4)
+            send, here = self.marks[:2]
             self.order = (others[2], others[0], others[1], chip)
             self.to_mate = [
                 remote(
@@ -1075,7 +1184,7 @@
         def prepare(self):
             size = width // 2
             top, bottom = pl.ds(0, size), pl.ds(size, size)
-            send, here = marks.many(6), marks.many(6)
+            send, here = self.marks[2:]
             x, y, across = others
             self.across = [
                 remote(self.piece(True, across), self.got(2).at[top], send(0), here(0), peers[0]),
@@ -1135,12 +1244,7 @@
                 pl.semaphore_signal(free_chips, inc=1, device_id=peers[p], device_id_type=MESH)
 
     def fill_branch(start):
-        @pl.loop(0, 4)
-        def _(c):
-            where = lanes(start, half)
-            total = dot(at[0, c, HEADROWS:, :rows], att[0, :, where], 0, 0)
-            total += dot(at[1, c, HEADROWS:, :rows], att[1, :, where], 0, 0)
-            part[block_rows(c), where] = total.astype(BF16)
+        heads_spread(HEADROWS, HDIM, att, lanes(start, half), part)
 
     small[...] = jnp.zeros(small.shape, F32)
     square_at = lax.broadcasted_iota(jnp.int32, (1, WIDE), 1)
@@ -1168,12 +1272,12 @@
     @pl.loop(0, 4)
     def _(c):
         at_rows = block_rows(c)
-        sending[0, at_rows] = (mid[at_rows] * inverse_two * gcol[at_rows, 1:2]).astype(BF16)
+        sending[0, at_rows] = (mid[at_rows] * inverse_two * gcol[at_rows, 1:2].astype(F32)).astype(BF16)
 
     def token_block(c):
         return low2.at[:, lanes(core * half + c * TILE)]
 
-    low_in = Gather(sending.at[0], token_block)
+    low_in = Gather(sending.at[0], token_block, tokens_in)
     cot_in.finish()
 
     @pl.loop(0, 4)
@@ -1217,12 +1321,14 @@
             gout[2, at_rows, where] = dot(gs[at_rows], hid[unit_rows], 1, 1).astype(BF16)
 
     main_back = MainGrads(gout, main_got, chip, plane, core, marks)
-    extra_back = Collect(gout.at[:, :, last], extra_got, extra_plane, chip, plane, core, marks)
+    extra_back = Collect(packed_back, extra_got, extra_plane, chip, plane, core, marks)
     load_marks = marks.many(3)
+
+    spare_lanes = [lanes((1 - core) * half + m * TILE) for m in range(3)]
 
     def add_tiles(slot, source):
         loads = [
-            pltpu.make_async_copy(source.at[m], ff.at[2, :, lanes(m * TILE)], load_marks(m))
+            pltpu.make_async_copy(source.at[m], gs.at[:, spare_lanes[m]], load_marks(m))
             for m in range(3)
         ]
         for load in loads:
@@ -1237,11 +1343,28 @@
             for m in range(3):
                 gout[m, at_rows, where] = (
                     gout[m, at_rows, where].astype(F32)
-                    + ff[2, at_rows, m * TILE : (m + 1) * TILE].astype(F32)
+                    + gs[at_rows, spare_lanes[m]].astype(F32)
                 ).astype(BF16)
 
     def add_extra(source):
-        add_tiles(4, source)
+        packed_rows = slice(0, 3 * rows)
+        loads = [
+            pltpu.make_async_copy(source.at[m], gs.at[packed_rows, spare_lanes[m]], load_marks(m))
+            for m in range(3)
+        ]
+        for load in loads:
+            load.start()
+        for load in loads:
+            load.wait()
+
+        @pl.loop(0, 3)
+        def _(b):
+            at_rows = block_rows(b)
+            for m in range(3):
+                packed_back[m, at_rows] = (
+                    packed_back[m, at_rows].astype(F32)
+                    + gs[at_rows, spare_lanes[m]].astype(F32)
+                ).astype(BF16)
 
     slots = [away(plane, 1), plane, away(plane, 2), away(plane, 3), 4]
     inner = is_inner(plane)
@@ -1259,6 +1382,7 @@
         @pl.when(turn == 4)
         def _():
             extra_line.arrive()
+            unpack(packed, ff)
 
         slot = sum((turn == i).astype(jnp.int32) * slots[i] for i in range(5))
         feed(slot)
@@ -1271,6 +1395,7 @@
 
     pl.when(inner)(lambda: main_back.start(1))
 
+    pack(gout, packed_back)
     extra_back.start()
     main_line.finish()
 
@@ -1283,9 +1408,10 @@
     def store_gsum(at_rows, total):
         gsum[at_rows] = total
 
-    two_sum = Sum(guard=True)
+    two_sum = Sum(True, branch_sum)
     two_sum.begin(fill_grad_two)
     two_sum.combine()
+    main_back.relay(3, add_tiles)
     two_sum.pass_on()
 
     def fill_ffn(start):
@@ -1304,11 +1430,10 @@
     ffn_sum.begin(fill_ffn)
     two_sum.finish(store_gsum)
 
-    main_back.relay(3, add_tiles)
     def norm_back(source, inverse, gain_lane, base, store):
         def add_dots(c, total):
             at_rows = block_rows(c)
-            gain = gcol[at_rows, gain_lane : gain_lane + 1]
+            gain = gcol[at_rows, gain_lane : gain_lane + 1].astype(F32)
             return total + jnp.sum(gsum[at_rows] * gain * source(at_rows), 0, keepdims=True)
 
         dots = lax.fori_loop(0, 4, add_dots, jnp.zeros((1, TILE), F32))
@@ -1317,7 +1442,7 @@
         @pl.loop(0, 4)
         def _(c):
             at_rows = block_rows(c)
-            gain = gcol[at_rows, gain_lane : gain_lane + 1]
+            gain = gcol[at_rows, gain_lane : gain_lane + 1].astype(F32)
             grad, value = gsum[at_rows], source(at_rows)
             store(at_rows, base(at_rows) + (grad * gain * inverse - value * scaled))
 
@@ -1337,7 +1462,7 @@
     gain_two_back = norm_back(
         lambda r: mid[r], inverse_two, 1, lambda r: gs[r, lanes(first)].astype(F32), store_middle
     )
-    mid_in = Gather(sending.at[1], token_block)
+    mid_in = Gather(sending.at[1], token_block, tokens_in)
     gain_two_back()
     ffn_sum.combine()
     mid_in.pass_on()
@@ -1346,33 +1471,34 @@
 
     @pl.loop(0, 2)
     def _(h):
-        total = dot(at[h, 0, HEADROWS:, :rows], low2[0:rows], 1, 0)
-        for c in range(1, 4):
-            total += dot(at[h, c, HEADROWS:, :rows], low2[c * rows : (c + 1) * rows], 1, 0)
+        total = heads_times(h, HEADROWS, HDIM, low2)
         gatt[h] = total.astype(BF16)
 
     main_back.relay(2, add_tiles)
 
     out_back, in_back = [
         [
-            Collect(
-                gat.at[a, :, span], att_got.at[a, :, :, span], 2 * core + a,
-                chip, plane, core, marks,
+            Collect(ref, slots_, 2 * core + a, chip, plane, core, marks)
+            for a in range(2)
+            for ref, slots_ in (
+                (gat.at[a, :, span, 0:whole], att_got.at[a, :, :, span]),
+                (gat_tail.at[a, :, tail_span], tail_got.at[a, :, :, tail_span]),
             )
-            for a in range(2)
         ]
-        for span in (out_rows, in_rows)
+        for span, tail_span in ((out_rows, tail_out), (in_rows, tail_in))
     ]
 
     def head_grads(left, right, start, size):
-        whole = rows // TILE * TILE
-
         @pl.loop(0, 2)
         def _(h):
             for c in range(4):
-                grad = dot(left[h], right[c * rows : (c + 1) * rows], 1, 1).astype(BF16)
-                gat[h, c, start : start + size, :whole] = grad[:, :whole]
-                gat[h, c, start : start + size, whole:rows] = grad[:, whole:]
+                gat[h, c, start : start + size, :whole] = dot(
+                    left[h], right[c * rows : c * rows + whole], 1, 1
+                ).astype(BF16)
+            for p in range(2):
+                gat_tail[h, p, lead + start : lead + start + size] = dot(
+                    left[h], leftover(right, p), 1, 1
+                ).astype(BF16)
 
     head_grads(att, low2, HEADROWS, HDIM)
     for item in out_back:
@@ -1416,9 +1542,8 @@
         gproj[h, 2 * FEAT :] = grad_raw.astype(BF16)
         columns = jnp.zeros((HDIM, TILE), F32)
         for j in range(CONV):
-            columns = jnp.where(tail == rows % TILE + j, sums[j], columns)
-        for c in range(4):
-            gat[h, c, 2 * FEAT : HEADROWS, WIDE - TILE :] = columns.astype(BF16)
+            columns = jnp.where(tail == j, sums[j], columns)
+        gat_tail[h, 0, 0:lead, 0:HDIM] = columns.T[0:lead].astype(BF16)
 
     head_grads(gproj, xs, 0, HEADROWS)
     for item in in_back:
@@ -1428,14 +1553,9 @@
     mid_in.finish()
 
     def fill_grad_one(start):
-        @pl.loop(0, 4)
-        def _(c):
-            where = lanes(start, half)
-            total = dot(at[0, c, :HEADROWS, :rows], gproj[0, :, where], 0, 0)
-            total += dot(at[1, c, :HEADROWS, :rows], gproj[1, :, where], 0, 0)
-            part[block_rows(c), where] = total.astype(BF16)
-
-    one_sum = Sum(guard=True)
+        heads_spread(0, HEADROWS, gproj, lanes(start, half), part)
+
+    one_sum = Sum(True, branch_sum)
     one_sum.begin(fill_grad_one)
     one_sum.combine()
     extra_back.relay(add_extra)
@@ -1471,6 +1591,43 @@
 
 
     one_sum.finish(store_gsum)
+    head_marks = marks.many(4)
+
+    def add_head(i, start, size, tail_start, tail_size):
+        a, is_tail = i // 2, i % 2
+        target, count = (gat_tail, 2) if is_tail else (gat, 4)
+        begin, extent = (tail_start, tail_size) if is_tail else (start, size)
+        wide = TILE if is_tail else whole
+
+        def add(source):
+            loads = [
+                pltpu.make_async_copy(
+                    source.at[c], part.at[c * BLOCKROWS : c * BLOCKROWS + extent, 0:wide],
+                    head_marks(c),
+                )
+                for c in range(count)
+            ]
+            for load in loads:
+                load.start()
+            for load in loads:
+                load.wait()
+            for c in range(count):
+                target[a, c, begin : begin + extent, 0:wide] = (
+                    target[a, c, begin : begin + extent, 0:wide].astype(F32)
+                    + part[c * BLOCKROWS : c * BLOCKROWS + extent, 0:wide].astype(F32)
+                ).astype(BF16)
+
+        return add
+
+    def add_out(i):
+        return add_head(i, HEADROWS, HDIM, lead + HEADROWS, HDIM)
+
+    def add_in(i):
+        return add_head(i, 0, HEADROWS, 0, lead + HEADROWS)
+
+    for i in range(4):
+        out_back[i].relay(add_out(i))
+
     inverse_own = inv_all[:, lanes(first)]
 
     def store_tokens(at_rows, value):
@@ -1509,6 +1666,34 @@
         copy.start()
     pending += backs
 
+    extra_back.total(add_extra)
+    pl.when(holds_extra)(lambda: unpack(packed_back, gout))
+    last_send, last_here, last_local = marks.many(4), marks.one(), marks.one()
+
+    def last_copy(c):
+        return remote(
+            gout.at[:, block_rows(c), last], out_ff.at[:, :, last], last_send(c), last_here,
+            device(c, plane, chip % 2),
+        )
+
+    def last_keep():
+        return pltpu.make_async_copy(
+            gout.at[:, block_rows(chip), last], out_ff.at[:, :, last], last_local
+        )
+
+    for c in range(4):
+        same = (c == chip) & (core == chip % 2)
+
+        @pl.when(holds_extra & same)
+        def _():
+            last_keep().start()
+
+        @pl.when(holds_extra & no(same))
+        def _():
+            last_copy(c).start()
+
+    for i in range(4):
+        in_back[i].relay(add_in(i))
     for copy in trio:
         copy.wait()
     small_b[0] = small[chip] + small_a[0] + small_a[1] + small_a[2]
@@ -1520,57 +1705,6 @@
     for copy in seven:
         copy.start()
 
-    extra_back.total(add_extra)
-    last_send, last_here, last_local = marks.many(4), marks.one(), marks.one()
-
-    def last_copy(c):
-        return remote(
-            gout.at[:, block_rows(c), last], out_ff.at[:, :, last], last_send(c), last_here,
-            device(c, plane, chip % 2),
-        )
-
-    def last_keep():
-        return pltpu.make_async_copy(
-            gout.at[:, block_rows(chip), last], out_ff.at[:, :, last], last_local
-        )
-
-    for c in range(4):
-        same = (c == chip) & (core == chip % 2)
-
-        @pl.when(holds_extra & same)
-        def _():
-            last_keep().start()
-
-        @pl.when(holds_extra & no(same))
-        def _():
-            last_copy(c).start()
-
-    head_marks = marks.many(4)
-
-    def add_head(a, start, size):
-        def add(source):
-            loads = [
-                pltpu.make_async_copy(
-                    source.at[c], part.at[c * BLOCKROWS : c * BLOCKROWS + size, 0:WIDE],
-                    head_marks(c),
-                )
-                for c in range(4)
-            ]
-            for load in loads:
-                load.start()
-            for load in loads:
-                load.wait()
-            for c in range(4):
-                gat[a, c, start : start + size] = (
-                    gat[a, c, start : start + size].astype(F32)
-                    + part[c * BLOCKROWS : c * BLOCKROWS + size, 0:WIDE].astype(F32)
-                ).astype(BF16)
-
-        return add
-
-    for items, start, size in ((out_back, HEADROWS, HDIM), (in_back, 0, HEADROWS)):
-        for a in range(2):
-            items[a].relay(add_head(a, start, size))
     class HeadsBack:
         def __init__(self, span):
             self.span, self.local = span, marks.one()
@@ -1609,12 +1743,20 @@
                         self.here(h), mate,
                     ).wait_recv()
 
-    heads_back = []
-    for items, start, size in ((out_back, HEADROWS, HDIM), (in_back, 0, HEADROWS)):
-        for a in range(2):
-            items[a].total(add_head(a, start, size))
-        heads_back.append(HeadsBack(pl.ds(start, size)))
-        heads_back[-1].start()
+    heads_back = [HeadsBack(out_rows), HeadsBack(in_rows)]
+    for i in range(4):
+        out_back[i].total(add_out(i))
+    pl.when(holds_att)(lambda: unpack_heads(HEADROWS, HDIM))
+    heads_back[0].start()
+    for i in range(4):
+        in_back[i].total(add_in(i))
+
+    @pl.when(holds_att)
+    def _():
+        unpack_heads(0, HEADROWS)
+        unpack_taps()
+
+    heads_back[1].start()
 
     for copy in seven:
         copy.wait()
@@ -1666,11 +1808,12 @@
             shape((rows, half), BF16),
             shape((8, WIDE), F32),
             shape((5,) + tiles, BF16),
-            shape((4,) + tiles, BF16),
-            shape((2, 4) + head, BF16),
+            shape((3, 3, 3 * rows, TILE), BF16),
+            shape((2, 3, 4, BLOCKROWS, rows // TILE * TILE), BF16),
+            shape((2, 3, 2, 16 + BLOCKROWS, TILE), BF16),
         ],
         in_specs=[ANY] * 10,
-        out_specs=[ANY] * 8,
+        out_specs=[ANY] * 9,
         scratch_shapes=[
             vmem((3, width, 5 * TILE), BF16),
             vmem((2,) + head, BF16),
@@ -1688,7 +1831,7 @@
             vmem((5 * TILE, seq), BF16),
             vmem((2 * TILE, seq), BF16),
             vmem((4, 2, 1, rows), BF16),
-            vmem((width, TILE), F32),
+            vmem((width, TILE), BF16),
             vmem((2, HDIM, seq), F32),
             vmem((2, FEAT, seq), BF16),
             vmem((2, FEAT, seq), BF16),
@@ -1706,15 +1849,17 @@
             vmem((4, 8, WIDE), F32),
             vmem((3, 8, WIDE), F32),
             vmem((8, 8, WIDE), F32),
-            vmem((3,) + w_gate.shape, BF16),
+            vmem(w_gate.shape, BF16),
             vmem(w_qkv.shape, BF16),
             vmem(w_out.shape, BF16),
             vmem(conv.shape, BF16),
             vmem((8, 2 * TILE), F32),
-            vmem((3, rows, TILE), BF16),
-            vmem((2, BLOCKROWS, WIDE), BF16),
             vmem((2, 1, rows), BF16),
             [vmem((rows,), BF16)] * 2,
+            vmem((3, 3 * rows, TILE), BF16),
+            vmem((3, 3 * rows, TILE), BF16),
+            vmem((2, 2, 16 + BLOCKROWS, TILE), BF16),
+            vmem((2, 2, 16 + BLOCKROWS, TILE), BF16),
             dma(MARKS),
             pltpu.SemaphoreType.REGULAR,
             pltpu.SemaphoreType.REGULAR,
@@ -1767,11 +1912,10 @@
         ff_out[m] = ff_in[m, :, :cols].astype(F32)
         store(ff_out.at[m], target)
     loads[5].wait()
-    rms_out[0] = small_in[0:1, :rows]
-    rms_out[1] = small_in[1:2, :rows]
-    rms_out[2] = jnp.sqrt(small_in[2:3, :rows] / count)
     for i, target in enumerate((to_mix, to_ffn, to_rms)):
-        store(rms_out.at[i], target)
+        row = small_in[i : i + 1, :rows].reshape(rows)
+        rms_out[i][...] = jnp.sqrt(row / count) if i == 2 else row
+        store(rms_out[i], target)
     for copy in stores:
         copy.wait()
 
@@ -1781,7 +1925,7 @@
     shape = jax.ShapeDtypeStruct
     shapes = [
         (rows, half), (2 * HEADROWS, rows), (CONV, 2 * HDIM), (2 * HDIM, rows),
-        (rows, ffn_cols), (rows, ffn_cols), (rows, ffn_cols), (1, rows), (1, rows), (1, rows),
+        (rows, ffn_cols), (rows, ffn_cols), (rows, ffn_cols), (rows,), (rows,), (rows,),
     ]
     vmem = pltpu.VMEM
     return pl.pallas_call(
@@ -1793,7 +1937,7 @@
             vmem(ff.shape, BF16), vmem(at.shape, BF16), vmem(tok.shape, BF16),
             vmem(small.shape, F32), vmem(shapes[0], F32), vmem(shapes[1], F32),
             vmem(shapes[2], F32), vmem(shapes[3], F32), vmem((3,) + shapes[4], F32),
-            vmem((3,) + shapes[7], F32), dma(24),
+            [vmem(shapes[7], F32)] * 3, dma(24),
         ],
         compiler_params=pltpu.CompilerParams(vmem_limit_bytes=60 * 2**20),
         name="outputs",
@@ -1813,7 +1957,7 @@
     to_tok, to_qkv, to_conv, to_out, to_gate, to_up, to_down, to_mix, to_ffn, to_rms = grads
     return (
         out_res, to_tok, to_qkv.T, to_conv, to_out, to_gate, to_up, to_down,
-        to_mix[0], to_ffn[0], to_rms[0, :3],
+        to_mix, to_ffn, to_rms[:3],
     )
 
 
@@ -1825,7 +1969,7 @@
         and lax.axis_size("col") == 8
         and total_rows == 4 * LONGEST
         and weights[0].shape[1] == 2 * HEADROWS
-        and 4 * TILE < weights[3].shape[1] <= 5 * TILE
+        and weights[3].shape[1] == 4 * TILE + 96
     ):
         return on_device_full(tokens, cotangent, *weights)
     return on_device_general(tokens, cotangent, lengths, deal_order, *weights)

time: 301 us -> 292 us (0.970)
  Pallas kernels: 296 us -> 289 us
    pallas_call x1, Pallas kernels: 292 us -> 285 us  [run_layer(): pl.pallas_call(layer_kernel, out_shape=[shape((3, rows, 5 * TILE), BF16),...]
where the time goes in v6:
time: 292 us; the launch traced here: 291 us
  Pallas kernels  289 us (99%)
    pallas_call x1, Pallas kernels, run_layer(): pl.pallas_call(layer_kernel, out_shape=[shape((3, rows, 5 * TILE), BF16),...  285 us

profile of v6, /device:TPU:4, one launch (start us, length us, event | category | flops | bytes accessed | tf_op | source)
XLA Modules:
  0.0 291.4 jit_solution(3301460117146615414)
XLA Ops:
  0.6 285.0 %layer.1 = (bf16[3,448,640]{2,1,0:T(8,128)(2,1)}, bf16[2,256,512]{2,1,0:T(8,128)(2,1)}, bf16[448,512]{1,0:T(8,128)(2,1)}, bf16[448,512]{1,0:T(8,128)(2,1)}, f32[...) custom-call(bf16[448,608]{1,0:T(8,128)(2,1)} %w_gate.1, ...), custom_call_target="tpu_custom_call" | custom-call | tf_op jit(solution)/shard_map/layer/pallas_call | solution.py:1802
  285.6 0.0 copy-start
  285.7 3.8 %outputs.1 = (f32[448,512]{1,0:T(8,128)}, f32[288,448]{1,0:T(8,128)}, f32[3,224]{1,0:T(4,128)}, f32[224,448]{1,0:T(8,128)}, f32[448,608]{1,0:T(8,128)}, /*index=...) custom-call(bf16[3,448,640]{2,1,0:T(8,128)(2,1)} %get-tuple-element.27.ff, ...), custom_call_target="tpu_custom_call" | custom-call | tf_op jit(solution)/shard_map/outputs/pallas_call | solution.py:1931
  289.4 1.2 slice.3
  290.6 0.0 copy-done
  290.6 0.8 copy.22
Async XLA Ops:
  285.6 5.0 %copy-start = (bf16[448,512]{1,0:T(8,128)(2,1)S(1)}, bf16[448,512]{1,0:T(8,128)(2,1)}, u32[]{:S(2)}) copy-start(bf16[448,512]{1,0:T(8,128)(2,1)} %get-tuple-element.52) | copy-start | bytes 1376260

commit v7 on v6

--- a/solution.py
+++ b/solution.py
@@ -592,6 +592,14 @@
             self.gout.at[:, :, lanes(slot * TILE)], self.slots.at[receive],
             self.sends(send), self.here(receive), device(chip, away(plane, to_step), core),
         )
+
+    def start_rows(self, at_rows):
+        chip, plane, core = self.spot
+        slot = away(plane, 1)
+        remote(
+            self.gout.at[:, at_rows, lanes(slot * TILE)], self.slots.at[0, :, at_rows],
+            self.sends(0), self.here(0), device(chip, slot, core),
+        ).start()
 
     def start(self, step):
         receive = {1: 0, 2: 4, 3: 3}[step]
@@ -945,6 +953,14 @@
     heads_in.finish()
     heads_out.finish()
 
+    short = ffn_cols - 4 * TILE
+    for m in range(3):
+        load = pltpu.make_async_copy(ffn_weights[m], raw_ff, early(5))
+        load.start()
+        load.wait()
+        last_tile[m, :, 0:short] = raw_ff[:, 4 * TILE :]
+        last_tile[m, :, short:] = jnp.zeros((rows, TILE - short), BF16)
+
     tokens_in.pass_on()
     main_send, main_here, main_local = marks.many(9), marks.many(9), marks.many(3)
     main_here_at = [ff.at[m, block_rows(chip), lanes(plane * TILE)] for m in range(3)]
@@ -965,14 +981,6 @@
     for copy in mains:
         copy.start()
 
-    short = ffn_cols - 4 * TILE
-    for m in range(3):
-        load = pltpu.make_async_copy(ffn_weights[m], raw_ff, early(5))
-        load.start()
-        load.wait()
-        last_tile[m, :, 0:short] = raw_ff[:, 4 * TILE :]
-        last_tile[m, :, short:] = jnp.zeros((rows, TILE - short), BF16)
-
     extra_send, extra_here, extra_local = marks.one(), marks.many(4), marks.one()
     extra_self = (extra_chip == chip) & holds_att
     last = lanes(4 * TILE)
@@ -1158,6 +1166,9 @@
                 copy.start()
             fill(core * half)
 
+        def release(self):
+            pl.semaphore_signal(free_mate, inc=1, device_id=mate, device_id_type=MESH)
+
         def combine(self):
             self.prepare()
             for i, c in enumerate(self.order):
@@ -1173,7 +1184,6 @@
 
                 if self.at_once:
                     self.send(i)
-            pl.semaphore_signal(free_mate, inc=1, device_id=mate, device_id_type=MESH)
             for copy in self.to_mate:
                 copy.wait_send()
 
@@ -1260,8 +1270,8 @@
     branch_sum = Sum(guard=False)
     branch_sum.begin(fill_branch)
     cot_in.pass_on()
-    cot_in.arrive()
     branch_sum.combine()
+    branch_sum.release()
     branch_sum.pass_on()
     main_line.relay()
     extra_line.start_inner()
@@ -1278,6 +1288,7 @@
         return low2.at[:, lanes(core * half + c * TILE)]
 
     low_in = Gather(sending.at[0], token_block, tokens_in)
+    cot_in.arrive()
     cot_in.finish()
 
     @pl.loop(0, 4)
@@ -1290,7 +1301,7 @@
 
     main_line.relay_far()
     extra_line.relay()
-    def feed(slot):
+    def feed_units(slot):
         where = lanes(slot * TILE)
         unit_rows = rows_at(slot * TILE, TILE, TILE)
         for m in range(3):
@@ -1310,15 +1321,18 @@
             ).astype(BF16)
             gg[TILE:, span] = (grad_hidden * activated).astype(BF16)
 
-        @pl.loop(0, 4)
-        def _(c):
-            at_rows = block_rows(c)
-            pair = jnp.concatenate([ff[0, at_rows, where], ff[1, at_rows, where]], 1)
-            acc3[at_rows] += dot(pair, gg[...], 1, 0)
-            grads = dot(low2[at_rows], gg[...], 1, 1).astype(BF16)
-            gout[0, at_rows, where] = grads[:, :TILE]
-            gout[1, at_rows, where] = grads[:, TILE:]
-            gout[2, at_rows, where] = dot(gs[at_rows], hid[unit_rows], 1, 1).astype(BF16)
+    def feed_input(slot, at_rows):
+        where = lanes(slot * TILE)
+        pair = jnp.concatenate([ff[0, at_rows, where], ff[1, at_rows, where]], 1)
+        acc3[at_rows] += dot(pair, gg[...], 1, 0)
+
+    def feed_weights(slot, at_rows):
+        where = lanes(slot * TILE)
+        unit_rows = rows_at(slot * TILE, TILE, TILE)
+        grads = dot(low2[at_rows], gg[...], 1, 1).astype(BF16)
+        gout[0, at_rows, where] = grads[:, :TILE]
+        gout[1, at_rows, where] = grads[:, TILE:]
+        gout[2, at_rows, where] = dot(gs[at_rows], hid[unit_rows], 1, 1).astype(BF16)
 
     main_back = MainGrads(gout, main_got, chip, plane, core, marks)
     extra_back = Collect(packed_back, extra_got, extra_plane, chip, plane, core, marks)
@@ -1366,10 +1380,10 @@
                     + gs[at_rows, spare_lanes[m]].astype(F32)
                 ).astype(BF16)
 
-    slots = [away(plane, 1), plane, away(plane, 2), away(plane, 3), 4]
+    slots = [away(plane, 1), plane, away(plane, 2), away(plane, 3)]
     inner = is_inner(plane)
 
-    @pl.loop(0, 5)
+    @pl.loop(0, 4)
     def _(turn):
         pl.when(turn == 2)(lambda: extra_line.relay_far())
 
@@ -1379,24 +1393,29 @@
             def _():
                 main_line.arrive(step)
 
-        @pl.when(turn == 4)
-        def _():
-            extra_line.arrive()
-            unpack(packed, ff)
-
-        slot = sum((turn == i).astype(jnp.int32) * slots[i] for i in range(5))
-        feed(slot)
-
-        for i, step in ((0, 1), (2, 2), (3, 3)):
+        slot = sum((turn == i).astype(jnp.int32) * slots[i] for i in range(4))
+        feed_units(slot)
+
+        @pl.loop(0, 4)
+        def _(c):
+            feed_input(slot, block_rows(c))
+            feed_weights(slot, block_rows(c))
+            pl.when((turn == 0) & no(inner))(lambda: main_back.start_rows(block_rows(c)))
+
+        for i, step in ((2, 2), (3, 3)):
 
             @pl.when((turn == i) & no(inner))
             def _():
                 main_back.start(step)
 
-    pl.when(inner)(lambda: main_back.start(1))
-
-    pack(gout, packed_back)
-    extra_back.start()
+    extra_line.arrive()
+    unpack(packed, ff)
+    feed_units(4)
+
+    @pl.loop(0, 4)
+    def _(c):
+        feed_input(4, block_rows(c))
+
     main_line.finish()
 
     def fill_grad_two(start):
@@ -1411,6 +1430,14 @@
     two_sum = Sum(True, branch_sum)
     two_sum.begin(fill_grad_two)
     two_sum.combine()
+    @pl.loop(0, 4)
+    def _(c):
+        feed_weights(4, block_rows(c))
+
+    two_sum.release()
+    pl.when(inner)(lambda: main_back.start(1))
+    pack(gout, packed_back)
+    extra_back.start()
     main_back.relay(3, add_tiles)
     two_sum.pass_on()
 
@@ -1465,6 +1492,7 @@
     mid_in = Gather(sending.at[1], token_block, tokens_in)
     gain_two_back()
     ffn_sum.combine()
+    ffn_sum.release()
     mid_in.pass_on()
     ffn_sum.send_all()
     mid_in.arrive()
@@ -1558,6 +1586,7 @@
     one_sum = Sum(True, branch_sum)
     one_sum.begin(fill_grad_one)
     one_sum.combine()
+    one_sum.release()
     extra_back.relay(add_extra)
 
     def store_result(at_rows, total):

time: 292 us -> 286 us (0.979)
  Pallas kernels: 289 us -> 283 us
    pallas_call x1, Pallas kernels: 285 us -> 279 us  [run_layer(): pl.pallas_call(layer_kernel, out_shape=[shape((3, rows, 5 * TILE), BF16),...]
where the time goes in v7:
time: 286 us; the launch traced here: 285 us
  Pallas kernels  283 us (99%)
    pallas_call x1, Pallas kernels, run_layer(): pl.pallas_call(layer_kernel, out_shape=[shape((3, rows, 5 * TILE), BF16),...  279 us

profile of v7, /device:TPU:4, one launch (start us, length us, event | category | flops | bytes accessed | tf_op | source)
XLA Modules:
  0.0 285.4 jit_solution(9678858021990258450)
XLA Ops:
  0.6 279.0 %layer.1 = (bf16[3,448,640]{2,1,0:T(8,128)(2,1)}, bf16[2,256,512]{2,1,0:T(8,128)(2,1)}, bf16[448,512]{1,0:T(8,128)(2,1)}, bf16[448,512]{1,0:T(8,128)(2,1)}, f32[...) custom-call(bf16[448,608]{1,0:T(8,128)(2,1)} %w_gate.1, ...), custom_call_target="tpu_custom_call" | custom-call | tf_op jit(solution)/shard_map/layer/pallas_call | solution.py:1831
  279.7 0.0 copy-start
  279.7 3.8 %outputs.1 = (f32[448,512]{1,0:T(8,128)}, f32[288,448]{1,0:T(8,128)}, f32[3,224]{1,0:T(4,128)}, f32[224,448]{1,0:T(8,128)}, f32[448,608]{1,0:T(8,128)}, /*index=...) custom-call(bf16[3,448,640]{2,1,0:T(8,128)(2,1)} %get-tuple-element.27.ff, ...), custom_call_target="tpu_custom_call" | custom-call | tf_op jit(solution)/shard_map/outputs/pallas_call | solution.py:1960
  283.4 1.2 slice.3
  284.6 0.0 copy-done
  284.6 0.8 copy.22
Async XLA Ops:
  279.7 5.0 %copy-start = (bf16[448,512]{1,0:T(8,128)(2,1)S(1)}, bf16[448,512]{1,0:T(8,128)(2,1)}, u32[]{:S(2)}) copy-start(bf16[448,512]{1,0:T(8,128)(2,1)} %get-tuple-element.52) | copy-start | bytes 1376260

commit v8 on v7

--- a/solution.py
+++ b/solution.py
@@ -1533,6 +1533,8 @@
         item.start()
 
 
+    ffn_sum.pass_on()
+
     @pl.loop(0, 2)
     def _(h):
         grad_keys = jnp.zeros((FEAT, seq), F32)
@@ -1577,25 +1579,13 @@
     for item in in_back:
         item.start()
 
-    ffn_sum.pass_on()
     mid_in.finish()
-
-    def fill_grad_one(start):
-        heads_spread(0, HEADROWS, gproj, lanes(start, half), part)
-
-    one_sum = Sum(True, branch_sum)
-    one_sum.begin(fill_grad_one)
-    one_sum.combine()
-    one_sum.release()
-    extra_back.relay(add_extra)
 
     def store_result(at_rows, total):
         note_square(1, total)
         total = mid[at_rows] + total
         note_square(2, total)
         sending[0, at_rows] = total.astype(BF16)
-
-    one_sum.pass_on()
 
     def hand_out(source, target):
         send, here = marks.many(3), marks.many(3)
@@ -1619,6 +1609,34 @@
     pending = hand_out(sending.at[0], out_res)
 
 
+    def fill_grad_one(start):
+        heads_spread(0, HEADROWS, gproj, lanes(start, half), part)
+
+    one_sum = Sum(True, branch_sum)
+    one_sum.begin(fill_grad_one)
+    one_sum.combine()
+    one_sum.release()
+    extra_back.relay(add_extra)
+
+    one_sum.pass_on()
+
+    main_back.total(add_tiles)
+    back_send, back_here = marks.many(3), marks.many(3)
+    mine = lanes(plane * TILE)
+    back_to = out_ff.at[:, :, lanes(chip * TILE)]
+    backs = [
+        remote(
+            gout.at[:, block_rows(others[p]), mine], back_to, back_send(p), back_here(p), peers[p]
+        )
+        for p in range(3)
+    ]
+    backs.append(
+        pltpu.make_async_copy(gout.at[:, block_rows(chip), mine], back_to, marks.one())
+    )
+    for copy in backs:
+        copy.start()
+    pending += backs
+
     one_sum.finish(store_gsum)
     head_marks = marks.many(4)
 
@@ -1678,23 +1696,6 @@
     for copy in trio:
         copy.start()
 
-    main_back.total(add_tiles)
-    back_send, back_here = marks.many(3), marks.many(3)
-    mine = lanes(plane * TILE)
-    back_to = out_ff.at[:, :, lanes(chip * TILE)]
-    backs = [
-        remote(
-            gout.at[:, block_rows(others[p]), mine], back_to, back_send(p), back_here(p), peers[p]
-        )
-        for p in range(3)
-    ]
-    backs.append(
-        pltpu.make_async_copy(gout.at[:, block_rows(chip), mine], back_to, marks.one())
-    )
-    for copy in backs:
-        copy.start()
-    pending += backs
-
     extra_back.total(add_extra)
     pl.when(holds_extra)(lambda: unpack(packed_back, gout))
     last_send, last_here, last_local = marks.many(4), marks.one(), marks.one()
@@ -1723,6 +1724,60 @@
 
     for i in range(4):
         in_back[i].relay(add_in(i))
+    class HeadsBack:
+        def __init__(self, span):
+            self.span, self.local = span, marks.one()
+            self.send, self.here = marks.many(4), marks.many(2)
+
+        def same(self, c):
+            return (c == chip) & (core == chip // 2)
+
+        def copy(self, c):
+            return remote(
+                gat.at[plane % 2, c, self.span], out_at.at[chip % 2, self.span], self.send(c),
+                self.here(chip % 2), device(c, plane, chip // 2),
+            )
+
+        def keep(self):
+            return pltpu.make_async_copy(
+                gat.at[plane % 2, chip, self.span], out_at.at[chip % 2, self.span], self.local
+            )
+
+        def start(self):
+            for c in range(4):
+                pl.when(holds_att & self.same(c))(lambda: self.keep().start())
+                pl.when(holds_att & no(self.same(c)))(lambda: self.copy(c).start())
+
+        def finish(self):
+            for c in range(4):
+                pl.when(holds_att & self.same(c))(lambda: self.keep().wait())
+                pl.when(holds_att & no(self.same(c)))(lambda: self.copy(c).wait_send())
+
+            for h in range(2):
+
+                @pl.when(no(att_self[h]))
+                def _():
+                    remote(
+                        gat.at[0, 0, self.span], out_at.at[h, self.span], self.send(0),
+                        self.here(h), mate,
+                    ).wait_recv()
+
+    heads_back = [HeadsBack(out_rows), HeadsBack(in_rows)]
+    for i in range(4):
+        out_back[i].total(add_out(i))
+    pl.when(holds_att)(lambda: unpack_heads(HEADROWS, HDIM))
+    heads_back[0].start()
+
+    for i in range(4):
+        in_back[i].total(add_in(i))
+
+    @pl.when(holds_att)
+    def _():
+        unpack_heads(0, HEADROWS)
+        unpack_taps()
+
+    heads_back[1].start()
+
     for copy in trio:
         copy.wait()
     small_b[0] = small[chip] + small_a[0] + small_a[1] + small_a[2]
@@ -1733,59 +1788,6 @@
     ]
     for copy in seven:
         copy.start()
-
-    class HeadsBack:
-        def __init__(self, span):
-            self.span, self.local = span, marks.one()
-            self.send, self.here = marks.many(4), marks.many(2)
-
-        def same(self, c):
-            return (c == chip) & (core == chip // 2)
-
-        def copy(self, c):
-            return remote(
-                gat.at[plane % 2, c, self.span], out_at.at[chip % 2, self.span], self.send(c),
-                self.here(chip % 2), device(c, plane, chip // 2),
-            )
-
-        def keep(self):
-            return pltpu.make_async_copy(
-                gat.at[plane % 2, chip, self.span], out_at.at[chip % 2, self.span], self.local
-            )
-
-        def start(self):
-            for c in range(4):
-                pl.when(holds_att & self.same(c))(lambda: self.keep().start())
-                pl.when(holds_att & no(self.same(c)))(lambda: self.copy(c).start())
-
-        def finish(self):
-            for c in range(4):
-                pl.when(holds_att & self.same(c))(lambda: self.keep().wait())
-                pl.when(holds_att & no(self.same(c)))(lambda: self.copy(c).wait_send())
-
-            for h in range(2):
-
-                @pl.when(no(att_self[h]))
-                def _():
-                    remote(
-                        gat.at[0, 0, self.span], out_at.at[h, self.span], self.send(0),
-                        self.here(h), mate,
-                    ).wait_recv()
-
-    heads_back = [HeadsBack(out_rows), HeadsBack(in_rows)]
-    for i in range(4):
-        out_back[i].total(add_out(i))
-    pl.when(holds_att)(lambda: unpack_heads(HEADROWS, HDIM))
-    heads_back[0].start()
-    for i in range(4):
-        in_back[i].total(add_in(i))
-
-    @pl.when(holds_att)
-    def _():
-        unpack_heads(0, HEADROWS)
-        unpack_taps()
-
-    heads_back[1].start()
 
     for copy in seven:
         copy.wait()
@@ -1901,8 +1903,8 @@
 
 
 def outputs_kernel(
-    count, ff, at, tok, small, to_tok, to_qkv, to_conv, to_out, to_gate, to_up, to_down,
-    to_mix, to_ffn, to_rms, ff_in, at_in, tok_in, small_in, tok_out, qkv_out, conv_out, out_out,
+    count, ff, at, res, tok, small, to_res, to_tok, to_qkv, to_conv, to_out, to_gate, to_up, to_down,
+    to_mix, to_ffn, to_rms, ff_in, at_in, res_in, tok_in, small_in, tok_out, qkv_out, conv_out, out_out,
     ff_out, rms_out, sem,
 ):
     rows, cols = to_gate.shape
@@ -1910,7 +1912,7 @@
     loads = [
         pltpu.make_async_copy(source, target, marks.one())
         for source, target in (
-            [(tok, tok_in), (at, at_in)] + [(ff.at[m], ff_in.at[m]) for m in range(3)]
+            [(tok, tok_in), (at, at_in), (res, res_in)] + [(ff.at[m], ff_in.at[m]) for m in range(3)]
             + [(small, small_in)]
         )
     ]
@@ -1931,46 +1933,48 @@
         out_out[h * HDIM : (h + 1) * HDIM] = at_in[h, HEADROWS:, :rows].astype(F32)
     store(qkv_out, to_qkv)
     store(out_out, to_out)
+    loads[2].wait()
+    store(res_in, to_res)
     taps = jnp.concatenate(
         [at_in[h, 2 * FEAT : HEADROWS, WIDE - TILE :].astype(F32) for h in range(2)], 0
     )
     conv_out[...] = taps.T[rows % TILE : rows % TILE + CONV]
     store(conv_out, to_conv)
     for m, target in enumerate((to_gate, to_up, to_down)):
-        loads[2 + m].wait()
+        loads[3 + m].wait()
         ff_out[m] = ff_in[m, :, :cols].astype(F32)
         store(ff_out.at[m], target)
-    loads[5].wait()
+    loads[6].wait()
     for i, target in enumerate((to_mix, to_ffn, to_rms)):
-        row = small_in[i : i + 1, :rows].reshape(rows)
+        row = small_in[i : i + 1, : target.shape[0]].reshape(target.shape[0])
         rms_out[i][...] = jnp.sqrt(row / count) if i == 2 else row
         store(rms_out[i], target)
     for copy in stores:
         copy.wait()
 
 
-def outputs(ff, at, tok, small, ffn_cols, count):
+def outputs(ff, at, res, tok, small, ffn_cols, count):
     rows, half = tok.shape
     shape = jax.ShapeDtypeStruct
     shapes = [
         (rows, half), (2 * HEADROWS, rows), (CONV, 2 * HDIM), (2 * HDIM, rows),
-        (rows, ffn_cols), (rows, ffn_cols), (rows, ffn_cols), (rows,), (rows,), (rows,),
+        (rows, ffn_cols), (rows, ffn_cols), (rows, ffn_cols), (rows,), (rows,), (3,),
     ]
     vmem = pltpu.VMEM
     return pl.pallas_call(
         functools.partial(outputs_kernel, count),
-        out_shape=[shape(s, F32) for s in shapes],
-        in_specs=[ANY] * 4,
-        out_specs=[ANY] * 10,
+        out_shape=[shape(res.shape, BF16)] + [shape(s, F32) for s in shapes],
+        in_specs=[ANY] * 5,
+        out_specs=[ANY] * 11,
         scratch_shapes=[
-            vmem(ff.shape, BF16), vmem(at.shape, BF16), vmem(tok.shape, BF16),
+            vmem(ff.shape, BF16), vmem(at.shape, BF16), vmem(res.shape, BF16), vmem(tok.shape, BF16),
             vmem(small.shape, F32), vmem(shapes[0], F32), vmem(shapes[1], F32),
             vmem(shapes[2], F32), vmem(shapes[3], F32), vmem((3,) + shapes[4], F32),
-            [vmem(shapes[7], F32)] * 3, dma(24),
+            [vmem(s, F32) for s in shapes[7:]], dma(24),
         ],
         compiler_params=pltpu.CompilerParams(vmem_limit_bytes=60 * 2**20),
         name="outputs",
-    )(ff, at, tok, small)
+    )(ff, at, res, tok, small)
 
 
 def on_device_full(
@@ -1982,12 +1986,10 @@
         w_gate, w_up, w_down, w_qkv.T, w_out, conv_weight, gain_mix, gain_ffn,
         tokens, cotangent,
     )[:5]
-    grads = outputs(out_ff, out_at, out_tok, small, ffn_cols, 8 * half * 4 * rows)
-    to_tok, to_qkv, to_conv, to_out, to_gate, to_up, to_down, to_mix, to_ffn, to_rms = grads
-    return (
-        out_res, to_tok, to_qkv.T, to_conv, to_out, to_gate, to_up, to_down,
-        to_mix, to_ffn, to_rms[:3],
-    )
+    result, to_tok, to_qkv, *others = outputs(
+        out_ff, out_at, out_res, out_tok, small, ffn_cols, 8 * half * 4 * rows
+    )
+    return (result, to_tok, to_qkv.T, *others)
 
 
 def on_device(tokens, cotangent, lengths, deal_order, *weights):

time: 286 us -> 282 us (0.986)
  Pallas kernels: 283 us -> 280 us
    pallas_call x1, Pallas kernels: 279 us -> 276 us  [run_layer(): pl.pallas_call(layer_kernel, out_shape=[shape((3, rows, 5 * TILE), BF16),...]
where the time goes in v8:
time: 282 us; the launch traced here: 281 us
  Pallas kernels  280 us (99%)
    pallas_call x1, Pallas kernels, run_layer(): pl.pallas_call(layer_kernel, out_shape=[shape((3, rows, 5 * TILE), BF16),...  276 us

profile of v8, /device:TPU:4, one launch (start us, length us, event | category | flops | bytes accessed | tf_op | source)
XLA Modules:
  0.0 280.8 jit_solution(8255274741974439722)
XLA Ops:
  0.6 276.1 %layer.1 = (bf16[3,448,640]{2,1,0:T(8,128)(2,1)}, bf16[2,256,512]{2,1,0:T(8,128)(2,1)}, bf16[448,512]{1,0:T(8,128)(2,1)}, bf16[448,512]{1,0:T(8,128)(2,1)}, f32[...) custom-call(bf16[448,608]{1,0:T(8,128)(2,1)} %w_gate.1, ...), custom_call_target="tpu_custom_call" | custom-call | tf_op jit(solution)/shard_map/layer/pallas_call | solution.py:1833
  276.8 3.9 %outputs.1 = (bf16[448,512]{1,0:T(8,128)(2,1)}, f32[448,512]{1,0:T(8,128)}, f32[288,448]{1,0:T(8,128)}, f32[3,224]{1,0:T(4,128)}, f32[224,448]{1,0:T(8,128)}, /*...) custom-call(bf16[3,448,640]{2,1,0:T(8,128)(2,1)} %get-tuple-element., ...), custom_call_target="tpu_custom_call" | custom-call | tf_op jit(solution)/shard_map/outputs/pallas_call | solution.py:1964

commit v9 on v8

--- a/solution.py
+++ b/solution.py
@@ -1575,10 +1575,6 @@
             columns = jnp.where(tail == j, sums[j], columns)
         gat_tail[h, 0, 0:lead, 0:HDIM] = columns.T[0:lead].astype(BF16)
 
-    head_grads(gproj, xs, 0, HEADROWS)
-    for item in in_back:
-        item.start()
-
     mid_in.finish()
 
     def store_result(at_rows, total):
@@ -1616,6 +1612,10 @@
     one_sum.begin(fill_grad_one)
     one_sum.combine()
     one_sum.release()
+    head_grads(gproj, xs, 0, HEADROWS)
+    for item in in_back:
+        item.start()
+
     extra_back.relay(add_extra)
 
     one_sum.pass_on()

time: 282 us -> 282 us (level)
  no operation moved by 1% of the time
where the time goes in v9:
time: 282 us; the launch traced here: 281 us
  Pallas kernels  280 us (99%)
    pallas_call x1, Pallas kernels, run_layer(): pl.pallas_call(layer_kernel, out_shape=[shape((3, rows, 5 * TILE), BF16),...  276 us

profile of v9, /device:TPU:4, one launch (start us, length us, event | category | flops | bytes accessed | tf_op | source)
XLA Modules:
  0.0 280.8 jit_solution(5855214329284721438)
XLA Ops:
  0.6 276.1 %layer.1 = (bf16[3,448,640]{2,1,0:T(8,128)(2,1)}, bf16[2,256,512]{2,1,0:T(8,128)(2,1)}, bf16[448,512]{1,0:T(8,128)(2,1)}, bf16[448,512]{1,0:T(8,128)(2,1)}, f32[...) custom-call(bf16[448,608]{1,0:T(8,128)(2,1)} %w_gate.1, ...), custom_call_target="tpu_custom_call" | custom-call | tf_op jit(solution)/shard_map/layer/pallas_call | solution.py:1833
  276.8 3.9 %outputs.1 = (bf16[448,512]{1,0:T(8,128)(2,1)}, f32[448,512]{1,0:T(8,128)}, f32[288,448]{1,0:T(8,128)}, f32[3,224]{1,0:T(4,128)}, f32[224,448]{1,0:T(8,128)}, /*...) custom-call(bf16[3,448,640]{2,1,0:T(8,128)(2,1)} %get-tuple-element., ...), custom_call_target="tpu_custom_call" | custom-call | tf_op jit(solution)/shard_map/outputs/pallas_call | solution.py:1964
